TPU v7x, 256 devices: a whole 4x4x8 slice. The times are simulated.
256 devices in a mesh: dp: 4 (over y), context: 16 (over z, core), tensor: 4 (over x).
Axes of the slice: x: 4, y: 4, z: 8, core: 2. Of those that a mesh axis runs over, the one named last changes fastest.
Arguments:
- cross_query: bfloat16 [4, 4096, 8192], P('dp', 'context', 'tensor'), may hold values from -28 to 28
- cross_grad: bfloat16 [4, 4096, 8192], P('dp', 'context', 'tensor'), may hold values from -48 to 48
- neighbour_kv: bfloat16 [512, 128, 2, 1024], P(('dp', 'context', 'tensor')), may hold values from -6 to 6
- span_neighbours: int32 [4, 64, 2], replicated, may hold values from 0 to 511, as said below
Outputs:
- cross_out: bfloat16 [4, 4096, 8192], P('dp', 'context', 'tensor')
- neighbour_grad: bfloat16 [512, 128, 2, 1024], P(('dp', 'context', 'tensor'))
Inputs may be any that keep to these rules, and one draw needn't show every extreme that they name: `span_neighbours`: every row of neighbour_kv is listed exactly once. Span u of sequence b lists only rows stored on devices (of any dp and tensor index) whose context index is that of the positions of span u; such a row's owner is b. Both rows of one device have the same owner; which owner that is differs between devices.
All inputs are finite; a program needn't handle non-finite values.
Results may differ from a plain program's by a relative error of at most 0.005.
Values may be sent and summed in bfloat16 or wider, within the bound.
No kernel may reach another device: no remote copies, remote signals or barrier semaphores. Data moves between devices by JAX's collectives and lax.ppermute only.
A program may use at most 64 MiB of HBM per device.

v0:
```python
import math

import jax
import jax.numpy as jnp
from jax import lax
from jax.sharding import PartitionSpec as P

HD = 128
SPAN = 64
NL = 128
KNB = 2


def passed_along(array, axis, by):
    size = lax.axis_size(axis)
    pairs = [(i, i + by) for i in range(size) if 0 <= i + by < size]
    return lax.ppermute(array, axis, pairs)


def cross_attention(queries, cotangent, context_rows):
    windows = context_rows.shape[0]
    query_width = queries.shape[1]
    kv_width = context_rows.shape[3]
    kv_heads = kv_width // HD
    groups = query_width // kv_width
    row_count = queries.shape[0]
    score_scale = 1.0 / math.sqrt(HD)

    def extend(values):
        head_rows = jnp.zeros((1, query_width), values.dtype)
        tail_rows = jnp.zeros((SPAN - 1, query_width), values.dtype)
        joined = jnp.concatenate([head_rows, values, tail_rows], 0)
        return joined.reshape(windows, SPAN, kv_heads, groups, HD)

    query_five = extend(queries)
    grad_five = extend(cotangent)
    key_part = context_rows[:, :, 0].reshape(windows, -1, kv_heads, HD)
    value_part = context_rows[:, :, 1].reshape(windows, -1, kv_heads, HD)
    scores = (
        jnp.einsum("wqkgd,wnkd->wkgqn", query_five, key_part, preferred_element_type=jnp.float32)
        * score_scale
    )
    peak_value = jnp.max(scores, axis=-1, keepdims=True)
    raised = jnp.exp(scores - peak_value)
    weights = raised / jnp.sum(raised, axis=-1, keepdims=True)
    weights_low = weights.astype(jnp.bfloat16)
    output = jnp.einsum(
        "wkgqn,wnkd->wqkgd", weights_low, value_part, preferred_element_type=jnp.float32
    )
    output = output.reshape(windows * SPAN, query_width)[1 : row_count + 1].astype(jnp.bfloat16)
    weight_slope = jnp.einsum(
        "wqkgd,wnkd->wkgqn", grad_five, value_part, preferred_element_type=jnp.float32
    )
    centre = jnp.sum(weights * weight_slope, axis=-1, keepdims=True)
    score_grad = (weights * (weight_slope - centre) * score_scale).astype(jnp.bfloat16)
    key_grad = jnp.einsum(
        "wkgqn,wqkgd->wnkd", score_grad, query_five, preferred_element_type=jnp.float32
    )
    value_grad = jnp.einsum(
        "wkgqn,wqkgd->wnkd", weights_low, grad_five, preferred_element_type=jnp.float32
    )
    return (output, jnp.stack([key_grad, value_grad], 2).reshape(windows, -1, 2, kv_width))


def shards(cross_query, cross_grad, neighbour_kv, span_neighbours):
    dp_size = lax.axis_size("dp")
    context_size = lax.axis_size("context")
    tensor_size = lax.axis_size("tensor")
    local_rows = neighbour_kv.shape[0]
    capacity = max(2, 2 * local_rows // dp_size)
    kv_width = neighbour_kv.shape[3]
    slice_width = kv_width // tensor_size
    row_count = cross_query.shape[1]
    spans = row_count // SPAN
    listed = span_neighbours.reshape(-1)
    total_rows = listed.shape[0]
    slot_of_row = (
        jnp.zeros((total_rows,), jnp.int32).at[listed].set(jnp.arange(total_rows, dtype=jnp.int32))
    )
    device = (
        lax.axis_index("dp") * context_size + lax.axis_index("context")
    ) * tensor_size + lax.axis_index("tensor")
    own_slots = lax.dynamic_slice_in_dim(slot_of_row, device * local_rows, local_rows, 0)
    owner_dp = own_slots // (context_size * spans * KNB)
    local_order = jnp.arange(local_rows, dtype=jnp.int32)
    ahead_count = jnp.sum(
        (owner_dp[None, :] == owner_dp[:, None]) & (local_order[None, :] < local_order[:, None]),
        axis=1,
    )
    position = owner_dp * capacity + ahead_count
    outgoing = (
        jnp.zeros((dp_size * capacity,) + neighbour_kv.shape[1:], neighbour_kv.dtype)
        .at[position]
        .set(neighbour_kv)
    )
    sequence_lists = lax.dynamic_index_in_dim(
        span_neighbours, lax.axis_index("dp"), 0, keepdims=False
    )
    wanted = lax.dynamic_slice_in_dim(
        sequence_lists, lax.axis_index("context") * spans, spans, 0
    ).reshape(-1)
    per_group = context_size * tensor_size * local_rows
    source_block = wanted // per_group * tensor_size + wanted // local_rows % tensor_size
    before = jnp.sum(
        (source_block[None, :] == source_block[:, None]) & (wanted[None, :] < wanted[:, None]),
        axis=1,
    )
    arrival_slot = source_block * capacity + before
    arrived = lax.all_to_all(
        lax.all_to_all(
            outgoing.reshape(dp_size, capacity, NL, 2, kv_width),
            "dp",
            split_axis=0,
            concat_axis=0,
            tiled=True,
        ),
        "tensor",
        split_axis=4,
        concat_axis=1,
        tiled=True,
    )
    arrived = arrived.reshape(dp_size * tensor_size * capacity, NL, 2, slice_width)
    local_context = arrived[arrival_slot].reshape(spans, KNB * NL, 2, slice_width)
    previous = passed_along(local_context[-1:], "context", 1)
    context_rows = jnp.concatenate([previous, local_context], 0)
    cross_out, window_grads = cross_attention(cross_query[0], cross_grad[0], context_rows)
    following = passed_along(window_grads[:1], "context", -1)
    span_terms = jnp.concatenate([window_grads[1:-1], window_grads[-1:] + following], 0)
    span_low = span_terms.astype(jnp.bfloat16).reshape(spans * KNB, NL, 2, slice_width)
    going_back = (
        jnp.zeros((dp_size * tensor_size * capacity, NL, 2, slice_width), jnp.bfloat16)
        .at[arrival_slot]
        .set(span_low)
    )
    returned = lax.all_to_all(
        lax.all_to_all(
            going_back.reshape(dp_size, tensor_size * capacity, NL, 2, slice_width),
            "dp",
            split_axis=0,
            concat_axis=0,
            tiled=True,
        ),
        "tensor",
        split_axis=1,
        concat_axis=4,
        tiled=True,
    )
    returned = returned.reshape(dp_size * capacity, NL, 2, kv_width)
    neighbour_grad = returned[position]
    return (cross_out[None], neighbour_grad)


def solution(mesh):
    return jax.shard_map(
        shards,
        mesh=mesh,
        in_specs=(
            P("dp", "context", "tensor"),
            P("dp", "context", "tensor"),
            P(("dp", "context", "tensor"), None, None, None),
            P(),
        ),
        out_specs=(P("dp", "context", "tensor"), P(("dp", "context", "tensor"), None, None, None)),
        check_vma=False,
    )
```

profile of v0, /device:TPU:224, one launch (start us, length us, event | category | flops | bytes accessed | tf_op | source)
XLA Modules:
  0.0 349.7 jit_solution(9948848790318241521)
XLA Ops:
  0.6 0.8 copy.119
  1.4 0.1 reshape.305
  1.6 2.4 scatter_custom_fusion
  4.1 0.1 and_select_fusion.6
  4.1 0.2 fusion.33
  4.3 0.1 compare_select_fusion.2
  4.4 1.5 copy.120
  5.9 2.5 broadcast_in_dim.8
  8.4 2.8 scatter_fusion
  11.2 11.1 %copy.121 = bf16[4,2,128,2,1024]{2,3,1,4,0:T(2,128)(2,1)} copy(bf16[4,2,128,2,1024]{4,2,3,1,0:T(8,128)(2,1)} %bitcast.94) | data formatting | bytes 8388608 | tf_op jit(solution)/shard_map/reshape | solution.py:111
  22.3 53.3 %all_to_all.40 = bf16[4,2,128,2,1024]{2,3,1,4,0:T(2,128)(2,1)S(1)} all-to-all(bf16[4,2,128,2,1024]{2,3,1,4,0:T(2,128)(2,1)} %copy.121), channel_id=1, replica_groups=mesh['dp'=4,'context'=16,'tensor'=4] {'dp'}, dimensions={0} | all-to-all | bytes 8388608 | tf_op jit(solution)/shard_map/all_to_all | solution.py:110
  75.6 4.8 %copy.122 = bf16[4,2,128,2,1024]{2,3,1,0,4:T(2,128)(2,1)} copy(bf16[4,2,128,2,1024]{2,3,1,4,0:T(2,128)(2,1)S(1)} %all_to_all.40) | data formatting | bytes 8388608 | tf_op jit(solution)/shard_map/all_to_all | solution.py:110
  80.4 4.8 %all-to-all-start.1 = ((bf16[4,2,128,2,1024]{2,3,1,0,4:T(2,128)(2,1)}), bf16[4,2,128,2,1024]{2,3,1,0,4:T(2,128)(2,1)}, u32[]{:S(2)}, u32[]{:S(2)}) async-start(bf16[4,2,128,2,1024]{2,3,1,0,4:T(2,128)(2,1)} %copy.122), calls=%async_computation.1 | async-start | bytes 8388608 | tf_op jit(solution)/shard_map/all_to_all | solution.py:109
  85.3 0.8 constant_dynamic-slice_fusion
  86.0 0.1 copy.125
  86.1 0.1 reshape.309
  86.4 0.2 convert_reduce_fusion
  86.6 46.6 %all-to-all-done.1 = bf16[4,2,128,2,1024]{2,3,1,0,4:T(2,128)(2,1)} async-done(((bf16[4,2,128,2,1024]{2,3,1,0,4:T(2,128)(2,1)}), bf16[4,2,128,2,1024]{2,3,1,0,4:T(2,128)(2,1)}, u32[]{:S(2)}, u32[]{:S(2)}) %all-to-all-start.1) | async-done | bytes 4194336 | tf_op jit(solution)/shard_map/all_to_all | solution.py:109
  133.2 5.2 %copy.123 = bf16[4,2,128,2,1024]{2,4,3,1,0:T(8,128)(2,1)} copy(bf16[4,2,128,2,1024]{2,3,1,0,4:T(2,128)(2,1)} %all-to-all-done.1) | data formatting | bytes 8388608 | tf_op jit(solution)/shard_map/all_to_all | solution.py:109
  138.4 7.3 %copy.124 = bf16[4,4,2,128,2,256]{5,3,4,2,1,0:T(8,128)(2,1)} copy(bf16[4,4,2,128,2,256]{3,5,1,4,2,0:T(8,128)(2,1)} %bitcast.95) | data formatting | bytes 8388608 | tf_op jit(solution)/shard_map/all_to_all | solution.py:109
  145.7 2.9 gather_fusion
  148.7 2.1 collective-permute-start
  150.9 1.0 maximum_bitcast_fusion.1
  151.9 0.3 copy.163
  152.2 0.3 copy.164
  152.5 0.6 copy-done.8
  153.1 0.1 copy.128
  153.2 3.3 collective-permute-done
  156.4 1.0 pad_maximum_fusion.1
  157.4 1.1 copy.131
  158.5 1.9 fusion.29
  160.4 3.4 fusion.43
  163.8 0.2 copy.130
  164.0 0.8 fusion.27
  164.9 1.6 copy-done
  166.5 0.9 fusion.42
  167.4 28.0 %fusion.4 = bf16[5,2,8,64,256]{4,3,2,1,0:T(8,128)(2,1)S(1)} fusion(f32[5,2,256,64,8]{2,3,4,1,0:T(8,128)S(1)} %fusion.27, f32[5,2,8,64,256]{4,3,2,1,0:T(8,128)S(1)} %copy-done, f32[5,2,8,64]{3,2,1,0:T(8,128)S(1)} %get-tuple-element.18), kind=kOutput, calls=%fused_computation.11 | output fusion | flops 9180415 | bytes 13127680 | tf_op jit(solution)/shard_map/sub | solution.py:55
  195.4 1.7 fusion.18
  197.2 1.7 fusion.21
  198.9 1.1 pad_maximum_fusion.2
  200.0 0.3 copy-done.6
  200.3 2.0 copy.142
  202.3 1.9 collective-permute-start.1
  204.2 2.3 fusion.17
  206.6 2.3 copy.144
  208.9 2.0 copy.143
  210.9 0.3 collective-permute-done.1
  211.2 1.3 add_convert_fusion
  212.5 1.2 pad_maximum_fusion
  213.7 1.0 copy.145
  214.8 2.4 broadcast_in_dim.11
  217.2 3.2 scatter_fusion.1
  220.4 54.2 %all_to_all.41 = bf16[4,8,128,2,256]{4,2,3,1,0:T(8,128)(2,1)S(1)} all-to-all(bf16[4,8,128,2,256]{4,2,3,1,0:T(8,128)(2,1)} %bitcast.93), channel_id=1, replica_groups=mesh['dp'=4,'context'=16,'tensor'=4] {'dp'}, dimensions={0} | all-to-all | bytes 8388608 | tf_op jit(solution)/shard_map/all_to_all | solution.py:136
  274.6 2.2 copy.146
  276.8 4.8 %all-to-all-start.3 = ((bf16[4,8,128,2,256]{4,2,3,0,1:T(8,128)(2,1)}), bf16[4,8,128,2,256]{4,2,3,0,1:T(8,128)(2,1)}, u32[]{:S(2)}, u32[]{:S(2)}) async-start(bf16[4,8,128,2,256]{4,2,3,0,1:T(8,128)(2,1)} %copy.146), calls=%async_computation.3 | async-start | bytes 8388608 | tf_op jit(solution)/shard_map/all_to_all | solution.py:135
  281.7 0.8 fusion.24
  282.6 0.9 copy.135
  283.4 0.6 reshape.312
  284.0 1.2 slice_bitcast_fusion
  285.3 45.9 %all-to-all-done.3 = bf16[4,8,128,2,256]{4,2,3,0,1:T(8,128)(2,1)} async-done(((bf16[4,8,128,2,256]{4,2,3,0,1:T(8,128)(2,1)}), bf16[4,8,128,2,256]{4,2,3,0,1:T(8,128)(2,1)}, u32[]{:S(2)}, u32[]{:S(2)}) %all-to-all-start.3) | async-done | bytes 4194336 | tf_op jit(solution)/shard_map/all_to_all | solution.py:135
  331.1 7.3 %copy.148 = bf16[4,2,128,2,4,256]{2,5,4,3,1,0:T(8,128)(2,1)} copy(bf16[4,2,128,2,4,256]{5,2,3,0,1,4:T(8,128)(2,1)} %bitcast.36) | data formatting | bytes 8388608 | tf_op jit(solution)/shard_map/all_to_all | solution.py:135
  338.4 6.5 %copy.149 = bf16[8,128,2,1024]{3,1,2,0:T(8,128)(2,1)} copy(bf16[8,128,2,1024]{1,3,2,0:T(8,128)(2,1)} %bitcast.96) | data formatting | bytes 8388608 | tf_op jit(solution)/shard_map/reshape | solution.py:148
  344.9 2.8 gather_fusion.1
  347.7 2.0 copy.150
  (33 shorter events, 0.3 us)
Async XLA Ops:
  80.4 52.8 %all-to-all-start.1 = ((bf16[4,2,128,2,1024]{2,3,1,0,4:T(2,128)(2,1)}), bf16[4,2,128,2,1024]{2,3,1,0,4:T(2,128)(2,1)}, u32[]{:S(2)}, u32[]{:S(2)}) async-start(bf16[4,2,128,2,1024]{2,3,1,0,4:T(2,128)(2,1)} %copy.122), calls=%async_computation.1 | async-start | bytes 8388608 | tf_op jit(solution)/shard_map/all_to_all | solution.py:109
  145.7 5.1 %copy-start.10 = (bf16[1,256,2048]{2,1,0:T(8,128)(2,1)S(1)}, bf16[1,256,2048]{2,1,0:T(8,128)(2,1)}, u32[]{:S(2)}) copy-start(bf16[1,256,2048]{2,1,0:T(8,128)(2,1)} %param.5) | copy-start | bytes 3145732
  145.7 5.1 %copy-start.11 = (bf16[1,256,2048]{2,1,0:T(8,128)(2,1)S(1)}, bf16[1,256,2048]{2,1,0:T(8,128)(2,1)}, u32[]{:S(2)}) copy-start(bf16[1,256,2048]{2,1,0:T(8,128)(2,1)} %param.4) | copy-start | bytes 3145732
  148.7 3.2 copy-start.7
  148.7 7.7 %collective-permute-start = (bf16[1,256,2,256]{3,1,2,0:T(8,128)(2,1)S(1)}, bf16[1,256,2,256]{3,1,2,0:T(8,128)(2,1)S(1)}, u32[]{:S(2)}, u32[]{:S(2)}) collective-permute-start(bf16[1,256,2,256]{3,1,2,0:T(8,128)(2,1)S(1)} %bitcast.113), channel_id=1, source_target_pairs={{0,4},{4,8},{8,12},{12,16},{16,20},{20,24},{24,28},{28,32},{32,36}... | collective-permute-start | bytes 786440 | tf_op jit(solution)/shard_map/ppermute | solution.py:17
  151.8 1.2 copy-start.8
  152.2 6.3 %copy-start.1 = (bf16[40,8,16,128]{3,2,1,0:T(8,128)(2,1)}, bf16[40,8,16,128]{3,2,1,0:T(8,128)(2,1)S(1)}, u32[]{:S(2)}) copy-start(bf16[40,8,16,128]{3,2,1,0:T(8,128)(2,1)S(1)} %copy.163) | copy-start | bytes 3932164
  153.1 11.0 %copy-start.3 = (bf16[40,8,16,128]{3,2,1,0:T(8,128)(2,1)}, bf16[40,8,16,128]{3,2,1,0:T(8,128)(2,1)S(1)}, u32[]{:S(2)}) copy-start(bf16[40,8,16,128]{3,2,1,0:T(8,128)(2,1)S(1)} %copy.164) | copy-start | bytes 3932164
  160.4 3.4 copy-start.9
  164.0 2.5 copy-start
  167.4 28.0 %copy-start.2 = (bf16[40,8,16,128]{3,2,1,0:T(8,128)(2,1)S(1)}, bf16[40,8,16,128]{3,2,1,0:T(8,128)(2,1)}, u32[]{:S(2)}) copy-start(bf16[40,8,16,128]{3,2,1,0:T(8,128)(2,1)} %copy-done.1) | copy-start | bytes 3932164
  195.4 1.7 copy-start.4
  197.2 1.7 copy-start.5
  198.9 1.4 copy-start.6
  202.3 8.9 %collective-permute-start.1 = (f32[1,256,2,256]{3,1,0,2:T(8,128)}, f32[1,256,2,256]{3,1,0,2:T(8,128)}, u32[]{:S(2)}, u32[]{:S(2)}) collective-permute-start(f32[1,256,2,256]{3,1,0,2:T(8,128)} %copy.142), channel_id=1, source_target_pairs={{4,0},{8,4},{12,8},{16,12},{20,16},{24,20},{28,24},{32,28},{36,32}... | collective-permute-start | bytes 1572872 | tf_op jit(solution)/shard_map/ppermute | solution.py:17
  276.8 54.3 %all-to-all-start.3 = ((bf16[4,8,128,2,256]{4,2,3,0,1:T(8,128)(2,1)}), bf16[4,8,128,2,256]{4,2,3,0,1:T(8,128)(2,1)}, u32[]{:S(2)}, u32[]{:S(2)}) async-start(bf16[4,8,128,2,256]{4,2,3,0,1:T(8,128)(2,1)} %copy.146), calls=%async_computation.3 | async-start | bytes 8388608 | tf_op jit(solution)/shard_map/all_to_all | solution.py:135
where the time goes:
time: 351 us; the launch traced here: 350 us
  blocking collectives  107 us (30%)
  waiting for transfers between devices  96 us (27%)
  local copies, waits for them, and re-layouts  83.8 us (24%)
  other arithmetic  40.7 us (12%)
  starting transfers between devices  13.7 us (4%)
  matrix products  7.04 us (2%)
    all_to_all x1, blocking collectives, shards(): lax.all_to_all(going_back.reshape(dp_size, tensor_size * capacity, NL, 2,...  54.2 us
    all_to_all x1, blocking collectives, shards(): lax.all_to_all(outgoing.reshape(dp_size, capacity, NL, 2, kv_width), 'dp'...  53.3 us
    all_to_all x1, waiting for transfers between devices, shards(): lax.all_to_all(lax.all_to_all(outgoing.reshape(dp_size, capacity, NL, 2,...  46.6 us
    all_to_all x1, waiting for transfers between devices, shards(): lax.all_to_all(lax.all_to_all(going_back.reshape(dp_size, tensor_size * c...  45.9 us
    sub x1, other arithmetic, cross_attention(): weight_slope - centre  28 us
    all_to_all x2, local copies, waits for them, and re-layouts, shards(): lax.all_to_all(lax.all_to_all(outgoing.reshape(dp_size, capacity, NL, 2,...  12.5 us
    reshape x1, local copies, waits for them, and re-layouts, shards(): outgoing.reshape(dp_size, capacity, NL, 2, kv_width)  11.1 us
    unnamed x29, local copies, waits for them, and re-layouts  7.5 us
  transfers between devices with their start and end apart: 4, of which 4 were waited for; matrix products, arithmetic and copies ran while one was open for 4% of the time, Pallas kernels for 0%

commit v1 on v0

v1 whole, which is shorter than its diff:
```python
import functools
import math

import jax
import jax.numpy as jnp
from jax import lax
from jax.experimental import pallas as pl
from jax.experimental.pallas import tpu as pltpu
from jax.sharding import PartitionSpec as P

HD = 128
SPAN = 64
NL = 128
KNB = 2
SLOTS = 2
LOG2E = 1.4426950408889634


def nt(a, b):
    return lax.dot_general(a, b, (((1,), (1,)), ((), ())), preferred_element_type=jnp.float32)


def nn(a, b):
    return lax.dot_general(a, b, (((1,), (0,)), ((), ())), preferred_element_type=jnp.float32)


def source_of(row, geometry):
    local_rows, context_size, tensor_size = geometry
    device = row // local_rows
    return device // (context_size * tensor_size) * tensor_size + device % tensor_size


def sources_of_owner(ids_ref, owner, count, per_owner, geometry):
    local_rows = geometry[0]
    found = [jnp.int32(0)] * per_owner
    seen = jnp.int32(0)
    for k in range(count):
        row = ids_ref[owner * count + k]
        first = row % local_rows == 0
        source = source_of(row, geometry)
        for m in range(per_owner):
            found[m] = jnp.where(first & (seen == m), source, found[m])
        seen = seen + first.astype(jnp.int32)
    return found


def deliver_kernel(ids_ref, held_ref, out_ref, *, owners, count, geometry):
    tensor_size = geometry[2]
    per_owner = out_ref.shape[1]
    width = out_ref.shape[3]
    for owner in range(owners):
        sources = sources_of_owner(ids_ref, owner, count, per_owner, geometry)
        for m in range(per_owner):
            block = held_ref[sources[m]]
            for t in range(tensor_size):
                out_ref[owner * tensor_size + t, m] = block[:, t * width : (t + 1) * width]


def collect_kernel(ids_ref, held_ref, out_ref, *, owners, count, geometry):
    tensor_size = geometry[2]
    per_owner = held_ref.shape[1]
    width = held_ref.shape[3]
    for owner in range(owners):
        sources = sources_of_owner(ids_ref, owner, count, per_owner, geometry)
        for m in range(per_owner):
            for t in range(tensor_size):
                out_ref[sources[m], :, t * width : (t + 1) * width] = held_ref[
                    owner * tensor_size + t, m
                ]


def attention_kernel(ids_ref, q_ref, g_ref, kv_ref, out_ref, grad_ref, *, count, geometry):
    local_rows = geometry[0]
    rows = kv_ref.shape[2]
    pieces = NL // rows
    kv_heads = kv_ref.shape[3] // HD
    groups = q_ref.shape[1] // (kv_heads * HD)
    scale = 1.0 / math.sqrt(HD)
    window = pl.program_id(0)
    places = []
    for n in range(KNB):
        row = ids_ref[window * KNB + n]
        start = row // local_rows * local_rows
        part = row % local_rows
        seen = jnp.int32(0)
        rank = jnp.int32(0)
        for k in range(count):
            other = ids_ref[k]
            rank = jnp.where(other == start, seen, rank)
            seen = seen + (other % local_rows == 0).astype(jnp.int32)
        for i in range(pieces):
            places.append((part * pieces + i, rank))
    half = local_rows * pieces
    for h in range(kv_heads):
        lanes = slice(h * HD, (h + 1) * HD)
        key = jnp.concatenate([kv_ref[j, m, :, lanes] for j, m in places], 0)
        value = jnp.concatenate([kv_ref[half + j, m, :, lanes] for j, m in places], 0)
        heads = [slice((h * groups + g) * HD, (h * groups + g + 1) * HD) for g in range(groups)]
        query = jnp.concatenate([q_ref[:, s] for s in heads], 0)
        grad = jnp.concatenate([g_ref[:, s] for s in heads], 0)
        scores = nt(key, query) * (scale * LOG2E)
        raised = jnp.exp2(scores - jnp.max(scores, axis=0, keepdims=True))
        weights = raised * (1.0 / jnp.sum(raised, axis=0, keepdims=True))
        low = weights.astype(jnp.bfloat16)
        out = nn(value.T, low).T.astype(jnp.bfloat16)
        for g, s in enumerate(heads):
            out_ref[:, s] = out[g * SPAN : (g + 1) * SPAN]
        value_grad = nn(low, grad).astype(jnp.bfloat16)
        slope = nt(value, grad)
        centre = jnp.sum(weights * slope, axis=0, keepdims=True)
        score_grad = (weights * (slope - centre) * scale).astype(jnp.bfloat16)
        key_grad = nn(score_grad, query).astype(jnp.bfloat16)
        for b, (j, m) in enumerate(places):
            grad_ref[j, m, :, lanes] = key_grad[b * rows : (b + 1) * rows]
            grad_ref[half + j, m, :, lanes] = value_grad[b * rows : (b + 1) * rows]


def whole(shape):
    return pl.BlockSpec(shape, lambda *_: (0,) * len(shape))


def shards(cross_query, cross_grad, neighbour_kv, span_neighbours):
    dp_size = lax.axis_size("dp")
    context_size = lax.axis_size("context")
    tensor_size = lax.axis_size("tensor")
    local_rows, _, _, kv_width = neighbour_kv.shape
    width = kv_width // tensor_size
    row_count, query_width = cross_query.shape[1:]
    spans = row_count // SPAN
    count = spans * KNB
    peers = dp_size * tensor_size
    per_owner = count // local_rows
    rows = local_rows * NL * SLOTS // peers
    pieces = NL // rows
    geometry = (local_rows, context_size, tensor_size)
    group = ("dp", "tensor")
    params = pltpu.CompilerParams(vmem_limit_bytes=32 * 1024 * 1024)

    back = [(i + 1, i) for i in range(context_size - 1)]
    forth = [(i, i + 1) for i in range(context_size - 1)]
    query = cross_query[0]
    grad = cross_grad[0]
    next_query = lax.ppermute(query[:SPAN], "context", back)
    next_grad = lax.ppermute(grad[:SPAN], "context", back)

    def ahead(own, following):
        return jnp.concatenate([own[SPAN - 1 :], following[: SPAN - 1]], 0)

    ids = lax.dynamic_slice_in_dim(
        span_neighbours, lax.axis_index("context") * spans, spans, 1
    ).reshape(-1)
    own_ids = lax.dynamic_slice_in_dim(ids, lax.axis_index("dp") * count, count, 0)

    spread = neighbour_kv.reshape(local_rows, pieces, rows, SLOTS, kv_width)
    spread = spread.transpose(3, 0, 1, 2, 4).reshape(peers, rows, kv_width)
    held = lax.all_to_all(spread, group, 0, 0, tiled=True)
    smem = pl.BlockSpec(memory_space=pltpu.SMEM)
    vmem = pl.BlockSpec(memory_space=pltpu.VMEM)
    delivered = pl.pallas_call(
        functools.partial(deliver_kernel, owners=dp_size, count=count, geometry=geometry),
        out_shape=jax.ShapeDtypeStruct((peers, per_owner, rows, width), jnp.bfloat16),
        in_specs=[smem, vmem],
        out_specs=vmem,
        compiler_params=params,
        name="deliver",
    )(ids, held)
    kv = lax.all_to_all(delivered, group, 0, 0, tiled=True)
    block = pl.BlockSpec((SPAN, query_width), lambda w: (w, 0))
    out_rows, kv_grad = pl.pallas_call(
        functools.partial(attention_kernel, count=count, geometry=geometry),
        grid=(spans,),
        out_shape=(
            jax.ShapeDtypeStruct((row_count, query_width), jnp.bfloat16),
            jax.ShapeDtypeStruct(kv.shape, jnp.bfloat16),
        ),
        in_specs=[smem, block, block, whole(kv.shape)],
        out_specs=(block, whole(kv.shape)),
        compiler_params=params,
        name="attention",
    )(own_ids, ahead(query, next_query), ahead(grad, next_grad), kv)
    before = lax.ppermute(out_rows[row_count - SPAN :], "context", forth)
    cross_out = jnp.concatenate([before[1:], out_rows[: row_count - SPAN + 1]], 0)

    returned = lax.all_to_all(kv_grad, group, 0, 0, tiled=True)
    collected = pl.pallas_call(
        functools.partial(collect_kernel, owners=dp_size, count=count, geometry=geometry),
        out_shape=jax.ShapeDtypeStruct((peers, rows, kv_width), jnp.bfloat16),
        in_specs=[smem, vmem],
        out_specs=vmem,
        compiler_params=params,
        name="collect",
    )(ids, returned)
    final = lax.all_to_all(collected, group, 0, 0, tiled=True)
    final = final.reshape(SLOTS, local_rows, pieces, rows, kv_width).transpose(1, 2, 3, 0, 4)
    return (cross_out[None], final.reshape(neighbour_kv.shape))


def solution(mesh):
    return jax.shard_map(
        shards,
        mesh=mesh,
        in_specs=(
            P("dp", "context", "tensor"),
            P("dp", "context", "tensor"),
            P(("dp", "context", "tensor"), None, None, None),
            P(),
        ),
        out_specs=(P("dp", "context", "tensor"), P(("dp", "context", "tensor"), None, None, None)),
        check_vma=False,
    )
```

time: 351 us -> 110 us (0.31)
  blocking collectives: 107 us -> 20 us
  local copies, waits for them, and re-layouts: 83.8 us -> 9.02 us
  waiting for transfers between devices: 96 us -> 43.6 us
  other arithmetic: 40.7 us -> 3.45 us
  Pallas kernels: 0 us -> 11.7 us
  starting transfers between devices: 13.7 us -> 21.3 us
  matrix products: 7.04 us -> 0 us
    all_to_all x2 -> x1, blocking collectives: 107 us -> 20 us  [shards(): returned = lax.all_to_all(kv_grad, group, 0, 0, tiled=True)]
    all_to_all x2 -> x3, waiting for transfers between devices: 92.4 us -> 37.9 us  [the longest x1 16.3 us: shards(): held = lax.all_to_all(spread, group, 0, 0, tiled=True)]
    sub x2 -> x0, other arithmetic: 31.4 us -> none  [the longest x1 28 us: cross_attention(): weight_slope - centre]
    all_to_all x5 -> x0, local copies, waits for them, and re-layouts: 26.8 us -> none  [the longest x2 12.5 us: shards(): lax.all_to_all(lax.all_to_all(outgoing.reshape(dp_size, capacity, NL, 2,...]
    reshape x6 -> x2, local copies, waits for them, and re-layouts: 18.5 us -> 2.57 us  [the longest x1 2.48 us: shards(): spread = neighbour_kv.reshape(local_rows, pieces, rows, SLOTS, kv_width)]
    pallas_call x0 -> x3, Pallas kernels: none -> 11.7 us  [the longest x1 7.58 us: shards(): pl.pallas_call(functools.partial(attention_kernel, count=count, geometry=...]
    scatter x3 -> x0, local copies, waits for them, and re-layouts: 8.45 us -> none  [the longest x1 3.22 us: shards(): going_back = jnp.zeros((dp_size * tensor_size * capacity, NL, 2, slice_wi...]
    dot_general x5 -> x0, matrix products: 7.04 us -> none  [the longest x1 1.91 us: cross_attention(): jnp.einsum('wqkgd,wnkd->wkgqn', query_five, key_part, preferred_element_t...]
  transfers between devices with their start and end apart: 4 -> 6, of which waited for: 4 -> 4; matrix products, arithmetic and copies ran while one was open for 4% -> 8% of each run, Pallas kernels for 0% -> 2%
where the time goes in v1:
time: 110 us
  waiting for transfers between devices  43.6 us (40%)
  starting transfers between devices  21.3 us (19%)
  blocking collectives  20 us (18%)
  Pallas kernels  11.7 us (11%)
  local copies, waits for them, and re-layouts  9.02 us (8%)
  other arithmetic  3.45 us (3%)
    all_to_all x1, blocking collectives, shards(): returned = lax.all_to_all(kv_grad, group, 0, 0, tiled=True)  20 us
    all_to_all x1, waiting for transfers between devices, shards(): held = lax.all_to_all(spread, group, 0, 0, tiled=True)  16.3 us
    all_to_all x1, waiting for transfers between devices, shards(): kv = lax.all_to_all(delivered, group, 0, 0, tiled=True)  14.3 us
    pallas_call x1, Pallas kernels, shards(): pl.pallas_call(functools.partial(attention_kernel, count=count, geometry=...  7.58 us
    all_to_all x1, waiting for transfers between devices, shards(): final = lax.all_to_all(collected, group, 0, 0, tiled=True)  7.37 us
    all_to_all x1, starting transfers between devices, shards(): held = lax.all_to_all(spread, group, 0, 0, tiled=True)  7.17 us
    ppermute x1, waiting for transfers between devices, shards(): before = lax.ppermute(out_rows[row_count - SPAN:], 'context', forth)  5.7 us
    all_to_all x1, starting transfers between devices, shards(): kv = lax.all_to_all(delivered, group, 0, 0, tiled=True)  3.79 us
  transfers between devices with their start and end apart: 6, of which 4 were waited for; matrix products, arithmetic and copies ran while one was open for 8% of the time, Pallas kernels for 2%

profile of v1, /device:TPU:224, one launch (start us, length us, event | category | flops | bytes accessed | tf_op | source)
XLA Modules:
  0.0 109.9 jit_solution(11370836097162130865)
XLA Ops:
  0.6 0.0 copy-start
  0.6 1.0 slice_bitcast_fusion.2
  1.6 2.4 %collective-permute-start.1 = (bf16[64,2048]{1,0:T(8,128)(2,1)S(1)}, bf16[64,2048]{1,0:T(8,128)(2,1)}, u32[]{:S(2)}, u32[]{:S(2)}) collective-permute-start(bf16[64,2048]{1,0:T(8,128)(2,1)S(1)} %slice_bitcast_fusion.2), channel_id=1, source_target_pairs={{4,0},{8,4},{12,8},{16,12},{20,16},{24,20},{28,24},{32,28},{36,32}... | collective-permute-start | bytes 786440 | tf_op jit(solution)/shard_map/ppermute | solution.py:144
  4.0 2.5 %copy.10 = bf16[2,4,32,2,1024]{4,2,1,0,3:T(8,128)(2,1)} copy(bf16[2,4,32,2,1024]{4,3,2,1,0:T(2,128)(2,1)} %bitcast.21) | data formatting | bytes 2097152 | tf_op jit(solution)/shard_map/reshape | solution.py:154
  6.5 0.0 copy-start.4
  6.5 7.2 %all-to-all-start = ((bf16[16,32,1024]{2,1,0:T(8,128)(2,1)}), bf16[16,32,1024]{2,1,0:T(8,128)(2,1)S(1)}, u32[]{:S(2)}, u32[]{:S(2)}) async-start(bf16[16,32,1024]{2,1,0:T(8,128)(2,1)} %bitcast.6), calls=%async_computation | async-start | bytes 2097152 | tf_op jit(solution)/shard_map/all_to_all | solution.py:156
  13.6 0.0 copy-done.4
  13.7 0.7 slice_bitcast_fusion.3
  14.4 2.3 %collective-permute-start = (bf16[64,2048]{1,0:T(8,128)(2,1)}, bf16[64,2048]{1,0:T(8,128)(2,1)}, u32[]{:S(2)}, u32[]{:S(2)}) collective-permute-start(bf16[64,2048]{1,0:T(8,128)(2,1)} %slice_bitcast_fusion.3), channel_id=1, source_target_pairs={{4,0},{8,4},{12,8},{16,12},{20,16},{24,20},{28,24},{32,28},{36,32}... | collective-permute-start | bytes 786440 | tf_op jit(solution)/shard_map/ppermute | solution.py:143
  16.7 0.0 copy-done
  16.7 0.1 constant_dynamic-slice_fusion
  16.8 0.1 copy.9
  16.9 0.1 reshape.23.ids_ref
  17.0 0.2 slice_bitcast_fusion.1
  17.2 16.3 %all-to-all-done.held_ref = bf16[16,32,1024]{2,1,0:T(8,128)(2,1)S(1)} async-done(((bf16[16,32,1024]{2,1,0:T(8,128)(2,1)}), bf16[16,32,1024]{2,1,0:T(8,128)(2,1)S(1)}, u32[]{:S(2)}, u32[]{:S(2)}) %all-to-all-start) | async-done | bytes 1048608 | tf_op jit(solution)/shard_map/all_to_all | solution.py:156
  33.5 2.0 %deliver.1 = bf16[16,4,32,256]{3,2,1,0:T(8,128)(2,1)} custom-call(s32[32]{0:T(128)S(1)} %reshape.23.ids_ref, bf16[16,32,1024]{2,1,0:T(8,128)(2,1)S(1)} %all-to-all-done.held_ref), custom_call_target="tpu_custom_call" | custom-call | tf_op jit(solution)/shard_map/deliver/pallas_call | solution.py:159
  35.5 0.0 copy-start.5
  35.5 3.8 %all-to-all-start.1 = ((bf16[16,4,32,256]{3,2,1,0:T(8,128)(2,1)}), bf16[16,4,32,256]{3,2,1,0:T(8,128)(2,1)S(1)}, u32[]{:S(2)}, u32[]{:S(2)}) async-start(bf16[16,4,32,256]{3,2,1,0:T(8,128)(2,1)} %deliver.1), calls=%async_computation.1 | async-start | bytes 2097152 | tf_op jit(solution)/shard_map/all_to_all | solution.py:167
  39.3 0.0 copy-done.5
  39.3 1.1 slice_bitcast_fusion
  40.4 0.1 dynamic_slice.7.ids_ref
  40.5 0.0 collective-permute-done
  40.5 0.0 copy-start.3
  40.5 1.2 %pad_maximum_fusion.q_ref = bf16[256,2048]{1,0:T(8,128)(2,1)S(1)} fusion(bf16[63,2048]{1,0:T(8,128)(2,1)} %bitcast.18, bf16[193,2048]{1,0:T(8,128)(2,1)S(1)} %slice_bitcast_fusion.1), kind=kLoop, calls=%fused_computation | loop fusion | flops 2097152 | bytes 2097152 | tf_op jit(solution)/shard_map/concatenate | solution.py:147
  41.7 0.0 collective-permute-done.1
  41.7 0.0 copy-done.3
  41.7 1.1 pad_maximum_fusion.1.g_ref
  42.8 14.3 %all-to-all-done.1.kv_ref = bf16[16,4,32,256]{3,2,1,0:T(8,128)(2,1)S(1)} async-done(((bf16[16,4,32,256]{3,2,1,0:T(8,128)(2,1)}), bf16[16,4,32,256]{3,2,1,0:T(8,128)(2,1)S(1)}, u32[]{:S(2)}, u32[]{:S(2)}) %all-to-all-start.1) | async-done | bytes 1048608 | tf_op jit(solution)/shard_map/all_to_all | solution.py:167
  57.0 7.6 %attention.1 = (bf16[256,2048]{1,0:T(8,128)(2,1)S(1)}, bf16[16,4,32,256]{3,2,1,0:T(8,128)(2,1)S(1)}) custom-call(s32[8]{0:T(128)S(1)} %dynamic_slice.7.ids_ref, bf16[256,2048]{1,0:T(8,128)(2,1)S(1)} %pad_maximum_fusion.q_ref, bf16[256,2048]{1,0:T(8,128)(2,1)S(1)} %pad_maximum_fusion.1.g_ref, bf16[16,4,32,256]{3,2,1,0:T(8,128)(2,1)S(1)} %all-to-all-done.1.kv_ref), custom_call_target="tpu_custom_call" | custom-call | tf_op jit(solution)/shard_map/attention/pallas_call | solution.py:169
  64.6 0.0 copy-start.1
  64.6 1.0 copy-done.1
  65.6 20.0 %all_to_all.20.held_ref = bf16[16,4,32,256]{3,2,1,0:T(8,128)(2,1)S(1)} all-to-all(bf16[16,4,32,256]{3,2,1,0:T(8,128)(2,1)S(1)} %get-tuple-element.5), channel_id=1, replica_groups=mesh['dp'=4,'context'=16,'tensor'=4] {'dp','tensor'}, dimensions={0} | all-to-all | bytes 2097152 | tf_op jit(solution)/shard_map/all_to_all | solution.py:184
  85.6 2.1 %collect.1 = bf16[16,32,1024]{2,1,0:T(8,128)(2,1)} custom-call(s32[32]{0:T(128)S(1)} %reshape.23.ids_ref, bf16[16,4,32,256]{3,2,1,0:T(8,128)(2,1)S(1)} %all_to_all.20.held_ref), custom_call_target="tpu_custom_call" | custom-call | tf_op jit(solution)/shard_map/collect/pallas_call | solution.py:185
  87.6 0.0 copy-start.2
  87.6 3.8 %all-to-all-start.3 = ((bf16[16,32,1024]{2,1,0:T(8,128)(2,1)}), bf16[16,32,1024]{2,1,0:T(8,128)(2,1)S(1)}, u32[]{:S(2)}, u32[]{:S(2)}) async-start(bf16[16,32,1024]{2,1,0:T(8,128)(2,1)} %collect.1), calls=%async_computation.3 | async-start | bytes 2097152 | tf_op jit(solution)/shard_map/all_to_all | solution.py:193
  91.4 0.0 copy-done.2
  91.5 1.9 %collective-permute-start.2 = (bf16[64,2048]{1,0:T(8,128)(2,1)S(1)}, bf16[64,2048]{1,0:T(8,128)(2,1)S(1)}, u32[]{:S(2)}, u32[]{:S(2)}) collective-permute-start(bf16[64,2048]{1,0:T(8,128)(2,1)S(1)} %slice.49), channel_id=1, source_target_pairs={{0,4},{4,8},{8,12},{12,16},{16,20},{20,24},{24,28},{28,32},{32,36}... | collective-permute-start | bytes 786440 | tf_op jit(solution)/shard_map/ppermute | solution.py:181
  93.4 0.1 slice.51
  93.4 5.7 %collective-permute-done.2 = bf16[64,2048]{1,0:T(8,128)(2,1)S(1)} collective-permute-done((bf16[64,2048]{1,0:T(8,128)(2,1)S(1)}, bf16[64,2048]{1,0:T(8,128)(2,1)S(1)}, u32[]{:S(2)}, u32[]{:S(2)}) %collective-permute-start.2) | collective-permute-done | bytes 262176 | tf_op jit(solution)/shard_map/ppermute | solution.py:181
  99.1 0.1 slice.54
  99.2 1.2 %maximum_bitcast_fusion = bf16[1,256,2048]{2,1,0:T(8,128)(2,1)} fusion(bf16[193,2048]{1,0:T(8,128)(2,1)S(1)} %slice.51, bf16[63,2048]{1,0:T(8,128)(2,1)S(1)} %slice.54), kind=kLoop, calls=%fused_computation.2 | loop fusion | flops 2097152 | bytes 2097152 | tf_op jit(solution)/shard_map/broadcast_in_dim | solution.py:195
  100.4 7.4 %all-to-all-done.3 = bf16[16,32,1024]{2,1,0:T(8,128)(2,1)S(1)} async-done(((bf16[16,32,1024]{2,1,0:T(8,128)(2,1)}), bf16[16,32,1024]{2,1,0:T(8,128)(2,1)S(1)}, u32[]{:S(2)}, u32[]{:S(2)}) %all-to-all-start.3) | async-done | bytes 1048608 | tf_op jit(solution)/shard_map/all_to_all | solution.py:193
  107.8 2.1 %copy.11 = bf16[2,4,32,2,1024]{4,3,2,1,0:T(2,128)(2,1)} copy(bf16[2,4,32,2,1024]{4,2,1,0,3:T(8,128)(2,1)S(1)} %bitcast.20) | data formatting | bytes 2097152 | tf_op jit(solution)/shard_map/transpose | solution.py:194
  (1 shorter events, 0.0 us)
Async XLA Ops:
  0.6 16.1 %copy-start = (s32[4,64,2]{1,2,0:T(2,128)S(1)}, s32[4,64,2]{1,2,0:T(2,128)}, u32[]{:S(2)}) copy-start(s32[4,64,2]{1,2,0:T(2,128)} %param.7) | copy-start | bytes 6148
  1.6 40.0 %collective-permute-start.1 = (bf16[64,2048]{1,0:T(8,128)(2,1)S(1)}, bf16[64,2048]{1,0:T(8,128)(2,1)}, u32[]{:S(2)}, u32[]{:S(2)}) collective-permute-start(bf16[64,2048]{1,0:T(8,128)(2,1)S(1)} %slice_bitcast_fusion.2), channel_id=1, source_target_pairs={{4,0},{8,4},{12,8},{16,12},{20,16},{24,20},{28,24},{32,28},{36,32}... | collective-permute-start | bytes 786440 | tf_op jit(solution)/shard_map/ppermute | solution.py:144
  6.5 7.2 %copy-start.4 = (bf16[1,256,2048]{2,1,0:T(8,128)(2,1)S(1)}, bf16[1,256,2048]{2,1,0:T(8,128)(2,1)}, u32[]{:S(2)}) copy-start(bf16[1,256,2048]{2,1,0:T(8,128)(2,1)} %param.4) | copy-start | bytes 3145732
  6.5 27.0 %all-to-all-start = ((bf16[16,32,1024]{2,1,0:T(8,128)(2,1)}), bf16[16,32,1024]{2,1,0:T(8,128)(2,1)S(1)}, u32[]{:S(2)}, u32[]{:S(2)}) async-start(bf16[16,32,1024]{2,1,0:T(8,128)(2,1)} %bitcast.6), calls=%async_computation | async-start | bytes 2097152 | tf_op jit(solution)/shard_map/all_to_all | solution.py:156
  14.4 26.1 %collective-permute-start = (bf16[64,2048]{1,0:T(8,128)(2,1)}, bf16[64,2048]{1,0:T(8,128)(2,1)}, u32[]{:S(2)}, u32[]{:S(2)}) collective-permute-start(bf16[64,2048]{1,0:T(8,128)(2,1)} %slice_bitcast_fusion.3), channel_id=1, source_target_pairs={{4,0},{8,4},{12,8},{16,12},{20,16},{24,20},{28,24},{32,28},{36,32}... | collective-permute-start | bytes 786440 | tf_op jit(solution)/shard_map/ppermute | solution.py:143
  35.5 3.8 %copy-start.5 = (bf16[1,256,2048]{2,1,0:T(8,128)(2,1)S(1)}, bf16[1,256,2048]{2,1,0:T(8,128)(2,1)}, u32[]{:S(2)}) copy-start(bf16[1,256,2048]{2,1,0:T(8,128)(2,1)} %param.5) | copy-start | bytes 3145732
  35.5 21.5 %all-to-all-start.1 = ((bf16[16,4,32,256]{3,2,1,0:T(8,128)(2,1)}), bf16[16,4,32,256]{3,2,1,0:T(8,128)(2,1)S(1)}, u32[]{:S(2)}, u32[]{:S(2)}) async-start(bf16[16,4,32,256]{3,2,1,0:T(8,128)(2,1)} %deliver.1), calls=%async_computation.1 | async-start | bytes 2097152 | tf_op jit(solution)/shard_map/all_to_all | solution.py:167
  40.5 1.2 %copy-start.3 = (bf16[193,2048]{1,0:T(8,128)(2,1)S(1)}, bf16[193,2048]{1,0:T(8,128)(2,1)}, u32[]{:S(2)}) copy-start(bf16[193,2048]{1,0:T(8,128)(2,1)} %slice_bitcast_fusion) | copy-start | bytes 2371588
  64.6 1.0 copy-start.1
  87.6 3.8 %copy-start.2 = (bf16[256,2048]{1,0:T(8,128)(2,1)S(1)}, bf16[256,2048]{1,0:T(8,128)(2,1)}, u32[]{:S(2)}) copy-start(bf16[256,2048]{1,0:T(8,128)(2,1)} %copy-done.1) | copy-start | bytes 3145732
  87.6 20.2 %all-to-all-start.3 = ((bf16[16,32,1024]{2,1,0:T(8,128)(2,1)}), bf16[16,32,1024]{2,1,0:T(8,128)(2,1)S(1)}, u32[]{:S(2)}, u32[]{:S(2)}) async-start(bf16[16,32,1024]{2,1,0:T(8,128)(2,1)} %collect.1), calls=%async_computation.3 | async-start | bytes 2097152 | tf_op jit(solution)/shard_map/all_to_all | solution.py:193
  91.5 7.7 %collective-permute-start.2 = (bf16[64,2048]{1,0:T(8,128)(2,1)S(1)}, bf16[64,2048]{1,0:T(8,128)(2,1)S(1)}, u32[]{:S(2)}, u32[]{:S(2)}) collective-permute-start(bf16[64,2048]{1,0:T(8,128)(2,1)S(1)} %slice.49), channel_id=1, source_target_pairs={{0,4},{4,8},{8,12},{12,16},{16,20},{20,24},{24,28},{28,32},{32,36}... | collective-permute-start | bytes 786440 | tf_op jit(solution)/shard_map/ppermute | solution.py:181

commit v2 on v1

v2 whole, which is shorter than its diff:
```python
import functools
import math

import jax
import jax.numpy as jnp
from jax import lax
from jax.experimental import pallas as pl
from jax.experimental.pallas import tpu as pltpu
from jax.sharding import PartitionSpec as P

HD = 128
SPAN = 64
NL = 128
KNB = 2
SLOTS = 2
LOG2E = 1.4426950408889634


def nt(a, b):
    return lax.dot_general(a, b, (((1,), (1,)), ((), ())), preferred_element_type=jnp.float32)


def nn(a, b):
    return lax.dot_general(a, b, (((1,), (0,)), ((), ())), preferred_element_type=jnp.float32)


def place_of(row, geometry):
    local_rows, context_size, tensor_size = geometry
    device = row // local_rows
    source = device // (context_size * tensor_size) * tensor_size + device % tensor_size
    return source, row % local_rows


def deliver_kernel(ids_ref, held_ref, *out_refs, geometry):
    owners = len(out_refs)
    count = out_refs[0].shape[0]
    me = ids_ref[owners * count]
    for s, out_ref in enumerate(out_refs):
        owner = (me + s) % owners
        for k in range(count):
            source, part = place_of(ids_ref[owner * count + k], geometry)
            for slot in range(SLOTS):
                out_ref[k, slot] = held_ref[source, slot, part]


def collect_kernel(ids_ref, *refs, geometry):
    held_refs, out_ref = refs[:-1], refs[-1]
    owners = len(held_refs)
    count = held_refs[0].shape[0]
    me = ids_ref[owners * count]
    for s, held_ref in enumerate(held_refs):
        owner = (me + s) % owners
        for k in range(count):
            source, part = place_of(ids_ref[owner * count + k], geometry)
            for slot in range(SLOTS):
                out_ref[source, slot, part] = held_ref[k, slot]


def attention_kernel(q_ref, g_ref, *refs):
    parts = len(refs) // 2
    kv_refs, out_ref, grad_refs = refs[:parts], refs[parts], refs[parts + 1 :]
    rows = kv_refs[0].shape[2]
    kv_heads = kv_refs[0].shape[3] // HD
    groups = q_ref.shape[1] // (kv_heads * HD)
    scale = 1.0 / math.sqrt(HD)
    places = [(p, n) for p in range(parts) for n in range(KNB)]
    for h in range(kv_heads):
        lanes = slice(h * HD, (h + 1) * HD)
        key = jnp.concatenate([kv_refs[p][n, 0, :, lanes] for p, n in places], 0)
        value = jnp.concatenate([kv_refs[p][n, 1, :, lanes] for p, n in places], 0)
        heads = [slice((h * groups + g) * HD, (h * groups + g + 1) * HD) for g in range(groups)]
        query = jnp.concatenate([q_ref[:, s] for s in heads], 0)
        grad = jnp.concatenate([g_ref[:, s] for s in heads], 0)
        scores = nt(key, query) * (scale * LOG2E)
        raised = jnp.exp2(scores - jnp.max(scores, axis=0, keepdims=True))
        weights = raised * (1.0 / jnp.sum(raised, axis=0, keepdims=True))
        low = weights.astype(jnp.bfloat16)
        out = nn(value.T, low).T.astype(jnp.bfloat16)
        for g, s in enumerate(heads):
            out_ref[:, s] = out[g * SPAN : (g + 1) * SPAN]
        value_grad = nn(low, grad).astype(jnp.bfloat16)
        slope = nt(value, grad)
        centre = jnp.sum(weights * slope, axis=0, keepdims=True)
        score_grad = (weights * (slope - centre) * scale).astype(jnp.bfloat16)
        key_grad = nn(score_grad, query).astype(jnp.bfloat16)
        for b, (p, n) in enumerate(places):
            grad_refs[p][n, 0, :, lanes] = key_grad[b * rows : (b + 1) * rows]
            grad_refs[p][n, 1, :, lanes] = value_grad[b * rows : (b + 1) * rows]


def shards(cross_query, cross_grad, neighbour_kv, span_neighbours):
    dp_size = lax.axis_size("dp")
    context_size = lax.axis_size("context")
    tensor_size = lax.axis_size("tensor")
    local_rows, _, _, kv_width = neighbour_kv.shape
    width = kv_width // tensor_size
    row_count, query_width = cross_query.shape[1:]
    spans = row_count // SPAN
    count = spans * KNB
    peers = dp_size * tensor_size
    rows = NL // dp_size
    geometry = (local_rows, context_size, tensor_size)
    group = ("dp", "tensor")
    params = pltpu.CompilerParams(vmem_limit_bytes=32 * 1024 * 1024)
    smem = pl.BlockSpec(memory_space=pltpu.SMEM)
    vmem = pl.BlockSpec(memory_space=pltpu.VMEM)

    def ring(array, by):
        return lax.ppermute(array, "dp", [(i, (i + by) % dp_size) for i in range(dp_size)])

    spread = neighbour_kv.transpose(2, 0, 1, 3)
    spread = spread.reshape(SLOTS, local_rows, dp_size, rows, tensor_size, width)
    spread = spread.transpose(2, 4, 0, 1, 3, 5).reshape(peers, SLOTS, local_rows, rows, width)
    held = lax.all_to_all(spread, group, 0, 0, tiled=True)

    ids = lax.dynamic_slice_in_dim(
        span_neighbours, lax.axis_index("context") * spans, spans, 1
    ).reshape(-1)
    ids = jnp.concatenate([ids, lax.axis_index("dp").astype(jnp.int32)[None]])

    held, halo_query, halo_grad = lax.optimization_barrier(
        (held, cross_query[0, :SPAN], cross_grad[0, :SPAN])
    )
    back = [(i + 1, i) for i in range(context_size - 1)]
    forth = [(i, i + 1) for i in range(context_size - 1)]
    following = lax.ppermute(jnp.stack([halo_query, halo_grad]), "context", back)
    query = jnp.concatenate([cross_query[0, SPAN - 1 :], following[0, : SPAN - 1]], 0)
    grad = jnp.concatenate([cross_grad[0, SPAN - 1 :], following[1, : SPAN - 1]], 0)

    part = jax.ShapeDtypeStruct((count, SLOTS, rows, width), jnp.bfloat16)
    delivered = pl.pallas_call(
        functools.partial(deliver_kernel, geometry=geometry),
        out_shape=(part,) * dp_size,
        in_specs=[smem, vmem],
        out_specs=(vmem,) * dp_size,
        compiler_params=params,
        name="deliver",
    )(ids, held)
    order = sorted(range(1, dp_size), key=lambda s: -min(s, dp_size - s))
    kv = {0: delivered[0]}
    for s in order:
        kv[s] = ring(delivered[s], s)
    block = pl.BlockSpec((SPAN, query_width), lambda w: (w, 0))
    kv_block = pl.BlockSpec((KNB, SLOTS, rows, width), lambda w: (w, 0, 0, 0))
    out_rows, *kv_grads = pl.pallas_call(
        attention_kernel,
        grid=(spans,),
        out_shape=(jax.ShapeDtypeStruct((row_count, query_width), jnp.bfloat16),)
        + (part,) * dp_size,
        in_specs=[block, block] + [kv_block] * dp_size,
        out_specs=(block,) + (kv_block,) * dp_size,
        compiler_params=params,
        name="attention",
    )(query, grad, *[kv[s] for s in range(dp_size)])
    returned = {0: kv_grads[0]}
    for s in order:
        returned[s] = ring(kv_grads[s], -s)

    before = lax.ppermute(out_rows[row_count - SPAN :], "context", forth)
    cross_out = jnp.concatenate([before[1:], out_rows[: row_count - SPAN + 1]], 0)

    collected = pl.pallas_call(
        functools.partial(collect_kernel, geometry=geometry),
        out_shape=jax.ShapeDtypeStruct(held.shape, jnp.bfloat16),
        in_specs=[smem] + [vmem] * dp_size,
        out_specs=vmem,
        compiler_params=params,
        name="collect",
    )(ids, *[returned[s] for s in range(dp_size)])
    final = lax.all_to_all(collected, group, 0, 0, tiled=True)
    final = final.reshape(dp_size, tensor_size, SLOTS, local_rows, rows, width)
    final = final.transpose(3, 0, 4, 2, 1, 5)
    return (cross_out[None], final.reshape(neighbour_kv.shape))


def solution(mesh):
    return jax.shard_map(
        shards,
        mesh=mesh,
        in_specs=(
            P("dp", "context", "tensor"),
            P("dp", "context", "tensor"),
            P(("dp", "context", "tensor"), None, None, None),
            P(),
        ),
        out_specs=(P("dp", "context", "tensor"), P(("dp", "context", "tensor"), None, None, None)),
        check_vma=False,
    )
```

time: 110 us -> 97.6 us (0.89)
  blocking collectives: 20 us -> 0 us
  waiting for transfers between devices: 43.6 us -> 56.4 us
  local copies, waits for them, and re-layouts: 9.02 us -> 6.88 us
  other arithmetic: 3.45 us -> 1.63 us
  Pallas kernels: 11.7 us -> 9.92 us
    ppermute x2 -> x7, waiting for transfers between devices: 0.01 us -> 25.9 us  [the longest x6 24.1 us: ring(): lax.ppermute(array, 'dp', [(i, (i + by) % dp_size) for i in range(dp_size)])]
    all_to_all x1 -> x0, blocking collectives: 20 us -> none  [shards(): returned = lax.all_to_all(kv_grad, group, 0, 0, tiled=True)]
    all_to_all x1 -> x0, waiting for transfers between devices: 14.3 us -> none  [shards(): kv = lax.all_to_all(delivered, group, 0, 0, tiled=True)]
    ppermute x2 -> x7, starting transfers between devices: 4.65 us -> 8.85 us  [the longest x6 6.93 us: ring(): lax.ppermute(array, 'dp', [(i, (i + by) % dp_size) for i in range(dp_size)])]
    all_to_all x1 -> x0, starting transfers between devices: 3.79 us -> none  [shards(): kv = lax.all_to_all(delivered, group, 0, 0, tiled=True)]
    slice x4 -> x0, local copies, waits for them, and re-layouts: 2.98 us -> none  [the longest x2 1.29 us: ahead(): return jnp.concatenate([own[SPAN - 1:], following[:SPAN - 1]], 0)]
    concatenate x2 -> x3, other arithmetic: 2.23 us -> 0.35 us  [the longest x1 0.15 us: shards(): jnp.concatenate([cross_grad[0, SPAN - 1:], following[1, :SPAN - 1]], 0)]
    pallas_call x3, Pallas kernels: 11.7 us -> 9.92 us  [the longest x1 6.94 us: shards(): pl.pallas_call(attention_kernel, grid=(spans,), out_shape=(jax.ShapeDtype...]
  transfers between devices with their start and end apart: 6 -> 10, of which waited for: 4 -> 8; matrix products, arithmetic and copies ran while one was open for 8% -> 4% of each run, Pallas kernels for 2% -> 1%
where the time goes in v2:
time: 97.6 us; the launch traced here: 97.2 us
  waiting for transfers between devices  56.4 us (58%)
  starting transfers between devices  21.6 us (22%)
  Pallas kernels  9.92 us (10%)
  local copies, waits for them, and re-layouts  6.88 us (7%)
  other arithmetic  1.63 us (2%)
    ppermute x6, waiting for transfers between devices, ring(): lax.ppermute(array, 'dp', [(i, (i + by) % dp_size) for i in range(dp_size)])  24.1 us
    all_to_all x1, waiting for transfers between devices, shards(): held = lax.all_to_all(spread, group, 0, 0, tiled=True)  16.1 us
    all_to_all x1, waiting for transfers between devices, shards(): final = lax.all_to_all(collected, group, 0, 0, tiled=True)  8.71 us
    all_to_all x1, starting transfers between devices, shards(): held = lax.all_to_all(spread, group, 0, 0, tiled=True)  7.17 us
    pallas_call x1, Pallas kernels, shards(): pl.pallas_call(attention_kernel, grid=(spans,), out_shape=(jax.ShapeDtype...  6.94 us
    ppermute x6, starting transfers between devices, ring(): lax.ppermute(array, 'dp', [(i, (i + by) % dp_size) for i in range(dp_size)])  6.93 us
    ppermute x1, waiting for transfers between devices, shards(): before = lax.ppermute(out_rows[row_count - SPAN:], 'context', forth)  5.7 us
    all_to_all x1, starting transfers between devices, shards(): final = lax.all_to_all(collected, group, 0, 0, tiled=True)  3.66 us
  transfers between devices with their start and end apart: 10, of which 8 were waited for; matrix products, arithmetic and copies ran while one was open for 4% of the time, Pallas kernels for 1%

profile of v2, /device:TPU:224, one launch (start us, length us, event | category | flops | bytes accessed | tf_op | source)
XLA Modules:
  0.0 97.2 jit_solution(1298271729126790888)
XLA Ops:
  0.6 0.0 copy-start
  0.6 1.7 %reshape.19 = bf16[2,2,4,32,4,256]{5,4,0,3,2,1:T(4,128)(2,1)S(1)} reshape(bf16[2,2,128,1024]{3,0,2,1:T(2,128)(2,1)} %bitcast.27) | data formatting | bytes 2097152 | tf_op jit(solution)/shard_map/reshape | solution.py:112
  2.4 1.2 %copy.9 = bf16[2,2,4,32,4,256]{5,3,1,0,4,2:T(8,128)(2,1)} copy(bf16[2,2,4,32,4,256]{5,4,0,3,2,1:T(4,128)(2,1)S(1)} %reshape.19) | data formatting | bytes 2097152 | tf_op jit(solution)/shard_map/reshape | solution.py:112
  3.6 0.0 copy-start.1
  3.6 7.2 %all-to-all-start = ((bf16[16,2,2,32,256]{4,3,2,1,0:T(8,128)(2,1)}), bf16[16,2,2,32,256]{4,3,2,1,0:T(8,128)(2,1)S(1)}, u32[]{:S(2)}, u32[]{:S(2)}) async-start(bf16[16,2,2,32,256]{4,3,2,1,0:T(8,128)(2,1)} %bitcast.3), calls=%async_computation | async-start | bytes 2097152 | tf_op jit(solution)/shard_map/all_to_all | solution.py:114
  10.8 0.0 copy-done
  10.8 0.1 constant_dynamic-slice_fusion
  10.9 0.1 copy.10
  11.0 0.1 reshape.21
  11.1 0.0 copy-done.1
  11.1 1.0 %slice_bitcast_fusion.4 = (bf16[64,2048]{1,0:T(8,128)(2,1)S(1)}, bf16[64,2048]{1,0:T(8,128)(2,1)S(1)}) fusion(bf16[1,256,2048]{2,1,0:T(8,128)(2,1)} %param.5, bf16[1,256,2048]{2,1,0:T(8,128)(2,1)S(1)} %copy-done.1), kind=kLoop, calls=%fused_computation.8 | loop fusion | bytes 1048576 | tf_op jit(solution)/shard_map/squeeze | solution.py:122
  12.1 0.2 slice_bitcast_fusion.1
  12.3 0.0 copy-start.2
  12.3 16.1 %all-to-all-done.held_ref = bf16[16,2,2,32,256]{4,3,2,1,0:T(8,128)(2,1)S(1)} async-done(((bf16[16,2,2,32,256]{4,3,2,1,0:T(8,128)(2,1)}), bf16[16,2,2,32,256]{4,3,2,1,0:T(8,128)(2,1)S(1)}, u32[]{:S(2)}, u32[]{:S(2)}) %all-to-all-start) | async-done | bytes 1048608 | tf_op jit(solution)/shard_map/all_to_all | solution.py:114
  28.4 0.1 pad_maximum_fusion.2
  28.5 1.9 %collective-permute-start = (bf16[2,64,2048]{2,1,0:T(8,128)(2,1)S(1)}, bf16[2,64,2048]{2,1,0:T(8,128)(2,1)S(1)}, u32[]{:S(2)}, u32[]{:S(2)}) collective-permute-start(bf16[2,64,2048]{2,1,0:T(8,128)(2,1)S(1)} %pad_maximum_fusion.2), channel_id=1, source_target_pairs={{4,0},{8,4},{12,8},{16,12},{20,16},{24,20},{28,24},{32,28},{36,32}... | collective-permute-start | bytes 1572872 | tf_op jit(solution)/shard_map/ppermute | solution.py:126
  30.4 0.1 pad_add_fusion.ids_ref
  30.5 0.0 copy-done.2
  30.5 0.2 slice_bitcast_fusion
  30.7 1.0 %deliver.1 = (bf16[8,2,32,256]{3,2,1,0:T(8,128)(2,1)S(1)}, bf16[8,2,32,256]{3,2,1,0:T(8,128)(2,1)S(1)}, bf16[8,2,32,256]{3,2,1,0:T(8,128)(2,1)S(1)}, bf16[8,2,32,256]{3,2,1,0:T(8,128)(2,1)S(1)}) custom-call(s32[33]{0:T(128)S(1)} %pad_add_fusion.ids_ref, bf16[16,2,2,32,256]{4,3,2,1,0:T(8,128)(2,1)S(1)} %all-to-all-done.held_ref), custom_call_target="tpu_custom_call" | custom-call | tf_op jit(solution)/shard_map/deliver/pallas_call | solution.py:131
  31.7 0.1 collective-permute-start.1
  31.8 1.8 %collective-permute-start.2 = (bf16[8,2,32,256]{3,2,1,0:T(8,128)(2,1)S(1)}, bf16[8,2,32,256]{3,2,1,0:T(8,128)(2,1)S(1)}, u32[]{:S(2)}, u32[]{:S(2)}) collective-permute-start(bf16[8,2,32,256]{3,2,1,0:T(8,128)(2,1)S(1)} %get-tuple-element.19), channel_id=1, source_target_pairs={{0,128},{64,192},{128,0},{192,64},{1,129},{65,193},{129,1},{193,65... | collective-permute-start | bytes 786440 | tf_op jit(solution)/shard_map/ppermute | solution.py:109
  33.6 1.7 %collective-permute-start.3 = (bf16[8,2,32,256]{3,2,1,0:T(8,128)(2,1)S(1)}, bf16[8,2,32,256]{3,2,1,0:T(8,128)(2,1)S(1)}, u32[]{:S(2)}, u32[]{:S(2)}) collective-permute-start(bf16[8,2,32,256]{3,2,1,0:T(8,128)(2,1)S(1)} %get-tuple-element.20), channel_id=1, source_target_pairs={{0,192},{64,0},{128,64},{192,128},{1,193},{65,1},{129,65},{193,129... | collective-permute-start | bytes 786440 | tf_op jit(solution)/shard_map/ppermute | solution.py:109
  35.3 1.8 %collective-permute-done = bf16[2,64,2048]{2,1,0:T(8,128)(2,1)S(1)} collective-permute-done((bf16[2,64,2048]{2,1,0:T(8,128)(2,1)S(1)}, bf16[2,64,2048]{2,1,0:T(8,128)(2,1)S(1)}, u32[]{:S(2)}, u32[]{:S(2)}) %collective-permute-start) | collective-permute-done | bytes 524320 | tf_op jit(solution)/shard_map/ppermute | solution.py:126
  37.1 0.1 pad_maximum_fusion.1.g_ref
  37.3 0.1 pad_maximum_fusion.q_ref
  37.4 9.9 %collective-permute-done.1.refs_1_ = bf16[8,2,32,256]{3,2,1,0:T(8,128)(2,1)S(1)} collective-permute-done((bf16[8,2,32,256]{3,2,1,0:T(8,128)(2,1)S(1)}, bf16[8,2,32,256]{3,2,1,0:T(8,128)(2,1)S(1)}, u32[]{:S(2)}, u32[]{:S(2)}) %collective-permute-start.1) | collective-permute-done | bytes 262176 | tf_op jit(solution)/shard_map/ppermute | solution.py:109
  47.3 0.0 collective-permute-done.2.refs_2_
  47.3 0.6 collective-permute-done.3.refs_3_
  48.0 6.9 %attention.1 = (bf16[256,2048]{1,0:T(8,128)(2,1)S(1)}, bf16[8,2,32,256]{3,2,1,0:T(8,128)(2,1)S(1)}, bf16[8,2,32,256]{3,2,1,0:T(8,128)(2,1)S(1)}, bf16[8,2,32,256...) custom-call(bf16[256,2048]{1,0:T(8,128)(2,1)S(1)} %pad_maximum_fusion.q_ref, ...), custom_call_target="tpu_custom_call" | custom-call | tf_op jit(solution)/shard_map/attention/pallas_call | solution.py:145
  54.9 2.4 %collective-permute-start.5 = (bf16[8,2,32,256]{3,2,1,0:T(8,128)(2,1)S(1)}, bf16[8,2,32,256]{3,2,1,0:T(8,128)(2,1)S(1)}, u32[]{:S(2)}, u32[]{:S(2)}) collective-permute-start(bf16[8,2,32,256]{3,2,1,0:T(8,128)(2,1)S(1)} %get-tuple-element.23), channel_id=1, source_target_pairs={{0,192},{64,0},{128,64},{192,128},{1,193},{65,1},{129,65},{193,129... | collective-permute-start | bytes 786440 | tf_op jit(solution)/shard_map/ppermute | solution.py:109
  57.3 0.0 collective-permute-start.6
  57.3 1.0 collective-permute-start.7
  58.3 10.2 %collective-permute-done.5.refs_1_ = bf16[8,2,32,256]{3,2,1,0:T(8,128)(2,1)S(1)} collective-permute-done((bf16[8,2,32,256]{3,2,1,0:T(8,128)(2,1)S(1)}, bf16[8,2,32,256]{3,2,1,0:T(8,128)(2,1)S(1)}, u32[]{:S(2)}, u32[]{:S(2)}) %collective-permute-start.5) | collective-permute-done | bytes 262176 | tf_op jit(solution)/shard_map/ppermute | solution.py:109
  68.4 0.0 collective-permute-done.6.refs_2_
  68.4 3.4 %collective-permute-done.7.refs_3_ = bf16[8,2,32,256]{3,2,1,0:T(8,128)(2,1)S(1)} collective-permute-done((bf16[8,2,32,256]{3,2,1,0:T(8,128)(2,1)S(1)}, bf16[8,2,32,256]{3,2,1,0:T(8,128)(2,1)S(1)}, u32[]{:S(2)}, u32[]{:S(2)}) %collective-permute-start.7) | collective-permute-done | bytes 262176 | tf_op jit(solution)/shard_map/ppermute | solution.py:109
  71.8 2.0 %collect.1 = bf16[16,2,2,32,256]{4,3,2,1,0:T(8,128)(2,1)} custom-call(s32[33]{0:T(128)S(1)} %pad_add_fusion.ids_ref, bf16[8,2,32,256]{3,2,1,0:T(8,128)(2,1)S(1)} %get-tuple-element.22.refs_0_, bf16[8,2,32,256]{3,2,1,0:T(8,128)(2,1)S(1)} %collective-permute-done.5.refs_1_, bf16[8,2,32,256]{3,2,1,0:T(8,128)(2,1)S(1)} %collective-permute-done.6.refs_2_, ...), custom_call_target="tpu_custom_call" | custom-call | tf_op jit(solution)/shard_map/collect/pallas_call | solution.py:162
  73.8 3.7 %all-to-all-start.1 = ((bf16[16,2,2,32,256]{4,3,2,1,0:T(8,128)(2,1)}), bf16[16,2,2,32,256]{4,3,2,1,0:T(8,128)(2,1)S(1)}, u32[]{:S(2)}, u32[]{:S(2)}) async-start(bf16[16,2,2,32,256]{4,3,2,1,0:T(8,128)(2,1)} %collect.1), calls=%async_computation.1 | async-start | bytes 2097152 | tf_op jit(solution)/shard_map/all_to_all | solution.py:170
  77.5 1.9 %collective-permute-start.4 = (bf16[64,2048]{1,0:T(8,128)(2,1)S(1)}, bf16[64,2048]{1,0:T(8,128)(2,1)S(1)}, u32[]{:S(2)}, u32[]{:S(2)}) collective-permute-start(bf16[64,2048]{1,0:T(8,128)(2,1)S(1)} %slice.33), channel_id=1, source_target_pairs={{0,4},{4,8},{8,12},{12,16},{16,20},{20,24},{24,28},{28,32},{32,36}... | collective-permute-start | bytes 786440 | tf_op jit(solution)/shard_map/ppermute | solution.py:159
  79.4 0.1 slice.35
  79.5 5.7 %collective-permute-done.4 = bf16[64,2048]{1,0:T(8,128)(2,1)S(1)} collective-permute-done((bf16[64,2048]{1,0:T(8,128)(2,1)S(1)}, bf16[64,2048]{1,0:T(8,128)(2,1)S(1)}, u32[]{:S(2)}, u32[]{:S(2)}) %collective-permute-start.4) | collective-permute-done | bytes 262176 | tf_op jit(solution)/shard_map/ppermute | solution.py:159
  85.2 0.1 slice.38
  85.3 1.2 %maximum_bitcast_fusion = bf16[1,256,2048]{2,1,0:T(8,128)(2,1)} fusion(bf16[193,2048]{1,0:T(8,128)(2,1)S(1)} %slice.35, bf16[63,2048]{1,0:T(8,128)(2,1)S(1)} %slice.38), kind=kLoop, calls=%fused_computation.2 | loop fusion | flops 2097152 | bytes 2097152 | tf_op jit(solution)/shard_map/broadcast_in_dim | solution.py:173
  86.5 8.7 %all-to-all-done.1 = bf16[16,2,2,32,256]{4,3,2,1,0:T(8,128)(2,1)S(1)} async-done(((bf16[16,2,2,32,256]{4,3,2,1,0:T(8,128)(2,1)}), bf16[16,2,2,32,256]{4,3,2,1,0:T(8,128)(2,1)S(1)}, u32[]{:S(2)}, u32[]{:S(2)}) %all-to-all-start.1) | async-done | bytes 1048608 | tf_op jit(solution)/shard_map/all_to_all | solution.py:170
  95.2 0.8 copy.11
  96.0 1.2 %reshape.23 = bf16[2,128,2,1024]{3,2,1,0:T(2,128)(2,1)} reshape(bf16[2,4,32,2,4,256]{5,4,3,2,1,0:T(4,128)(2,1)S(1)} %copy.11) | data formatting | bytes 2097152 | tf_op jit(solution)/shard_map/reshape | solution.py:173
  (2 shorter events, 0.1 us)
Async XLA Ops:
  0.6 10.2 %copy-start = (s32[4,64,2]{1,2,0:T(2,128)S(1)}, s32[4,64,2]{1,2,0:T(2,128)}, u32[]{:S(2)}) copy-start(s32[4,64,2]{1,2,0:T(2,128)} %param.7) | copy-start | bytes 6148
  3.6 7.5 %copy-start.1 = (bf16[1,256,2048]{2,1,0:T(8,128)(2,1)S(1)}, bf16[1,256,2048]{2,1,0:T(8,128)(2,1)}, u32[]{:S(2)}) copy-start(bf16[1,256,2048]{2,1,0:T(8,128)(2,1)} %param.4) | copy-start | bytes 3145732
  3.6 24.8 %all-to-all-start = ((bf16[16,2,2,32,256]{4,3,2,1,0:T(8,128)(2,1)}), bf16[16,2,2,32,256]{4,3,2,1,0:T(8,128)(2,1)S(1)}, u32[]{:S(2)}, u32[]{:S(2)}) async-start(bf16[16,2,2,32,256]{4,3,2,1,0:T(8,128)(2,1)} %bitcast.3), calls=%async_computation | async-start | bytes 2097152 | tf_op jit(solution)/shard_map/all_to_all | solution.py:114
  12.3 18.2 %copy-start.2 = (bf16[1,256,2048]{2,1,0:T(8,128)(2,1)S(1)}, bf16[1,256,2048]{2,1,0:T(8,128)(2,1)}, u32[]{:S(2)}) copy-start(bf16[1,256,2048]{2,1,0:T(8,128)(2,1)} %param.5) | copy-start | bytes 3145732
  28.5 8.6 %collective-permute-start = (bf16[2,64,2048]{2,1,0:T(8,128)(2,1)S(1)}, bf16[2,64,2048]{2,1,0:T(8,128)(2,1)S(1)}, u32[]{:S(2)}, u32[]{:S(2)}) collective-permute-start(bf16[2,64,2048]{2,1,0:T(8,128)(2,1)S(1)} %pad_maximum_fusion.2), channel_id=1, source_target_pairs={{4,0},{8,4},{12,8},{16,12},{20,16},{24,20},{28,24},{32,28},{36,32}... | collective-permute-start | bytes 1572872 | tf_op jit(solution)/shard_map/ppermute | solution.py:126
  31.7 15.6 %collective-permute-start.1 = (bf16[8,2,32,256]{3,2,1,0:T(8,128)(2,1)S(1)}, bf16[8,2,32,256]{3,2,1,0:T(8,128)(2,1)S(1)}, u32[]{:S(2)}, u32[]{:S(2)}) collective-permute-start(bf16[8,2,32,256]{3,2,1,0:T(8,128)(2,1)S(1)} %get-tuple-element.18), channel_id=1, source_target_pairs={{0,64},{64,128},{128,192},{192,0},{1,65},{65,129},{129,193},{193,1... | collective-permute-start | bytes 786440 | tf_op jit(solution)/shard_map/ppermute | solution.py:109
  31.8 15.6 %collective-permute-start.2 = (bf16[8,2,32,256]{3,2,1,0:T(8,128)(2,1)S(1)}, bf16[8,2,32,256]{3,2,1,0:T(8,128)(2,1)S(1)}, u32[]{:S(2)}, u32[]{:S(2)}) collective-permute-start(bf16[8,2,32,256]{3,2,1,0:T(8,128)(2,1)S(1)} %get-tuple-element.19), channel_id=1, source_target_pairs={{0,128},{64,192},{128,0},{192,64},{1,129},{65,193},{129,1},{193,65... | collective-permute-start | bytes 786440 | tf_op jit(solution)/shard_map/ppermute | solution.py:109
  33.6 14.4 %collective-permute-start.3 = (bf16[8,2,32,256]{3,2,1,0:T(8,128)(2,1)S(1)}, bf16[8,2,32,256]{3,2,1,0:T(8,128)(2,1)S(1)}, u32[]{:S(2)}, u32[]{:S(2)}) collective-permute-start(bf16[8,2,32,256]{3,2,1,0:T(8,128)(2,1)S(1)} %get-tuple-element.20), channel_id=1, source_target_pairs={{0,192},{64,0},{128,64},{192,128},{1,193},{65,1},{129,65},{193,129... | collective-permute-start | bytes 786440 | tf_op jit(solution)/shard_map/ppermute | solution.py:109
  54.9 13.5 %collective-permute-start.5 = (bf16[8,2,32,256]{3,2,1,0:T(8,128)(2,1)S(1)}, bf16[8,2,32,256]{3,2,1,0:T(8,128)(2,1)S(1)}, u32[]{:S(2)}, u32[]{:S(2)}) collective-permute-start(bf16[8,2,32,256]{3,2,1,0:T(8,128)(2,1)S(1)} %get-tuple-element.23), channel_id=1, source_target_pairs={{0,192},{64,0},{128,64},{192,128},{1,193},{65,1},{129,65},{193,129... | collective-permute-start | bytes 786440 | tf_op jit(solution)/shard_map/ppermute | solution.py:109
  57.3 11.1 %collective-permute-start.6 = (bf16[8,2,32,256]{3,2,1,0:T(8,128)(2,1)S(1)}, bf16[8,2,32,256]{3,2,1,0:T(8,128)(2,1)S(1)}, u32[]{:S(2)}, u32[]{:S(2)}) collective-permute-start(bf16[8,2,32,256]{3,2,1,0:T(8,128)(2,1)S(1)} %get-tuple-element.24), channel_id=1, source_target_pairs={{0,128},{64,192},{128,0},{192,64},{1,129},{65,193},{129,1},{193,65... | collective-permute-start | bytes 786440 | tf_op jit(solution)/shard_map/ppermute | solution.py:109
  57.3 14.5 %collective-permute-start.7 = (bf16[8,2,32,256]{3,2,1,0:T(8,128)(2,1)S(1)}, bf16[8,2,32,256]{3,2,1,0:T(8,128)(2,1)S(1)}, u32[]{:S(2)}, u32[]{:S(2)}) collective-permute-start(bf16[8,2,32,256]{3,2,1,0:T(8,128)(2,1)S(1)} %get-tuple-element.25), channel_id=1, source_target_pairs={{0,64},{64,128},{128,192},{192,0},{1,65},{65,129},{129,193},{193,1... | collective-permute-start | bytes 786440 | tf_op jit(solution)/shard_map/ppermute | solution.py:109
  73.8 21.4 %all-to-all-start.1 = ((bf16[16,2,2,32,256]{4,3,2,1,0:T(8,128)(2,1)}), bf16[16,2,2,32,256]{4,3,2,1,0:T(8,128)(2,1)S(1)}, u32[]{:S(2)}, u32[]{:S(2)}) async-start(bf16[16,2,2,32,256]{4,3,2,1,0:T(8,128)(2,1)} %collect.1), calls=%async_computation.1 | async-start | bytes 2097152 | tf_op jit(solution)/shard_map/all_to_all | solution.py:170
  77.5 7.7 %collective-permute-start.4 = (bf16[64,2048]{1,0:T(8,128)(2,1)S(1)}, bf16[64,2048]{1,0:T(8,128)(2,1)S(1)}, u32[]{:S(2)}, u32[]{:S(2)}) collective-permute-start(bf16[64,2048]{1,0:T(8,128)(2,1)S(1)} %slice.33), channel_id=1, source_target_pairs={{0,4},{4,8},{8,12},{12,16},{16,20},{20,24},{24,28},{28,32},{32,36}... | collective-permute-start | bytes 786440 | tf_op jit(solution)/shard_map/ppermute | solution.py:159

commit v3 on v2

v3 whole, which is shorter than its diff:
```python
import functools
import math

import jax
import jax.numpy as jnp
from jax import lax
from jax.experimental import pallas as pl
from jax.experimental.pallas import tpu as pltpu
from jax.sharding import PartitionSpec as P

HD = 128
SPAN = 64
NL = 128
KNB = 2
SLOTS = 2
CHUNKS = 2
LOG2E = 1.4426950408889634


def nt(a, b):
    return lax.dot_general(a, b, (((1,), (1,)), ((), ())), preferred_element_type=jnp.float32)


def nn(a, b):
    return lax.dot_general(a, b, (((1,), (0,)), ((), ())), preferred_element_type=jnp.float32)


def place_of(row, geometry):
    local_rows, context_size, tensor_size = geometry
    device = row // local_rows
    source = device // (context_size * tensor_size) * tensor_size + device % tensor_size
    return source, row % local_rows


def deliver_kernel(ids_ref, held_ref, *out_refs, owners, geometry):
    length = out_refs[0].shape[0]
    count = len(out_refs) // owners * length
    me = ids_ref[owners * count]
    for o, out_ref in enumerate(out_refs):
        owner = (me + o % owners) % owners
        for k in range(length):
            row = ids_ref[owner * count + o // owners * length + k]
            source, part = place_of(row, geometry)
            for slot in range(SLOTS):
                out_ref[k, slot] = held_ref[source, slot, part]


def collect_kernel(ids_ref, *refs, owners, geometry):
    held_refs, out_ref = refs[:-1], refs[-1]
    length = held_refs[0].shape[0]
    count = len(held_refs) // owners * length
    me = ids_ref[owners * count]
    for o, held_ref in enumerate(held_refs):
        owner = (me + o % owners) % owners
        for k in range(length):
            row = ids_ref[owner * count + o // owners * length + k]
            source, part = place_of(row, geometry)
            for slot in range(SLOTS):
                out_ref[source, slot, part] = held_ref[k, slot]


def attention_kernel(*refs, parts, halo):
    ahead_refs, refs = refs[:2], refs[2:]
    last_refs, refs = refs[:2], refs[2:]
    if halo:
        halo_refs, refs = refs[:2], refs[2:]
        at_end = pl.program_id(0) == pl.num_programs(0) - 1
    kv_refs, out_ref, grad_refs = refs[:parts], refs[parts], refs[parts + 1 :]
    rows = kv_refs[0].shape[2]
    kv_heads = kv_refs[0].shape[3] // HD
    groups = out_ref.shape[1] // (kv_heads * HD)
    tail = last_refs[0].shape[0]
    scale = 1.0 / math.sqrt(HD)
    places = [(p, n) for p in range(parts) for n in range(KNB)]
    swap = lax.broadcasted_iota(jnp.int32, (tail, HD), 0) == tail - 1

    def window(i, lanes):
        values = ahead_refs[i][:, lanes]
        if halo:
            values = jnp.where(at_end, halo_refs[i][:, lanes], values)
        end = jnp.where(swap, last_refs[i][:, lanes], values[SPAN - tail :])
        return [values[: SPAN - tail], end]

    for h in range(kv_heads):
        lanes = slice(h * HD, (h + 1) * HD)
        key = jnp.concatenate([kv_refs[p][n, 0, :, lanes] for p, n in places], 0)
        value = jnp.concatenate([kv_refs[p][n, 1, :, lanes] for p, n in places], 0)
        heads = [slice((h * groups + g) * HD, (h * groups + g + 1) * HD) for g in range(groups)]
        query = jnp.concatenate(sum([window(0, s) for s in heads], []), 0)
        grad = jnp.concatenate(sum([window(1, s) for s in heads], []), 0)
        scores = nt(key, query) * (scale * LOG2E)
        raised = jnp.exp2(scores - jnp.max(scores, axis=0, keepdims=True))
        weights = raised * (1.0 / jnp.sum(raised, axis=0, keepdims=True))
        low = weights.astype(jnp.bfloat16)
        out = nn(value.T, low).T.astype(jnp.bfloat16)
        for g, s in enumerate(heads):
            out_ref[:, s] = out[g * SPAN : (g + 1) * SPAN]
        value_grad = nn(low, grad).astype(jnp.bfloat16)
        slope = nt(value, grad)
        centre = jnp.sum(weights * slope, axis=0, keepdims=True)
        score_grad = (weights * (slope - centre) * scale).astype(jnp.bfloat16)
        key_grad = nn(score_grad, query).astype(jnp.bfloat16)
        for b, (p, n) in enumerate(places):
            grad_refs[p][n, 0, :, lanes] = key_grad[b * rows : (b + 1) * rows]
            grad_refs[p][n, 1, :, lanes] = value_grad[b * rows : (b + 1) * rows]


def shards(cross_query, cross_grad, neighbour_kv, span_neighbours):
    dp_size = lax.axis_size("dp")
    context_size = lax.axis_size("context")
    tensor_size = lax.axis_size("tensor")
    local_rows, _, _, kv_width = neighbour_kv.shape
    width = kv_width // tensor_size
    row_count, query_width = cross_query.shape[1:]
    spans = row_count // SPAN
    count = spans * KNB
    peers = dp_size * tensor_size
    rows = NL // dp_size
    geometry = (local_rows, context_size, tensor_size)
    group = ("dp", "tensor")
    params = pltpu.CompilerParams(vmem_limit_bytes=32 * 1024 * 1024)
    smem = pl.BlockSpec(memory_space=pltpu.SMEM)
    vmem = pl.BlockSpec(memory_space=pltpu.VMEM)

    def ring(array, by):
        return lax.ppermute(array, "dp", [(i, (i + by) % dp_size) for i in range(dp_size)])

    spread = neighbour_kv.transpose(2, 0, 1, 3)
    spread = spread.reshape(SLOTS, local_rows, dp_size, rows, tensor_size, width)
    spread = spread.transpose(2, 4, 0, 1, 3, 5).reshape(peers, SLOTS, local_rows, rows, width)
    ids = lax.dynamic_slice_in_dim(
        span_neighbours, lax.axis_index("context") * spans, spans, 1
    ).reshape(-1)
    ids = jnp.concatenate([ids, lax.axis_index("dp").astype(jnp.int32)[None]])
    query, grad = cross_query[0], cross_grad[0]
    spread, halo_rows = lax.optimization_barrier((spread, (query[:SPAN], grad[:SPAN])))
    held = lax.all_to_all(spread, group, 0, 0, tiled=True)

    back = [(i + 1, i) for i in range(context_size - 1)]
    forth = [(i, i + 1) for i in range(context_size - 1)]
    halo = [lax.ppermute(values, "context", back) for values in halo_rows]

    chunks = CHUNKS
    length = count // chunks
    chunk_rows = row_count // chunks
    part = jax.ShapeDtypeStruct((length, SLOTS, rows, width), jnp.bfloat16)
    delivered = pl.pallas_call(
        functools.partial(deliver_kernel, owners=dp_size, geometry=geometry),
        out_shape=(part,) * (dp_size * chunks),
        in_specs=[smem, vmem],
        out_specs=(vmem,) * (dp_size * chunks),
        compiler_params=params,
        name="deliver",
    )(ids, held)
    order = sorted(range(1, dp_size), key=lambda s: -min(s, dp_size - s))
    tail = 16
    per_chunk = spans // chunks
    block = pl.BlockSpec((SPAN, query_width), lambda w: (w, 0))
    only = pl.BlockSpec((SPAN, query_width), lambda w: (0, 0))
    kv_block = pl.BlockSpec((KNB, SLOTS, rows, width), lambda w: (w, 0, 0, 0))
    kv = []
    for c in range(chunks):
        mine = delivered[c * dp_size : (c + 1) * dp_size]
        arrived = {0: mine[0]}
        for s in order:
            arrived[s] = ring(mine[s], s)
        kv.append([arrived[s] for s in range(dp_size)])
    out_parts = []
    returned = []
    for c in range(chunks):
        ends = c == chunks - 1
        ahead = pl.BlockSpec(
            (SPAN, query_width),
            lambda w, c=c: (jnp.minimum(c * per_chunk + w + 1, spans - 1), 0),
        )
        last = pl.BlockSpec(
            (tail, query_width),
            lambda w, c=c: ((c * per_chunk + w + 1) * (SPAN // tail) - 1, 0),
        )
        out_rows, *kv_grads = pl.pallas_call(
            functools.partial(attention_kernel, parts=dp_size, halo=ends),
            grid=(per_chunk,),
            out_shape=(jax.ShapeDtypeStruct((chunk_rows, query_width), jnp.bfloat16),)
            + (part,) * dp_size,
            in_specs=[ahead, ahead, last, last] + [only] * (2 * ends) + [kv_block] * dp_size,
            out_specs=(block,) + (kv_block,) * dp_size,
            compiler_params=params,
            name="attention",
        )(query, grad, query, grad, *(halo if ends else []), *kv[c])
        out_parts.append(out_rows)
        arrived = {0: kv_grads[0]}
        for s in order:
            arrived[s] = ring(kv_grads[s], -s)
        returned += [arrived[s] for s in range(dp_size)]

    windows = jnp.concatenate(out_parts, 0)
    before = lax.ppermute(windows[row_count - SPAN :], "context", forth)
    position = lax.broadcasted_iota(jnp.int32, windows.shape, 0)
    cross_out = jnp.where(
        position % SPAN == SPAN - 1,
        windows,
        jnp.concatenate([before, windows[: row_count - SPAN]], 0),
    )
    collected = pl.pallas_call(
        functools.partial(collect_kernel, owners=dp_size, geometry=geometry),
        out_shape=jax.ShapeDtypeStruct(held.shape, jnp.bfloat16),
        in_specs=[smem] + [vmem] * (dp_size * chunks),
        out_specs=vmem,
        compiler_params=params,
        name="collect",
    )(ids, *returned)
    final = lax.all_to_all(collected, group, 0, 0, tiled=True)
    final = final.reshape(dp_size, tensor_size, SLOTS, local_rows, rows, width)
    final = final.transpose(3, 0, 4, 2, 1, 5)
    return (cross_out[None], final.reshape(neighbour_kv.shape))


def solution(mesh):
    return jax.shard_map(
        shards,
        mesh=mesh,
        in_specs=(
            P("dp", "context", "tensor"),
            P("dp", "context", "tensor"),
            P(("dp", "context", "tensor"), None, None, None),
            P(),
        ),
        out_specs=(P("dp", "context", "tensor"), P(("dp", "context", "tensor"), None, None, None)),
        check_vma=False,
    )
```

time: 97.6 us -> 87.1 us (0.89)
  waiting for transfers between devices: 56.4 us -> 34.3 us
  starting transfers between devices: 21.6 us -> 32.3 us
  Pallas kernels: 9.92 us -> 11 us
    ppermute x6 -> x12, waiting for transfers between devices: 24.1 us -> 11 us  [ring(): lax.ppermute(array, 'dp', [(i, (i + by) % dp_size) for i in range(dp_size)])]
    ppermute x6 -> x12, starting transfers between devices: 6.93 us -> 14.6 us  [ring(): lax.ppermute(array, 'dp', [(i, (i + by) % dp_size) for i in range(dp_size)])]
    all_to_all x1, waiting for transfers between devices: 16.1 us -> 12.3 us  [shards(): held = lax.all_to_all(spread, group, 0, 0, tiled=True)]
    all_to_all x1, waiting for transfers between devices: 8.71 us -> 5.31 us  [shards(): final = lax.all_to_all(collected, group, 0, 0, tiled=True)]
    ppermute x2 -> x3, starting transfers between devices: 3.84 us -> 6.86 us  [the longest x2 4.94 us: shards(): halo = [lax.ppermute(values, 'context', back) for values in halo_rows]]
    ppermute x2 -> x3, waiting for transfers between devices: 7.54 us -> 5.68 us  [the longest x1 5.68 us: shards(): before = lax.ppermute(windows[row_count - SPAN:], 'context', forth)]
    squeeze x4 -> x0, local copies, waits for them, and re-layouts: 1.44 us -> none  [the longest x1 1.02 us: shards(): cross_grad[0, :SPAN]]
    select_n x0 -> x1, other arithmetic: none -> 1.31 us  [shards(): jnp.where(position % SPAN == SPAN - 1, windows, jnp.concatenate([before,...]
  transfers between devices with their start and end apart: 10 -> 17, of which waited for: 8 -> 9; matrix products, arithmetic and copies ran while one was open for 4% -> 2% of each run, Pallas kernels for 1% -> 10%
where the time goes in v3:
time: 87.1 us; the launch traced here: 86.7 us
  waiting for transfers between devices  34.3 us (39%)
  starting transfers between devices  32.3 us (37%)
  Pallas kernels  11 us (13%)
  local copies, waits for them, and re-layouts  6.82 us (8%)
  other arithmetic  1.46 us (2%)
    ppermute x12, starting transfers between devices, ring(): lax.ppermute(array, 'dp', [(i, (i + by) % dp_size) for i in range(dp_size)])  14.6 us
    all_to_all x1, waiting for transfers between devices, shards(): held = lax.all_to_all(spread, group, 0, 0, tiled=True)  12.3 us
    ppermute x12, waiting for transfers between devices, ring(): lax.ppermute(array, 'dp', [(i, (i + by) % dp_size) for i in range(dp_size)])  11 us
    pallas_call x2, Pallas kernels, shards(): pl.pallas_call(functools.partial(attention_kernel, parts=dp_size, halo=en...  8 us
    all_to_all x1, starting transfers between devices, shards(): held = lax.all_to_all(spread, group, 0, 0, tiled=True)  7.03 us
    ppermute x1, waiting for transfers between devices, shards(): before = lax.ppermute(windows[row_count - SPAN:], 'context', forth)  5.68 us
    all_to_all x1, waiting for transfers between devices, shards(): final = lax.all_to_all(collected, group, 0, 0, tiled=True)  5.31 us
    ppermute x2, starting transfers between devices, shards(): halo = [lax.ppermute(values, 'context', back) for values in halo_rows]  4.94 us
  transfers between devices with their start and end apart: 17, of which 9 were waited for; matrix products, arithmetic and copies ran while one was open for 2% of the time, Pallas kernels for 10%

profile of v3, /device:TPU:224, one launch (start us, length us, event | category | flops | bytes accessed | tf_op | source)
XLA Modules:
  0.0 86.7 jit_solution(14704826104594394274)
XLA Ops:
  0.6 0.0 copy-start
  0.6 1.7 %reshape.135 = bf16[2,2,4,32,4,256]{5,4,0,3,2,1:T(4,128)(2,1)S(1)} reshape(bf16[2,2,128,1024]{3,0,2,1:T(2,128)(2,1)} %bitcast.33) | data formatting | bytes 2097152 | tf_op jit(solution)/shard_map/reshape | solution.py:129
  2.4 0.0 copy-start.1
  2.4 0.0 copy-start.2
  2.4 1.2 %copy.10 = bf16[2,2,4,32,4,256]{5,3,1,0,4,2:T(8,128)(2,1)} copy(bf16[2,2,4,32,4,256]{5,4,0,3,2,1:T(4,128)(2,1)S(1)} %reshape.135) | data formatting | bytes 2097152 | tf_op jit(solution)/shard_map/reshape | solution.py:129
  3.6 0.1 copy-done.1
  3.7 0.6 copy-done.2
  4.3 0.8 slice_bitcast_fusion
  5.1 7.0 %all-to-all-start = ((bf16[16,2,2,32,256]{4,3,2,1,0:T(8,128)(2,1)}), bf16[16,2,2,32,256]{4,3,2,1,0:T(8,128)(2,1)S(1)}, u32[]{:S(2)}, u32[]{:S(2)}) async-start(bf16[16,2,2,32,256]{4,3,2,1,0:T(8,128)(2,1)} %bitcast.31), calls=%async_computation | async-start | bytes 2097152 | tf_op jit(solution)/shard_map/all_to_all | solution.py:137
  12.2 2.1 %collective-permute-start.3 = (bf16[64,2048]{1,0:T(8,128)(2,1)}, bf16[64,2048]{1,0:T(8,128)(2,1)S(1)}, u32[]{:S(2)}, u32[]{:S(2)}) collective-permute-start(bf16[64,2048]{1,0:T(8,128)(2,1)} %get-tuple-element.29), channel_id=1, source_target_pairs={{4,0},{8,4},{12,8},{16,12},{20,16},{24,20},{28,24},{32,28},{36,32}... | collective-permute-start | bytes 786440 | tf_op jit(solution)/shard_map/ppermute | solution.py:141
  14.3 2.9 %collective-permute-start.4 = (bf16[64,2048]{1,0:T(8,128)(2,1)}, bf16[64,2048]{1,0:T(8,128)(2,1)}, u32[]{:S(2)}, u32[]{:S(2)}) collective-permute-start(bf16[64,2048]{1,0:T(8,128)(2,1)} %get-tuple-element.30), channel_id=1, source_target_pairs={{4,0},{8,4},{12,8},{16,12},{20,16},{24,20},{28,24},{32,28},{36,32}... | collective-permute-start | bytes 786440 | tf_op jit(solution)/shard_map/ppermute | solution.py:141
  17.1 0.0 copy-done
  17.2 0.1 constant_dynamic-slice_fusion
  17.2 0.1 copy.9
  17.3 0.1 reshape.134
  17.4 0.1 pad_add_fusion.ids_ref
  17.5 12.3 %all-to-all-done.held_ref = bf16[16,2,2,32,256]{4,3,2,1,0:T(8,128)(2,1)S(1)} async-done(((bf16[16,2,2,32,256]{4,3,2,1,0:T(8,128)(2,1)}), bf16[16,2,2,32,256]{4,3,2,1,0:T(8,128)(2,1)S(1)}, u32[]{:S(2)}, u32[]{:S(2)}) %all-to-all-start) | async-done | bytes 1048608 | tf_op jit(solution)/shard_map/all_to_all | solution.py:137
  29.8 1.0 %deliver.1 = (bf16[4,2,32,256]{3,2,1,0:T(8,128)(2,1)S(1)}, bf16[4,2,32,256]{3,2,1,0:T(8,128)(2,1)S(1)}, bf16[4,2,32,256]{3,2,1,0:T(8,128)(2,1)S(1)}, bf16[4,2,32...) custom-call(s32[33]{0:T(128)S(1)} %pad_add_fusion.ids_ref, ...), custom_call_target="tpu_custom_call" | custom-call | tf_op jit(solution)/shard_map/deliver/pallas_call | solution.py:147
  30.8 0.1 collective-permute-start.5
  30.9 1.8 %collective-permute-start.6 = (bf16[4,2,32,256]{3,2,1,0:T(8,128)(2,1)S(1)}, bf16[4,2,32,256]{3,2,1,0:T(8,128)(2,1)S(1)}, u32[]{:S(2)}, u32[]{:S(2)}) collective-permute-start(bf16[4,2,32,256]{3,2,1,0:T(8,128)(2,1)S(1)} %get-tuple-element.33), channel_id=1, source_target_pairs={{0,128},{64,192},{128,0},{192,64},{1,129},{65,193},{129,1},{193,65... | collective-permute-start | bytes 393224 | tf_op jit(solution)/shard_map/ppermute | solution.py:126
  32.7 1.7 %collective-permute-start.7 = (bf16[4,2,32,256]{3,2,1,0:T(8,128)(2,1)S(1)}, bf16[4,2,32,256]{3,2,1,0:T(8,128)(2,1)S(1)}, u32[]{:S(2)}, u32[]{:S(2)}) collective-permute-start(bf16[4,2,32,256]{3,2,1,0:T(8,128)(2,1)S(1)} %get-tuple-element.34), channel_id=1, source_target_pairs={{0,192},{64,0},{128,64},{192,128},{1,193},{65,1},{129,65},{193,129... | collective-permute-start | bytes 393224 | tf_op jit(solution)/shard_map/ppermute | solution.py:126
  34.4 0.0 collective-permute-done.3.refs_4_
  34.4 0.6 collective-permute-start
  35.0 0.0 collective-permute-done.4.refs_5_
  35.0 2.2 %collective-permute-start.1 = (bf16[4,2,32,256]{3,2,1,0:T(8,128)(2,1)S(1)}, bf16[4,2,32,256]{3,2,1,0:T(8,128)(2,1)S(1)}, u32[]{:S(2)}, u32[]{:S(2)}) collective-permute-start(bf16[4,2,32,256]{3,2,1,0:T(8,128)(2,1)S(1)} %get-tuple-element.26), channel_id=1, source_target_pairs={{0,128},{64,192},{128,0},{192,64},{1,129},{65,193},{129,1},{193,65... | collective-permute-start | bytes 393224 | tf_op jit(solution)/shard_map/ppermute | solution.py:126
  37.2 3.9 %collective-permute-done.5.refs_7_ = bf16[4,2,32,256]{3,2,1,0:T(8,128)(2,1)S(1)} collective-permute-done((bf16[4,2,32,256]{3,2,1,0:T(8,128)(2,1)S(1)}, bf16[4,2,32,256]{3,2,1,0:T(8,128)(2,1)S(1)}, u32[]{:S(2)}, u32[]{:S(2)}) %collective-permute-start.5) | collective-permute-done | bytes 131104 | tf_op jit(solution)/shard_map/ppermute | solution.py:126
  41.1 0.0 collective-permute-start.2
  41.1 0.0 collective-permute-done.6.refs_8_
  41.1 0.6 collective-permute-done.7.refs_9_
  41.7 4.5 %attention.3 = (bf16[128,2048]{1,0:T(8,128)(2,1)S(1)}, bf16[4,2,32,256]{3,2,1,0:T(8,128)(2,1)S(1)}, bf16[4,2,32,256]{3,2,1,0:T(8,128)(2,1)S(1)}, bf16[4,2,32,256...) custom-call(bf16[256,2048]{1,0:T(8,128)(2,1)S(1)} %bitcast.21, bf16[256,2048]{1,0:T(8,128)(2,1)S(1)} %bitcast.25, ...), custom_call_target="tpu_custom_call" | custom-call | tf_op jit(solution)/shard_map/attention/pallas_call | solution.py:180
  46.2 2.6 %collective-permute-start.12 = (bf16[4,2,32,256]{3,2,1,0:T(8,128)(2,1)S(1)}, bf16[4,2,32,256]{3,2,1,0:T(8,128)(2,1)S(1)}, u32[]{:S(2)}, u32[]{:S(2)}) collective-permute-start(bf16[4,2,32,256]{3,2,1,0:T(8,128)(2,1)S(1)} %get-tuple-element.41), channel_id=1, source_target_pairs={{0,192},{64,0},{128,64},{192,128},{1,193},{65,1},{129,65},{193,129... | collective-permute-start | bytes 393224 | tf_op jit(solution)/shard_map/ppermute | solution.py:126
  48.8 0.9 %collective-permute-start.13 = (bf16[4,2,32,256]{3,2,1,0:T(8,128)(2,1)S(1)}, bf16[4,2,32,256]{3,2,1,0:T(8,128)(2,1)S(1)}, u32[]{:S(2)}, u32[]{:S(2)}) collective-permute-start(bf16[4,2,32,256]{3,2,1,0:T(8,128)(2,1)S(1)} %get-tuple-element.42), channel_id=1, source_target_pairs={{0,128},{64,192},{128,0},{192,64},{1,129},{65,193},{129,1},{193,65... | collective-permute-start | bytes 393224 | tf_op jit(solution)/shard_map/ppermute | solution.py:126
  49.7 0.0 collective-permute-done.refs_5_
  49.7 0.0 collective-permute-start.14
  49.8 0.0 collective-permute-done.1.refs_6_
  49.8 0.0 collective-permute-done.2.refs_7_
  49.8 3.5 %attention.2 = (bf16[128,2048]{1,0:T(8,128)(2,1)S(1)}, bf16[4,2,32,256]{3,2,1,0:T(8,128)(2,1)S(1)}, bf16[4,2,32,256]{3,2,1,0:T(8,128)(2,1)S(1)}, bf16[4,2,32,256...) custom-call(bf16[256,2048]{1,0:T(8,128)(2,1)S(1)} %bitcast.23, bf16[256,2048]{1,0:T(8,128)(2,1)S(1)} %bitcast.27, ...), custom_call_target="tpu_custom_call" | custom-call | tf_op jit(solution)/shard_map/attention/pallas_call | solution.py:180
  53.3 3.3 %collective-permute-start.9 = (bf16[4,2,32,256]{3,2,1,0:T(8,128)(2,1)S(1)}, bf16[4,2,32,256]{3,2,1,0:T(8,128)(2,1)S(1)}, u32[]{:S(2)}, u32[]{:S(2)}) collective-permute-start(bf16[4,2,32,256]{3,2,1,0:T(8,128)(2,1)S(1)} %get-tuple-element.37), channel_id=1, source_target_pairs={{0,192},{64,0},{128,64},{192,128},{1,193},{65,1},{129,65},{193,129... | collective-permute-start | bytes 393224 | tf_op jit(solution)/shard_map/ppermute | solution.py:126
  56.6 1.4 %collective-permute-start.10 = (bf16[4,2,32,256]{3,2,1,0:T(8,128)(2,1)S(1)}, bf16[4,2,32,256]{3,2,1,0:T(8,128)(2,1)S(1)}, u32[]{:S(2)}, u32[]{:S(2)}) collective-permute-start(bf16[4,2,32,256]{3,2,1,0:T(8,128)(2,1)S(1)} %get-tuple-element.38), channel_id=1, source_target_pairs={{0,128},{64,192},{128,0},{192,64},{1,129},{65,193},{129,1},{193,65... | collective-permute-start | bytes 393224 | tf_op jit(solution)/shard_map/ppermute | solution.py:126
  58.0 0.0 collective-permute-done.12.refs_5_
  58.0 0.0 collective-permute-start.11
  58.0 0.0 collective-permute-done.13.refs_6_
  58.0 1.1 %collective-permute-done.14.refs_7_ = bf16[4,2,32,256]{3,2,1,0:T(8,128)(2,1)S(1)} collective-permute-done((bf16[4,2,32,256]{3,2,1,0:T(8,128)(2,1)S(1)}, bf16[4,2,32,256]{3,2,1,0:T(8,128)(2,1)S(1)}, u32[]{:S(2)}, u32[]{:S(2)}) %collective-permute-start.14) | collective-permute-done | bytes 131104 | tf_op jit(solution)/shard_map/ppermute | solution.py:126
  59.1 1.4 %collective-permute-done.9.refs_1_ = bf16[4,2,32,256]{3,2,1,0:T(8,128)(2,1)S(1)} collective-permute-done((bf16[4,2,32,256]{3,2,1,0:T(8,128)(2,1)S(1)}, bf16[4,2,32,256]{3,2,1,0:T(8,128)(2,1)S(1)}, u32[]{:S(2)}, u32[]{:S(2)}) %collective-permute-start.9) | collective-permute-done | bytes 131104 | tf_op jit(solution)/shard_map/ppermute | solution.py:126
  60.5 2.6 %collective-permute-done.10.refs_2_ = bf16[4,2,32,256]{3,2,1,0:T(8,128)(2,1)S(1)} collective-permute-done((bf16[4,2,32,256]{3,2,1,0:T(8,128)(2,1)S(1)}, bf16[4,2,32,256]{3,2,1,0:T(8,128)(2,1)S(1)}, u32[]{:S(2)}, u32[]{:S(2)}) %collective-permute-start.10) | collective-permute-done | bytes 131104 | tf_op jit(solution)/shard_map/ppermute | solution.py:126
  63.1 1.4 %collective-permute-done.11.refs_3_ = bf16[4,2,32,256]{3,2,1,0:T(8,128)(2,1)S(1)} collective-permute-done((bf16[4,2,32,256]{3,2,1,0:T(8,128)(2,1)S(1)}, bf16[4,2,32,256]{3,2,1,0:T(8,128)(2,1)S(1)}, u32[]{:S(2)}, u32[]{:S(2)}) %collective-permute-start.11) | collective-permute-done | bytes 131104 | tf_op jit(solution)/shard_map/ppermute | solution.py:126
  64.5 2.0 %collect.1 = bf16[16,2,2,32,256]{4,3,2,1,0:T(8,128)(2,1)} custom-call(s32[33]{0:T(128)S(1)} %pad_add_fusion.ids_ref, bf16[4,2,32,256]{3,2,1,0:T(8,128)(2,1)S(1)} %get-tuple-element.36.refs_0_, bf16[4,2,32,256]{3,2,1,0:T(8,128)(2,1)S(1)} %collective-permute-done.9.refs_1_, bf16[4,2,32,256]{3,2,1,0:T(8,128)(2,1)S(1)} %collective-permute-done.10.refs_2_, ...), custom_call_target="tpu_custom_call" | custom-call | tf_op jit(solution)/shard_map/collect/pallas_call | solution.py:204
  66.5 3.8 %all-to-all-start.1 = ((bf16[16,2,2,32,256]{4,3,2,1,0:T(8,128)(2,1)}), bf16[16,2,2,32,256]{4,3,2,1,0:T(8,128)(2,1)S(1)}, u32[]{:S(2)}, u32[]{:S(2)}) async-start(bf16[16,2,2,32,256]{4,3,2,1,0:T(8,128)(2,1)} %collect.1), calls=%async_computation.1 | async-start | bytes 2097152 | tf_op jit(solution)/shard_map/all_to_all | solution.py:212
  70.3 1.9 %collective-permute-start.8 = (bf16[64,2048]{1,0:T(8,128)(2,1)S(1)}, bf16[64,2048]{1,0:T(8,128)(2,1)S(1)}, u32[]{:S(2)}, u32[]{:S(2)}) collective-permute-start(bf16[64,2048]{1,0:T(8,128)(2,1)S(1)} %slice.22), channel_id=1, source_target_pairs={{0,4},{4,8},{8,12},{12,16},{16,20},{20,24},{24,28},{28,32},{32,36}... | collective-permute-start | bytes 786440 | tf_op jit(solution)/shard_map/ppermute | solution.py:197
  72.3 0.1 fusion.1
  72.3 5.7 %collective-permute-done.8 = bf16[64,2048]{1,0:T(8,128)(2,1)S(1)} collective-permute-done((bf16[64,2048]{1,0:T(8,128)(2,1)S(1)}, bf16[64,2048]{1,0:T(8,128)(2,1)S(1)}, u32[]{:S(2)}, u32[]{:S(2)}) %collective-permute-start.8) | collective-permute-done | bytes 262176 | tf_op jit(solution)/shard_map/ppermute | solution.py:197
  78.0 1.3 %fusion = bf16[1,256,2048]{2,1,0:T(8,128)(2,1)} fusion(bf16[1,128,2048]{2,1,0:T(8,128)(2,1)S(1)} %bitcast.29, bf16[1,128,2048]{2,1,0:T(8,128)(2,1)S(1)} %bitcast.30, bf16[1,192,2048]{2,1,0:T(8,128)(2,1)S(1)} %fusion.1, bf16[1,64,2048]{2,1,0:T(8,128)(2,1)S(1)} %bitcast.34, s32[256]{0:T(256)S(1)} %get-tuple-element.46, s32[256]{0:T(256)S(1)} %get-tuple-element.47, ...), kind=kLoop, calls=%fused_computation.1 | loop fusion | flops 5767168 | bytes 3148032 | tf_op jit(solution)/shard_map/jit(_where)/select_n | solution.py:199
  79.3 5.3 %all-to-all-done.1 = bf16[16,2,2,32,256]{4,3,2,1,0:T(8,128)(2,1)S(1)} async-done(((bf16[16,2,2,32,256]{4,3,2,1,0:T(8,128)(2,1)}), bf16[16,2,2,32,256]{4,3,2,1,0:T(8,128)(2,1)S(1)}, u32[]{:S(2)}, u32[]{:S(2)}) %all-to-all-start.1) | async-done | bytes 1048608 | tf_op jit(solution)/shard_map/all_to_all | solution.py:212
  84.6 0.8 copy.11
  85.5 1.2 %reshape.138 = bf16[2,128,2,1024]{3,2,1,0:T(2,128)(2,1)} reshape(bf16[2,4,32,2,4,256]{5,4,3,2,1,0:T(4,128)(2,1)S(1)} %copy.11) | data formatting | bytes 2097152 | tf_op jit(solution)/shard_map/reshape | solution.py:215
  (3 shorter events, 0.0 us)
Async XLA Ops:
  0.6 16.5 %copy-start = (s32[4,64,2]{1,2,0:T(2,128)S(1)}, s32[4,64,2]{1,2,0:T(2,128)}, u32[]{:S(2)}) copy-start(s32[4,64,2]{1,2,0:T(2,128)} %param.7) | copy-start | bytes 6148
  2.4 1.3 %copy-start.1 = (bf16[1,256,2048]{2,1,0:T(8,128)(2,1)S(1)}, bf16[1,256,2048]{2,1,0:T(8,128)(2,1)}, u32[]{:S(2)}) copy-start(bf16[1,256,2048]{2,1,0:T(8,128)(2,1)} %param.4) | copy-start | bytes 3145732
  2.4 1.9 %copy-start.2 = (bf16[1,256,2048]{2,1,0:T(8,128)(2,1)S(1)}, bf16[1,256,2048]{2,1,0:T(8,128)(2,1)}, u32[]{:S(2)}) copy-start(bf16[1,256,2048]{2,1,0:T(8,128)(2,1)} %param.5) | copy-start | bytes 3145732
  5.1 24.7 %all-to-all-start = ((bf16[16,2,2,32,256]{4,3,2,1,0:T(8,128)(2,1)}), bf16[16,2,2,32,256]{4,3,2,1,0:T(8,128)(2,1)S(1)}, u32[]{:S(2)}, u32[]{:S(2)}) async-start(bf16[16,2,2,32,256]{4,3,2,1,0:T(8,128)(2,1)} %bitcast.31), calls=%async_computation | async-start | bytes 2097152 | tf_op jit(solution)/shard_map/all_to_all | solution.py:137
  12.2 22.2 %collective-permute-start.3 = (bf16[64,2048]{1,0:T(8,128)(2,1)}, bf16[64,2048]{1,0:T(8,128)(2,1)S(1)}, u32[]{:S(2)}, u32[]{:S(2)}) collective-permute-start(bf16[64,2048]{1,0:T(8,128)(2,1)} %get-tuple-element.29), channel_id=1, source_target_pairs={{4,0},{8,4},{12,8},{16,12},{20,16},{24,20},{28,24},{32,28},{36,32}... | collective-permute-start | bytes 786440 | tf_op jit(solution)/shard_map/ppermute | solution.py:141
  14.3 20.7 %collective-permute-start.4 = (bf16[64,2048]{1,0:T(8,128)(2,1)}, bf16[64,2048]{1,0:T(8,128)(2,1)}, u32[]{:S(2)}, u32[]{:S(2)}) collective-permute-start(bf16[64,2048]{1,0:T(8,128)(2,1)} %get-tuple-element.30), channel_id=1, source_target_pairs={{4,0},{8,4},{12,8},{16,12},{20,16},{24,20},{28,24},{32,28},{36,32}... | collective-permute-start | bytes 786440 | tf_op jit(solution)/shard_map/ppermute | solution.py:141
  30.8 10.2 %collective-permute-start.5 = (bf16[4,2,32,256]{3,2,1,0:T(8,128)(2,1)S(1)}, bf16[4,2,32,256]{3,2,1,0:T(8,128)(2,1)S(1)}, u32[]{:S(2)}, u32[]{:S(2)}) collective-permute-start(bf16[4,2,32,256]{3,2,1,0:T(8,128)(2,1)S(1)} %get-tuple-element.32), channel_id=1, source_target_pairs={{0,64},{64,128},{128,192},{192,0},{1,65},{65,129},{129,193},{193,1... | collective-permute-start | bytes 393224 | tf_op jit(solution)/shard_map/ppermute | solution.py:126
  30.9 10.2 %collective-permute-start.6 = (bf16[4,2,32,256]{3,2,1,0:T(8,128)(2,1)S(1)}, bf16[4,2,32,256]{3,2,1,0:T(8,128)(2,1)S(1)}, u32[]{:S(2)}, u32[]{:S(2)}) collective-permute-start(bf16[4,2,32,256]{3,2,1,0:T(8,128)(2,1)S(1)} %get-tuple-element.33), channel_id=1, source_target_pairs={{0,128},{64,192},{128,0},{192,64},{1,129},{65,193},{129,1},{193,65... | collective-permute-start | bytes 393224 | tf_op jit(solution)/shard_map/ppermute | solution.py:126
  32.7 9.0 %collective-permute-start.7 = (bf16[4,2,32,256]{3,2,1,0:T(8,128)(2,1)S(1)}, bf16[4,2,32,256]{3,2,1,0:T(8,128)(2,1)S(1)}, u32[]{:S(2)}, u32[]{:S(2)}) collective-permute-start(bf16[4,2,32,256]{3,2,1,0:T(8,128)(2,1)S(1)} %get-tuple-element.34), channel_id=1, source_target_pairs={{0,192},{64,0},{128,64},{192,128},{1,193},{65,1},{129,65},{193,129... | collective-permute-start | bytes 393224 | tf_op jit(solution)/shard_map/ppermute | solution.py:126
  34.4 15.4 %collective-permute-start = (bf16[4,2,32,256]{3,2,1,0:T(8,128)(2,1)S(1)}, bf16[4,2,32,256]{3,2,1,0:T(8,128)(2,1)S(1)}, u32[]{:S(2)}, u32[]{:S(2)}) collective-permute-start(bf16[4,2,32,256]{3,2,1,0:T(8,128)(2,1)S(1)} %get-tuple-element.25), channel_id=1, source_target_pairs={{0,64},{64,128},{128,192},{192,0},{1,65},{65,129},{129,193},{193,1... | collective-permute-start | bytes 393224 | tf_op jit(solution)/shard_map/ppermute | solution.py:126
  35.0 14.8 %collective-permute-start.1 = (bf16[4,2,32,256]{3,2,1,0:T(8,128)(2,1)S(1)}, bf16[4,2,32,256]{3,2,1,0:T(8,128)(2,1)S(1)}, u32[]{:S(2)}, u32[]{:S(2)}) collective-permute-start(bf16[4,2,32,256]{3,2,1,0:T(8,128)(2,1)S(1)} %get-tuple-element.26), channel_id=1, source_target_pairs={{0,128},{64,192},{128,0},{192,64},{1,129},{65,193},{129,1},{193,65... | collective-permute-start | bytes 393224 | tf_op jit(solution)/shard_map/ppermute | solution.py:126
  41.1 8.7 %collective-permute-start.2 = (bf16[4,2,32,256]{3,2,1,0:T(8,128)(2,1)S(1)}, bf16[4,2,32,256]{3,2,1,0:T(8,128)(2,1)S(1)}, u32[]{:S(2)}, u32[]{:S(2)}) collective-permute-start(bf16[4,2,32,256]{3,2,1,0:T(8,128)(2,1)S(1)} %get-tuple-element.27), channel_id=1, source_target_pairs={{0,192},{64,0},{128,64},{192,128},{1,193},{65,1},{129,65},{193,129... | collective-permute-start | bytes 393224 | tf_op jit(solution)/shard_map/ppermute | solution.py:126
  46.2 11.8 %collective-permute-start.12 = (bf16[4,2,32,256]{3,2,1,0:T(8,128)(2,1)S(1)}, bf16[4,2,32,256]{3,2,1,0:T(8,128)(2,1)S(1)}, u32[]{:S(2)}, u32[]{:S(2)}) collective-permute-start(bf16[4,2,32,256]{3,2,1,0:T(8,128)(2,1)S(1)} %get-tuple-element.41), channel_id=1, source_target_pairs={{0,192},{64,0},{128,64},{192,128},{1,193},{65,1},{129,65},{193,129... | collective-permute-start | bytes 393224 | tf_op jit(solution)/shard_map/ppermute | solution.py:126
  48.8 9.2 %collective-permute-start.13 = (bf16[4,2,32,256]{3,2,1,0:T(8,128)(2,1)S(1)}, bf16[4,2,32,256]{3,2,1,0:T(8,128)(2,1)S(1)}, u32[]{:S(2)}, u32[]{:S(2)}) collective-permute-start(bf16[4,2,32,256]{3,2,1,0:T(8,128)(2,1)S(1)} %get-tuple-element.42), channel_id=1, source_target_pairs={{0,128},{64,192},{128,0},{192,64},{1,129},{65,193},{129,1},{193,65... | collective-permute-start | bytes 393224 | tf_op jit(solution)/shard_map/ppermute | solution.py:126
  49.7 9.3 %collective-permute-start.14 = (bf16[4,2,32,256]{3,2,1,0:T(8,128)(2,1)S(1)}, bf16[4,2,32,256]{3,2,1,0:T(8,128)(2,1)S(1)}, u32[]{:S(2)}, u32[]{:S(2)}) collective-permute-start(bf16[4,2,32,256]{3,2,1,0:T(8,128)(2,1)S(1)} %get-tuple-element.43), channel_id=1, source_target_pairs={{0,64},{64,128},{128,192},{192,0},{1,65},{65,129},{129,193},{193,1... | collective-permute-start | bytes 393224 | tf_op jit(solution)/shard_map/ppermute | solution.py:126
  53.3 7.2 %collective-permute-start.9 = (bf16[4,2,32,256]{3,2,1,0:T(8,128)(2,1)S(1)}, bf16[4,2,32,256]{3,2,1,0:T(8,128)(2,1)S(1)}, u32[]{:S(2)}, u32[]{:S(2)}) collective-permute-start(bf16[4,2,32,256]{3,2,1,0:T(8,128)(2,1)S(1)} %get-tuple-element.37), channel_id=1, source_target_pairs={{0,192},{64,0},{128,64},{192,128},{1,193},{65,1},{129,65},{193,129... | collective-permute-start | bytes 393224 | tf_op jit(solution)/shard_map/ppermute | solution.py:126
  56.6 6.5 %collective-permute-start.10 = (bf16[4,2,32,256]{3,2,1,0:T(8,128)(2,1)S(1)}, bf16[4,2,32,256]{3,2,1,0:T(8,128)(2,1)S(1)}, u32[]{:S(2)}, u32[]{:S(2)}) collective-permute-start(bf16[4,2,32,256]{3,2,1,0:T(8,128)(2,1)S(1)} %get-tuple-element.38), channel_id=1, source_target_pairs={{0,128},{64,192},{128,0},{192,64},{1,129},{65,193},{129,1},{193,65... | collective-permute-start | bytes 393224 | tf_op jit(solution)/shard_map/ppermute | solution.py:126
  58.0 6.5 %collective-permute-start.11 = (bf16[4,2,32,256]{3,2,1,0:T(8,128)(2,1)S(1)}, bf16[4,2,32,256]{3,2,1,0:T(8,128)(2,1)S(1)}, u32[]{:S(2)}, u32[]{:S(2)}) collective-permute-start(bf16[4,2,32,256]{3,2,1,0:T(8,128)(2,1)S(1)} %get-tuple-element.39), channel_id=1, source_target_pairs={{0,64},{64,128},{128,192},{192,0},{1,65},{65,129},{129,193},{193,1... | collective-permute-start | bytes 393224 | tf_op jit(solution)/shard_map/ppermute | solution.py:126
  66.5 18.2 %all-to-all-start.1 = ((bf16[16,2,2,32,256]{4,3,2,1,0:T(8,128)(2,1)}), bf16[16,2,2,32,256]{4,3,2,1,0:T(8,128)(2,1)S(1)}, u32[]{:S(2)}, u32[]{:S(2)}) async-start(bf16[16,2,2,32,256]{4,3,2,1,0:T(8,128)(2,1)} %collect.1), calls=%async_computation.1 | async-start | bytes 2097152 | tf_op jit(solution)/shard_map/all_to_all | solution.py:212
  70.3 7.7 %collective-permute-start.8 = (bf16[64,2048]{1,0:T(8,128)(2,1)S(1)}, bf16[64,2048]{1,0:T(8,128)(2,1)S(1)}, u32[]{:S(2)}, u32[]{:S(2)}) collective-permute-start(bf16[64,2048]{1,0:T(8,128)(2,1)S(1)} %slice.22), channel_id=1, source_target_pairs={{0,4},{4,8},{8,12},{12,16},{16,20},{20,24},{24,28},{28,32},{32,36}... | collective-permute-start | bytes 786440 | tf_op jit(solution)/shard_map/ppermute | solution.py:197

commit v4 on v3

v4 whole, which is shorter than its diff:
```python
import functools
import math

import jax
import jax.numpy as jnp
from jax import lax
from jax.experimental import pallas as pl
from jax.experimental.pallas import tpu as pltpu
from jax.sharding import PartitionSpec as P

HD = 128
SPAN = 64
NL = 128
KNB = 2
SLOTS = 2
CHUNKS = 2
TAIL = 16
LOG2E = 1.4426950408889634


def nt(a, b):
    return lax.dot_general(a, b, (((1,), (1,)), ((), ())), preferred_element_type=jnp.float32)


def nn(a, b):
    return lax.dot_general(a, b, (((1,), (0,)), ((), ())), preferred_element_type=jnp.float32)


def place_of(row, geometry):
    local_rows, dp_size, context_size, tensor_size = geometry
    device = row // local_rows
    source = device % tensor_size * dp_size + device // (context_size * tensor_size)
    return source, row % local_rows


def deliver_kernel(ids_ref, held_ref, *out_refs, owners, geometry):
    length = out_refs[0].shape[0]
    count = len(out_refs) // owners * length
    me = ids_ref[owners * count]
    for o, out_ref in enumerate(out_refs):
        owner = (me + o % owners) % owners
        for k in range(length):
            row = ids_ref[owner * count + o // owners * length + k]
            source, part = place_of(row, geometry)
            for slot in range(SLOTS):
                out_ref[k, slot] = held_ref[source, slot, part]


def collect_kernel(ids_ref, *refs, owners, geometry):
    held_refs, out_ref = refs[:-1], refs[-1]
    length = held_refs[0].shape[0]
    count = len(held_refs) // owners * length
    me = ids_ref[owners * count]
    for o, held_ref in enumerate(held_refs):
        owner = (me + o % owners) % owners
        for k in range(length):
            row = ids_ref[owner * count + o // owners * length + k]
            source, part = place_of(row, geometry)
            for slot in range(SLOTS):
                out_ref[source, slot, part] = held_ref[k, slot]


def attention_kernel(q_ref, g_ref, *refs, parts, halo, first):
    if halo:
        halo_q_ref, halo_g_ref, *refs = refs
    kv_refs, out_ref, grad_refs = refs[:parts], refs[parts], refs[parts + 1 :]
    rows = kv_refs[0].shape[2]
    kv_heads = kv_refs[0].shape[3] // HD
    groups = out_ref.shape[1] // (kv_heads * HD)
    spans = out_ref.shape[0] // SPAN
    scale = 1.0 / math.sqrt(HD)
    swap = lax.broadcasted_iota(jnp.int32, (TAIL, HD), 0) == TAIL - 1

    def window(ref, halo_ref, span, lanes):
        end = (first + span + 1) * SPAN
        source, start = (halo_ref, 0) if halo and span == spans - 1 else (ref, end)
        stop = start + SPAN - TAIL
        tail = jnp.where(swap, ref[end - TAIL : end, lanes], source[stop : stop + TAIL, lanes])
        return [source[start:stop, lanes], tail]

    def load(span, h):
        places = [(p, span * KNB + n) for p in range(parts) for n in range(KNB)]
        lanes = slice(h * HD, (h + 1) * HD)
        heads = [slice((h * groups + g) * HD, (h * groups + g + 1) * HD) for g in range(groups)]
        key = jnp.concatenate([kv_refs[p][n, 0, :, lanes] for p, n in places], 0)
        value = jnp.concatenate([kv_refs[p][n, 1, :, lanes] for p, n in places], 0)
        halos = (halo_q_ref, halo_g_ref) if halo else (None, None)
        query, grad = (
            jnp.concatenate(sum([window(ref, halo_ref, span, s) for s in heads], []), 0)
            for ref, halo_ref in zip((q_ref, g_ref), halos)
        )
        return places, lanes, heads, key, value, query, grad

    for span in range(spans):
        loaded = [load(span, h) for h in range(kv_heads)]
        all_scores = [nt(key, query) for _, _, _, key, _, query, _ in loaded]
        slopes = [nt(value, grad) for _, _, _, _, value, _, grad in loaded]
        all_weights = []
        for scores in all_scores:
            scores = scores * (scale * LOG2E)
            raised = jnp.exp2(scores - jnp.max(scores, axis=0, keepdims=True))
            all_weights.append(raised * (1.0 / jnp.sum(raised, axis=0, keepdims=True)))
        for (places, lanes, heads, key, value, query, grad), weights, slope in zip(
            loaded, all_weights, slopes
        ):
            low = weights.astype(jnp.bfloat16)
            out = nn(value.T, low).T.astype(jnp.bfloat16)
            for g, s in enumerate(heads):
                out_ref[span * SPAN : (span + 1) * SPAN, s] = out[g * SPAN : (g + 1) * SPAN]
            value_grad = nn(low, grad).astype(jnp.bfloat16)
            centre = jnp.sum(weights * slope, axis=0, keepdims=True)
            score_grad = (weights * (slope - centre) * scale).astype(jnp.bfloat16)
            key_grad = nn(score_grad, query).astype(jnp.bfloat16)
            for b, (p, n) in enumerate(places):
                grad_refs[p][n, 0, :, lanes] = key_grad[b * rows : (b + 1) * rows]
                grad_refs[p][n, 1, :, lanes] = value_grad[b * rows : (b + 1) * rows]


def shards(cross_query, cross_grad, neighbour_kv, span_neighbours):
    dp_size = lax.axis_size("dp")
    context_size = lax.axis_size("context")
    tensor_size = lax.axis_size("tensor")
    local_rows, _, _, kv_width = neighbour_kv.shape
    width = kv_width // tensor_size
    row_count, query_width = cross_query.shape[1:]
    spans = row_count // SPAN
    count = spans * KNB
    peers = dp_size * tensor_size
    rows = NL // dp_size
    geometry = (local_rows, dp_size, context_size, tensor_size)
    group = ("tensor", "dp")
    params = pltpu.CompilerParams(vmem_limit_bytes=8 * 1024 * 1024)
    smem = pl.BlockSpec(memory_space=pltpu.SMEM)
    vmem = pl.BlockSpec(memory_space=pltpu.VMEM)

    def ring(array, by):
        return lax.ppermute(array, "dp", [(i, (i + by) % dp_size) for i in range(dp_size)])

    spread = neighbour_kv.transpose(2, 0, 1, 3)
    spread = spread.reshape(SLOTS, local_rows, dp_size, rows, tensor_size, width)
    spread = spread.transpose(4, 2, 0, 1, 3, 5).reshape(peers, SLOTS, local_rows, rows, width)
    ids = lax.dynamic_slice_in_dim(
        span_neighbours, lax.axis_index("context") * spans, spans, 1
    ).reshape(-1)
    ids = jnp.concatenate([ids, lax.axis_index("dp").astype(jnp.int32)[None]])
    query, grad = cross_query[0], cross_grad[0]
    spread, query, grad = lax.optimization_barrier((spread, query, grad))
    held = lax.all_to_all(spread, group, 0, 0, tiled=True)

    back = [(i + 1, i) for i in range(context_size - 1)]
    forth = [(i, i + 1) for i in range(context_size - 1)]
    halo = [lax.ppermute(values[:SPAN], "context", back) for values in (query, grad)]

    chunks = CHUNKS
    length = count // chunks
    chunk_rows = row_count // chunks
    part = jax.ShapeDtypeStruct((length, SLOTS, rows, width), jnp.bfloat16)
    delivered = pl.pallas_call(
        functools.partial(deliver_kernel, owners=dp_size, geometry=geometry),
        out_shape=(part,) * (dp_size * chunks),
        in_specs=[smem, vmem],
        out_specs=(vmem,) * (dp_size * chunks),
        compiler_params=params,
        name="deliver",
    )(ids, held)
    order = sorted(range(1, dp_size), key=lambda s: -min(s, dp_size - s))
    kv = []
    for c in range(chunks):
        mine = delivered[c * dp_size : (c + 1) * dp_size]
        arrived = {0: mine[0]}
        for s in order:
            arrived[s] = ring(mine[s], s)
        kv.append([arrived[s] for s in range(dp_size)])
    out_parts = []
    returned = []
    for c in range(chunks):
        ends = c == chunks - 1
        operands = [query, grad] + (halo if ends else []) + kv[c]
        out_rows, *kv_grads = pl.pallas_call(
            functools.partial(
                attention_kernel, parts=dp_size, halo=ends, first=c * spans // chunks
            ),
            out_shape=(jax.ShapeDtypeStruct((chunk_rows, query_width), jnp.bfloat16),)
            + (part,) * dp_size,
            in_specs=[vmem] * len(operands),
            out_specs=(vmem,) * (1 + dp_size),
            compiler_params=pltpu.CompilerParams(vmem_limit_bytes=16 * 1024 * 1024),
            name="attention",
        )(*operands)
        out_parts.append(out_rows)
        arrived = {0: kv_grads[0]}
        for s in order:
            arrived[s] = ring(kv_grads[s], -s)
        returned += [arrived[s] for s in range(dp_size)]

    windows = jnp.concatenate(out_parts, 0)
    before = lax.ppermute(windows[row_count - SPAN :], "context", forth)
    position = lax.broadcasted_iota(jnp.int32, windows.shape, 0)
    cross_out = jnp.where(
        position % SPAN == SPAN - 1,
        windows,
        jnp.concatenate([before, windows[: row_count - SPAN]], 0),
    )
    collected = pl.pallas_call(
        functools.partial(collect_kernel, owners=dp_size, geometry=geometry),
        out_shape=jax.ShapeDtypeStruct(held.shape, jnp.bfloat16),
        in_specs=[smem] + [vmem] * (dp_size * chunks),
        out_specs=vmem,
        compiler_params=params,
        name="collect",
    )(ids, *returned)
    final = lax.all_to_all(collected, group, 0, 0, tiled=True)
    final = final.reshape(tensor_size, dp_size, SLOTS, local_rows, rows, width)
    final = final.transpose(3, 1, 4, 2, 0, 5)
    return (cross_out[None], final.reshape(neighbour_kv.shape))


def solution(mesh):
    return jax.shard_map(
        shards,
        mesh=mesh,
        in_specs=(
            P("dp", "context", "tensor"),
            P("dp", "context", "tensor"),
            P(("dp", "context", "tensor"), None, None, None),
            P(),
        ),
        out_specs=(P("dp", "context", "tensor"), P(("dp", "context", "tensor"), None, None, None)),
        check_vma=False,
    )
```

time: 87.1 us -> 81.8 us (0.939)
  Pallas kernels: 11 us -> 8.44 us
  waiting for transfers between devices: 34.3 us -> 31.8 us
    pallas_call x2, Pallas kernels: 8 us -> 5.44 us  [shards(): pl.pallas_call(functools.partial(attention_kernel, parts=dp_size, halo=en...]
    all_to_all x1, waiting for transfers between devices: 5.31 us -> 3.87 us  [shards(): final = lax.all_to_all(collected, group, 0, 0, tiled=True)]
    all_to_all x1, waiting for transfers between devices: 12.3 us -> 10.9 us  [shards(): held = lax.all_to_all(spread, group, 0, 0, tiled=True)]
  transfers between devices with their start and end apart: 17 -> 17, of which waited for: 9 -> 9; matrix products, arithmetic and copies ran while one was open for 2% -> 4% of each run, Pallas kernels for 10% -> 8%
where the time goes in v4:
time: 81.8 us; the launch traced here: 81.4 us
  starting transfers between devices  32.1 us (39%)
  waiting for transfers between devices  31.8 us (39%)
  Pallas kernels  8.44 us (10%)
  local copies, waits for them, and re-layouts  6.76 us (8%)
  other arithmetic  1.46 us (2%)
    ppermute x12, starting transfers between devices, ring(): lax.ppermute(array, 'dp', [(i, (i + by) % dp_size) for i in range(dp_size)])  14.4 us
    ppermute x12, waiting for transfers between devices, ring(): lax.ppermute(array, 'dp', [(i, (i + by) % dp_size) for i in range(dp_size)])  11.4 us
    all_to_all x1, waiting for transfers between devices, shards(): held = lax.all_to_all(spread, group, 0, 0, tiled=True)  10.9 us
    all_to_all x1, starting transfers between devices, shards(): held = lax.all_to_all(spread, group, 0, 0, tiled=True)  7.17 us
    ppermute x1, waiting for transfers between devices, shards(): before = lax.ppermute(windows[row_count - SPAN:], 'context', forth)  5.68 us
    pallas_call x2, Pallas kernels, shards(): pl.pallas_call(functools.partial(attention_kernel, parts=dp_size, halo=en...  5.44 us
    ppermute x2, starting transfers between devices, shards(): lax.ppermute(values[:SPAN], 'context', back)  4.92 us
    all_to_all x1, waiting for transfers between devices, shards(): final = lax.all_to_all(collected, group, 0, 0, tiled=True)  3.87 us
  transfers between devices with their start and end apart: 17, of which 9 were waited for; matrix products, arithmetic and copies ran while one was open for 4% of the time, Pallas kernels for 8%

profile of v4, /device:TPU:224, one launch (start us, length us, event | category | flops | bytes accessed | tf_op | source)
XLA Modules:
  0.0 81.4 jit_solution(10032573919813721331)
XLA Ops:
  0.6 0.0 copy-start
  0.6 1.7 %reshape.132 = bf16[2,2,4,32,4,256]{5,4,0,3,2,1:T(4,128)(2,1)S(1)} reshape(bf16[2,2,128,1024]{3,0,2,1:T(2,128)(2,1)} %bitcast.27) | data formatting | bytes 2097152 | tf_op jit(solution)/shard_map/reshape | solution.py:140
  2.4 1.2 %copy.9 = bf16[2,2,4,32,4,256]{5,3,1,0,2,4:T(8,128)(2,1)} copy(bf16[2,2,4,32,4,256]{5,4,0,3,2,1:T(4,128)(2,1)S(1)} %reshape.132) | data formatting | bytes 2097152 | tf_op jit(solution)/shard_map/reshape | solution.py:140
  3.6 0.0 copy-start.2
  3.6 0.0 copy-start.1
  3.6 7.2 %all-to-all-start = ((bf16[16,2,2,32,256]{4,3,2,1,0:T(8,128)(2,1)}), bf16[16,2,2,32,256]{4,3,2,1,0:T(8,128)(2,1)S(1)}, u32[]{:S(2)}, u32[]{:S(2)}) async-start(bf16[16,2,2,32,256]{4,3,2,1,0:T(8,128)(2,1)} %bitcast.25), calls=%async_computation | async-start | bytes 2097152 | tf_op jit(solution)/shard_map/all_to_all | solution.py:148
  10.8 0.0 copy-done.2
  10.8 0.7 slice.13
  11.5 2.1 %collective-permute-start.4 = (bf16[64,2048]{1,0:T(8,128)(2,1)}, bf16[64,2048]{1,0:T(8,128)(2,1)S(1)}, u32[]{:S(2)}, u32[]{:S(2)}) collective-permute-start(bf16[64,2048]{1,0:T(8,128)(2,1)} %slice.13), channel_id=1, source_target_pairs={{4,0},{8,4},{12,8},{16,12},{20,16},{24,20},{28,24},{32,28},{36,32}... | collective-permute-start | bytes 786440 | tf_op jit(solution)/shard_map/ppermute | solution.py:152
  13.6 0.0 copy-done.1
  13.6 0.7 slice.12
  14.3 2.9 %collective-permute-start.3 = (bf16[64,2048]{1,0:T(8,128)(2,1)}, bf16[64,2048]{1,0:T(8,128)(2,1)}, u32[]{:S(2)}, u32[]{:S(2)}) collective-permute-start(bf16[64,2048]{1,0:T(8,128)(2,1)} %slice.12), channel_id=1, source_target_pairs={{4,0},{8,4},{12,8},{16,12},{20,16},{24,20},{28,24},{32,28},{36,32}... | collective-permute-start | bytes 786440 | tf_op jit(solution)/shard_map/ppermute | solution.py:152
  17.2 0.0 copy-done
  17.2 0.1 constant_dynamic-slice_fusion
  17.3 0.1 copy.10
  17.4 0.1 reshape.134
  17.5 0.1 pad_add_fusion.ids_ref
  17.6 10.9 %all-to-all-done.held_ref = bf16[16,2,2,32,256]{4,3,2,1,0:T(8,128)(2,1)S(1)} async-done(((bf16[16,2,2,32,256]{4,3,2,1,0:T(8,128)(2,1)}), bf16[16,2,2,32,256]{4,3,2,1,0:T(8,128)(2,1)S(1)}, u32[]{:S(2)}, u32[]{:S(2)}) %all-to-all-start) | async-done | bytes 1048608 | tf_op jit(solution)/shard_map/all_to_all | solution.py:148
  28.5 1.0 %deliver.1 = (bf16[4,2,32,256]{3,2,1,0:T(8,128)(2,1)S(1)}, bf16[4,2,32,256]{3,2,1,0:T(8,128)(2,1)S(1)}, bf16[4,2,32,256]{3,2,1,0:T(8,128)(2,1)S(1)}, bf16[4,2,32...) custom-call(s32[33]{0:T(128)S(1)} %pad_add_fusion.ids_ref, ...), custom_call_target="tpu_custom_call" | custom-call | tf_op jit(solution)/shard_map/deliver/pallas_call | solution.py:158
  29.5 0.6 collective-permute-start.5
  30.1 1.1 %collective-permute-start.6 = (bf16[4,2,32,256]{3,2,1,0:T(8,128)(2,1)S(1)}, bf16[4,2,32,256]{3,2,1,0:T(8,128)(2,1)S(1)}, u32[]{:S(2)}, u32[]{:S(2)}) collective-permute-start(bf16[4,2,32,256]{3,2,1,0:T(8,128)(2,1)S(1)} %get-tuple-element.33), channel_id=1, source_target_pairs={{0,128},{64,192},{128,0},{192,64},{1,129},{65,193},{129,1},{193,65... | collective-permute-start | bytes 393224 | tf_op jit(solution)/shard_map/ppermute | solution.py:137
  31.2 1.8 %collective-permute-start.7 = (bf16[4,2,32,256]{3,2,1,0:T(8,128)(2,1)S(1)}, bf16[4,2,32,256]{3,2,1,0:T(8,128)(2,1)S(1)}, u32[]{:S(2)}, u32[]{:S(2)}) collective-permute-start(bf16[4,2,32,256]{3,2,1,0:T(8,128)(2,1)S(1)} %get-tuple-element.34), channel_id=1, source_target_pairs={{0,192},{64,0},{128,64},{192,128},{1,193},{65,1},{129,65},{193,129... | collective-permute-start | bytes 393224 | tf_op jit(solution)/shard_map/ppermute | solution.py:137
  32.9 0.0 collective-permute-done.4.refs_1_
  33.0 0.7 collective-permute-start
  33.7 0.0 collective-permute-done.3.refs_0_
  33.7 2.2 %collective-permute-start.1 = (bf16[4,2,32,256]{3,2,1,0:T(8,128)(2,1)S(1)}, bf16[4,2,32,256]{3,2,1,0:T(8,128)(2,1)S(1)}, u32[]{:S(2)}, u32[]{:S(2)}) collective-permute-start(bf16[4,2,32,256]{3,2,1,0:T(8,128)(2,1)S(1)} %get-tuple-element.28), channel_id=1, source_target_pairs={{0,128},{64,192},{128,0},{192,64},{1,129},{65,193},{129,1},{193,65... | collective-permute-start | bytes 393224 | tf_op jit(solution)/shard_map/ppermute | solution.py:137
  35.8 4.0 %collective-permute-done.5.refs_3_ = bf16[4,2,32,256]{3,2,1,0:T(8,128)(2,1)S(1)} collective-permute-done((bf16[4,2,32,256]{3,2,1,0:T(8,128)(2,1)S(1)}, bf16[4,2,32,256]{3,2,1,0:T(8,128)(2,1)S(1)}, u32[]{:S(2)}, u32[]{:S(2)}) %collective-permute-start.5) | collective-permute-done | bytes 131104 | tf_op jit(solution)/shard_map/ppermute | solution.py:137
  39.8 0.0 collective-permute-start.2
  39.8 0.0 collective-permute-done.6.refs_4_
  39.9 0.9 %collective-permute-done.7.refs_5_ = bf16[4,2,32,256]{3,2,1,0:T(8,128)(2,1)S(1)} collective-permute-done((bf16[4,2,32,256]{3,2,1,0:T(8,128)(2,1)S(1)}, bf16[4,2,32,256]{3,2,1,0:T(8,128)(2,1)S(1)}, u32[]{:S(2)}, u32[]{:S(2)}) %collective-permute-start.7) | collective-permute-done | bytes 131104 | tf_op jit(solution)/shard_map/ppermute | solution.py:137
  40.8 3.2 %attention.3 = (bf16[128,2048]{1,0:T(8,128)(2,1)S(1)}, bf16[4,2,32,256]{3,2,1,0:T(8,128)(2,1)S(1)}, bf16[4,2,32,256]{3,2,1,0:T(8,128)(2,1)S(1)}, bf16[4,2,32,256...) custom-call(bf16[256,2048]{1,0:T(8,128)(2,1)S(1)} %bitcast.18, bf16[256,2048]{1,0:T(8,128)(2,1)S(1)} %bitcast.21, ...), custom_call_target="tpu_custom_call" | custom-call | tf_op jit(solution)/shard_map/attention/pallas_call | solution.py:179
  44.0 2.4 %collective-permute-start.12 = (bf16[4,2,32,256]{3,2,1,0:T(8,128)(2,1)S(1)}, bf16[4,2,32,256]{3,2,1,0:T(8,128)(2,1)S(1)}, u32[]{:S(2)}, u32[]{:S(2)}) collective-permute-start(bf16[4,2,32,256]{3,2,1,0:T(8,128)(2,1)S(1)} %get-tuple-element.41), channel_id=1, source_target_pairs={{0,192},{64,0},{128,64},{192,128},{1,193},{65,1},{129,65},{193,129... | collective-permute-start | bytes 393224 | tf_op jit(solution)/shard_map/ppermute | solution.py:137
  46.3 0.9 %collective-permute-start.13 = (bf16[4,2,32,256]{3,2,1,0:T(8,128)(2,1)S(1)}, bf16[4,2,32,256]{3,2,1,0:T(8,128)(2,1)S(1)}, u32[]{:S(2)}, u32[]{:S(2)}) collective-permute-start(bf16[4,2,32,256]{3,2,1,0:T(8,128)(2,1)S(1)} %get-tuple-element.42), channel_id=1, source_target_pairs={{0,128},{64,192},{128,0},{192,64},{1,129},{65,193},{129,1},{193,65... | collective-permute-start | bytes 393224 | tf_op jit(solution)/shard_map/ppermute | solution.py:137
  47.2 0.0 collective-permute-done.refs_1_
  47.2 0.1 collective-permute-start.14
  47.3 0.0 collective-permute-done.1.refs_2_
  47.3 0.0 collective-permute-done.2.refs_3_
  47.3 2.2 %attention.2 = (bf16[128,2048]{1,0:T(8,128)(2,1)S(1)}, bf16[4,2,32,256]{3,2,1,0:T(8,128)(2,1)S(1)}, bf16[4,2,32,256]{3,2,1,0:T(8,128)(2,1)S(1)}, bf16[4,2,32,256...) custom-call(bf16[256,2048]{1,0:T(8,128)(2,1)S(1)} %bitcast.19, bf16[256,2048]{1,0:T(8,128)(2,1)S(1)} %bitcast.22, ...), custom_call_target="tpu_custom_call" | custom-call | tf_op jit(solution)/shard_map/attention/pallas_call | solution.py:179
  49.6 3.2 %collective-permute-start.9 = (bf16[4,2,32,256]{3,2,1,0:T(8,128)(2,1)S(1)}, bf16[4,2,32,256]{3,2,1,0:T(8,128)(2,1)S(1)}, u32[]{:S(2)}, u32[]{:S(2)}) collective-permute-start(bf16[4,2,32,256]{3,2,1,0:T(8,128)(2,1)S(1)} %get-tuple-element.37), channel_id=1, source_target_pairs={{0,192},{64,0},{128,64},{192,128},{1,193},{65,1},{129,65},{193,129... | collective-permute-start | bytes 393224 | tf_op jit(solution)/shard_map/ppermute | solution.py:137
  52.8 1.4 %collective-permute-start.10 = (bf16[4,2,32,256]{3,2,1,0:T(8,128)(2,1)S(1)}, bf16[4,2,32,256]{3,2,1,0:T(8,128)(2,1)S(1)}, u32[]{:S(2)}, u32[]{:S(2)}) collective-permute-start(bf16[4,2,32,256]{3,2,1,0:T(8,128)(2,1)S(1)} %get-tuple-element.38), channel_id=1, source_target_pairs={{0,128},{64,192},{128,0},{192,64},{1,129},{65,193},{129,1},{193,65... | collective-permute-start | bytes 393224 | tf_op jit(solution)/shard_map/ppermute | solution.py:137
  54.2 0.0 collective-permute-done.12.refs_5_
  54.3 0.0 collective-permute-start.11
  54.3 0.0 collective-permute-done.13.refs_6_
  54.3 0.7 collective-permute-done.14.refs_7_
  54.9 1.8 %collective-permute-done.9.refs_1_ = bf16[4,2,32,256]{3,2,1,0:T(8,128)(2,1)S(1)} collective-permute-done((bf16[4,2,32,256]{3,2,1,0:T(8,128)(2,1)S(1)}, bf16[4,2,32,256]{3,2,1,0:T(8,128)(2,1)S(1)}, u32[]{:S(2)}, u32[]{:S(2)}) %collective-permute-start.9) | collective-permute-done | bytes 131104 | tf_op jit(solution)/shard_map/ppermute | solution.py:137
  56.7 2.6 %collective-permute-done.10.refs_2_ = bf16[4,2,32,256]{3,2,1,0:T(8,128)(2,1)S(1)} collective-permute-done((bf16[4,2,32,256]{3,2,1,0:T(8,128)(2,1)S(1)}, bf16[4,2,32,256]{3,2,1,0:T(8,128)(2,1)S(1)}, u32[]{:S(2)}, u32[]{:S(2)}) %collective-permute-start.10) | collective-permute-done | bytes 131104 | tf_op jit(solution)/shard_map/ppermute | solution.py:137
  59.3 1.4 %collective-permute-done.11.refs_3_ = bf16[4,2,32,256]{3,2,1,0:T(8,128)(2,1)S(1)} collective-permute-done((bf16[4,2,32,256]{3,2,1,0:T(8,128)(2,1)S(1)}, bf16[4,2,32,256]{3,2,1,0:T(8,128)(2,1)S(1)}, u32[]{:S(2)}, u32[]{:S(2)}) %collective-permute-start.11) | collective-permute-done | bytes 131104 | tf_op jit(solution)/shard_map/ppermute | solution.py:137
  60.7 2.0 %collect.1 = bf16[16,2,2,32,256]{4,3,2,1,0:T(8,128)(2,1)} custom-call(s32[33]{0:T(128)S(1)} %pad_add_fusion.ids_ref, bf16[4,2,32,256]{3,2,1,0:T(8,128)(2,1)S(1)} %get-tuple-element.36.refs_0_, bf16[4,2,32,256]{3,2,1,0:T(8,128)(2,1)S(1)} %collective-permute-done.9.refs_1_, bf16[4,2,32,256]{3,2,1,0:T(8,128)(2,1)S(1)} %collective-permute-done.10.refs_2_, ...), custom_call_target="tpu_custom_call" | custom-call | tf_op jit(solution)/shard_map/collect/pallas_call | solution.py:204
  62.7 3.7 %all-to-all-start.1 = ((bf16[16,2,2,32,256]{4,3,2,1,0:T(8,128)(2,1)}), bf16[16,2,2,32,256]{4,3,2,1,0:T(8,128)(2,1)S(1)}, u32[]{:S(2)}, u32[]{:S(2)}) async-start(bf16[16,2,2,32,256]{4,3,2,1,0:T(8,128)(2,1)} %collect.1), calls=%async_computation.1 | async-start | bytes 2097152 | tf_op jit(solution)/shard_map/all_to_all | solution.py:212
  66.5 1.9 %collective-permute-start.8 = (bf16[64,2048]{1,0:T(8,128)(2,1)S(1)}, bf16[64,2048]{1,0:T(8,128)(2,1)S(1)}, u32[]{:S(2)}, u32[]{:S(2)}) collective-permute-start(bf16[64,2048]{1,0:T(8,128)(2,1)S(1)} %slice.14), channel_id=1, source_target_pairs={{0,4},{4,8},{8,12},{12,16},{16,20},{20,24},{24,28},{28,32},{32,36}... | collective-permute-start | bytes 786440 | tf_op jit(solution)/shard_map/ppermute | solution.py:197
  68.4 0.1 fusion.1
  68.5 5.7 %collective-permute-done.8 = bf16[64,2048]{1,0:T(8,128)(2,1)S(1)} collective-permute-done((bf16[64,2048]{1,0:T(8,128)(2,1)S(1)}, bf16[64,2048]{1,0:T(8,128)(2,1)S(1)}, u32[]{:S(2)}, u32[]{:S(2)}) %collective-permute-start.8) | collective-permute-done | bytes 262176 | tf_op jit(solution)/shard_map/ppermute | solution.py:197
  74.2 1.3 %fusion = bf16[1,256,2048]{2,1,0:T(8,128)(2,1)} fusion(bf16[1,128,2048]{2,1,0:T(8,128)(2,1)S(1)} %bitcast.23, bf16[1,128,2048]{2,1,0:T(8,128)(2,1)S(1)} %bitcast.24, bf16[1,192,2048]{2,1,0:T(8,128)(2,1)S(1)} %fusion.1, bf16[1,64,2048]{2,1,0:T(8,128)(2,1)S(1)} %bitcast.28, s32[256]{0:T(256)S(1)} %get-tuple-element.44, s32[256]{0:T(256)S(1)} %get-tuple-element.45, ...), kind=kLoop, calls=%fused_computation.1 | loop fusion | flops 5767168 | bytes 3148032 | tf_op jit(solution)/shard_map/jit(_where)/select_n | solution.py:199
  75.5 3.9 %all-to-all-done.1 = bf16[16,2,2,32,256]{4,3,2,1,0:T(8,128)(2,1)S(1)} async-done(((bf16[16,2,2,32,256]{4,3,2,1,0:T(8,128)(2,1)}), bf16[16,2,2,32,256]{4,3,2,1,0:T(8,128)(2,1)S(1)}, u32[]{:S(2)}, u32[]{:S(2)}) %all-to-all-start.1) | async-done | bytes 1048608 | tf_op jit(solution)/shard_map/all_to_all | solution.py:212
  79.3 0.8 %copy.11 = bf16[2,4,32,2,4,256]{5,4,3,2,1,0:T(4,128)(2,1)S(1)} copy(bf16[2,4,32,2,4,256]{5,2,0,3,1,4:T(8,128)(2,1)S(1)} %bitcast.26) | data formatting | bytes 2097152 | tf_op jit(solution)/shard_map/transpose | solution.py:214
  80.1 1.2 %reshape.136 = bf16[2,128,2,1024]{3,2,1,0:T(2,128)(2,1)} reshape(bf16[2,4,32,2,4,256]{5,4,3,2,1,0:T(4,128)(2,1)S(1)} %copy.11) | data formatting | bytes 2097152 | tf_op jit(solution)/shard_map/reshape | solution.py:215
  (3 shorter events, 0.0 us)
Async XLA Ops:
  0.6 16.6 %copy-start = (s32[4,64,2]{1,2,0:T(2,128)S(1)}, s32[4,64,2]{1,2,0:T(2,128)}, u32[]{:S(2)}) copy-start(s32[4,64,2]{1,2,0:T(2,128)} %param.7) | copy-start | bytes 6148
  3.6 7.2 %copy-start.2 = (bf16[1,256,2048]{2,1,0:T(8,128)(2,1)S(1)}, bf16[1,256,2048]{2,1,0:T(8,128)(2,1)}, u32[]{:S(2)}) copy-start(bf16[1,256,2048]{2,1,0:T(8,128)(2,1)} %param.5) | copy-start | bytes 3145732
  3.6 10.0 %copy-start.1 = (bf16[1,256,2048]{2,1,0:T(8,128)(2,1)S(1)}, bf16[1,256,2048]{2,1,0:T(8,128)(2,1)}, u32[]{:S(2)}) copy-start(bf16[1,256,2048]{2,1,0:T(8,128)(2,1)} %param.4) | copy-start | bytes 3145732
  3.6 24.9 %all-to-all-start = ((bf16[16,2,2,32,256]{4,3,2,1,0:T(8,128)(2,1)}), bf16[16,2,2,32,256]{4,3,2,1,0:T(8,128)(2,1)S(1)}, u32[]{:S(2)}, u32[]{:S(2)}) async-start(bf16[16,2,2,32,256]{4,3,2,1,0:T(8,128)(2,1)} %bitcast.25), calls=%async_computation | async-start | bytes 2097152 | tf_op jit(solution)/shard_map/all_to_all | solution.py:148
  11.5 21.4 %collective-permute-start.4 = (bf16[64,2048]{1,0:T(8,128)(2,1)}, bf16[64,2048]{1,0:T(8,128)(2,1)S(1)}, u32[]{:S(2)}, u32[]{:S(2)}) collective-permute-start(bf16[64,2048]{1,0:T(8,128)(2,1)} %slice.13), channel_id=1, source_target_pairs={{4,0},{8,4},{12,8},{16,12},{20,16},{24,20},{28,24},{32,28},{36,32}... | collective-permute-start | bytes 786440 | tf_op jit(solution)/shard_map/ppermute | solution.py:152
  14.3 19.3 %collective-permute-start.3 = (bf16[64,2048]{1,0:T(8,128)(2,1)}, bf16[64,2048]{1,0:T(8,128)(2,1)}, u32[]{:S(2)}, u32[]{:S(2)}) collective-permute-start(bf16[64,2048]{1,0:T(8,128)(2,1)} %slice.12), channel_id=1, source_target_pairs={{4,0},{8,4},{12,8},{16,12},{20,16},{24,20},{28,24},{32,28},{36,32}... | collective-permute-start | bytes 786440 | tf_op jit(solution)/shard_map/ppermute | solution.py:152
  29.5 10.4 %collective-permute-start.5 = (bf16[4,2,32,256]{3,2,1,0:T(8,128)(2,1)S(1)}, bf16[4,2,32,256]{3,2,1,0:T(8,128)(2,1)S(1)}, u32[]{:S(2)}, u32[]{:S(2)}) collective-permute-start(bf16[4,2,32,256]{3,2,1,0:T(8,128)(2,1)S(1)} %get-tuple-element.32), channel_id=1, source_target_pairs={{0,64},{64,128},{128,192},{192,0},{1,65},{65,129},{129,193},{193,1... | collective-permute-start | bytes 393224 | tf_op jit(solution)/shard_map/ppermute | solution.py:137
  30.1 9.7 %collective-permute-start.6 = (bf16[4,2,32,256]{3,2,1,0:T(8,128)(2,1)S(1)}, bf16[4,2,32,256]{3,2,1,0:T(8,128)(2,1)S(1)}, u32[]{:S(2)}, u32[]{:S(2)}) collective-permute-start(bf16[4,2,32,256]{3,2,1,0:T(8,128)(2,1)S(1)} %get-tuple-element.33), channel_id=1, source_target_pairs={{0,128},{64,192},{128,0},{192,64},{1,129},{65,193},{129,1},{193,65... | collective-permute-start | bytes 393224 | tf_op jit(solution)/shard_map/ppermute | solution.py:137
  31.2 9.6 %collective-permute-start.7 = (bf16[4,2,32,256]{3,2,1,0:T(8,128)(2,1)S(1)}, bf16[4,2,32,256]{3,2,1,0:T(8,128)(2,1)S(1)}, u32[]{:S(2)}, u32[]{:S(2)}) collective-permute-start(bf16[4,2,32,256]{3,2,1,0:T(8,128)(2,1)S(1)} %get-tuple-element.34), channel_id=1, source_target_pairs={{0,192},{64,0},{128,64},{192,128},{1,193},{65,1},{129,65},{193,129... | collective-permute-start | bytes 393224 | tf_op jit(solution)/shard_map/ppermute | solution.py:137
  33.0 14.3 %collective-permute-start = (bf16[4,2,32,256]{3,2,1,0:T(8,128)(2,1)S(1)}, bf16[4,2,32,256]{3,2,1,0:T(8,128)(2,1)S(1)}, u32[]{:S(2)}, u32[]{:S(2)}) collective-permute-start(bf16[4,2,32,256]{3,2,1,0:T(8,128)(2,1)S(1)} %get-tuple-element.27), channel_id=1, source_target_pairs={{0,64},{64,128},{128,192},{192,0},{1,65},{65,129},{129,193},{193,1... | collective-permute-start | bytes 393224 | tf_op jit(solution)/shard_map/ppermute | solution.py:137
  33.7 13.7 %collective-permute-start.1 = (bf16[4,2,32,256]{3,2,1,0:T(8,128)(2,1)S(1)}, bf16[4,2,32,256]{3,2,1,0:T(8,128)(2,1)S(1)}, u32[]{:S(2)}, u32[]{:S(2)}) collective-permute-start(bf16[4,2,32,256]{3,2,1,0:T(8,128)(2,1)S(1)} %get-tuple-element.28), channel_id=1, source_target_pairs={{0,128},{64,192},{128,0},{192,64},{1,129},{65,193},{129,1},{193,65... | collective-permute-start | bytes 393224 | tf_op jit(solution)/shard_map/ppermute | solution.py:137
  39.8 7.5 %collective-permute-start.2 = (bf16[4,2,32,256]{3,2,1,0:T(8,128)(2,1)S(1)}, bf16[4,2,32,256]{3,2,1,0:T(8,128)(2,1)S(1)}, u32[]{:S(2)}, u32[]{:S(2)}) collective-permute-start(bf16[4,2,32,256]{3,2,1,0:T(8,128)(2,1)S(1)} %get-tuple-element.29), channel_id=1, source_target_pairs={{0,192},{64,0},{128,64},{192,128},{1,193},{65,1},{129,65},{193,129... | collective-permute-start | bytes 393224 | tf_op jit(solution)/shard_map/ppermute | solution.py:137
  44.0 10.3 %collective-permute-start.12 = (bf16[4,2,32,256]{3,2,1,0:T(8,128)(2,1)S(1)}, bf16[4,2,32,256]{3,2,1,0:T(8,128)(2,1)S(1)}, u32[]{:S(2)}, u32[]{:S(2)}) collective-permute-start(bf16[4,2,32,256]{3,2,1,0:T(8,128)(2,1)S(1)} %get-tuple-element.41), channel_id=1, source_target_pairs={{0,192},{64,0},{128,64},{192,128},{1,193},{65,1},{129,65},{193,129... | collective-permute-start | bytes 393224 | tf_op jit(solution)/shard_map/ppermute | solution.py:137
  46.3 7.9 %collective-permute-start.13 = (bf16[4,2,32,256]{3,2,1,0:T(8,128)(2,1)S(1)}, bf16[4,2,32,256]{3,2,1,0:T(8,128)(2,1)S(1)}, u32[]{:S(2)}, u32[]{:S(2)}) collective-permute-start(bf16[4,2,32,256]{3,2,1,0:T(8,128)(2,1)S(1)} %get-tuple-element.42), channel_id=1, source_target_pairs={{0,128},{64,192},{128,0},{192,64},{1,129},{65,193},{129,1},{193,65... | collective-permute-start | bytes 393224 | tf_op jit(solution)/shard_map/ppermute | solution.py:137
  47.2 7.7 %collective-permute-start.14 = (bf16[4,2,32,256]{3,2,1,0:T(8,128)(2,1)S(1)}, bf16[4,2,32,256]{3,2,1,0:T(8,128)(2,1)S(1)}, u32[]{:S(2)}, u32[]{:S(2)}) collective-permute-start(bf16[4,2,32,256]{3,2,1,0:T(8,128)(2,1)S(1)} %get-tuple-element.43), channel_id=1, source_target_pairs={{0,64},{64,128},{128,192},{192,0},{1,65},{65,129},{129,193},{193,1... | collective-permute-start | bytes 393224 | tf_op jit(solution)/shard_map/ppermute | solution.py:137
  49.6 7.2 %collective-permute-start.9 = (bf16[4,2,32,256]{3,2,1,0:T(8,128)(2,1)S(1)}, bf16[4,2,32,256]{3,2,1,0:T(8,128)(2,1)S(1)}, u32[]{:S(2)}, u32[]{:S(2)}) collective-permute-start(bf16[4,2,32,256]{3,2,1,0:T(8,128)(2,1)S(1)} %get-tuple-element.37), channel_id=1, source_target_pairs={{0,192},{64,0},{128,64},{192,128},{1,193},{65,1},{129,65},{193,129... | collective-permute-start | bytes 393224 | tf_op jit(solution)/shard_map/ppermute | solution.py:137
  52.8 6.5 %collective-permute-start.10 = (bf16[4,2,32,256]{3,2,1,0:T(8,128)(2,1)S(1)}, bf16[4,2,32,256]{3,2,1,0:T(8,128)(2,1)S(1)}, u32[]{:S(2)}, u32[]{:S(2)}) collective-permute-start(bf16[4,2,32,256]{3,2,1,0:T(8,128)(2,1)S(1)} %get-tuple-element.38), channel_id=1, source_target_pairs={{0,128},{64,192},{128,0},{192,64},{1,129},{65,193},{129,1},{193,65... | collective-permute-start | bytes 393224 | tf_op jit(solution)/shard_map/ppermute | solution.py:137
  54.3 6.4 %collective-permute-start.11 = (bf16[4,2,32,256]{3,2,1,0:T(8,128)(2,1)S(1)}, bf16[4,2,32,256]{3,2,1,0:T(8,128)(2,1)S(1)}, u32[]{:S(2)}, u32[]{:S(2)}) collective-permute-start(bf16[4,2,32,256]{3,2,1,0:T(8,128)(2,1)S(1)} %get-tuple-element.39), channel_id=1, source_target_pairs={{0,64},{64,128},{128,192},{192,0},{1,65},{65,129},{129,193},{193,1... | collective-permute-start | bytes 393224 | tf_op jit(solution)/shard_map/ppermute | solution.py:137
  62.7 16.6 %all-to-all-start.1 = ((bf16[16,2,2,32,256]{4,3,2,1,0:T(8,128)(2,1)}), bf16[16,2,2,32,256]{4,3,2,1,0:T(8,128)(2,1)S(1)}, u32[]{:S(2)}, u32[]{:S(2)}) async-start(bf16[16,2,2,32,256]{4,3,2,1,0:T(8,128)(2,1)} %collect.1), calls=%async_computation.1 | async-start | bytes 2097152 | tf_op jit(solution)/shard_map/all_to_all | solution.py:212
  66.5 7.7 %collective-permute-start.8 = (bf16[64,2048]{1,0:T(8,128)(2,1)S(1)}, bf16[64,2048]{1,0:T(8,128)(2,1)S(1)}, u32[]{:S(2)}, u32[]{:S(2)}) collective-permute-start(bf16[64,2048]{1,0:T(8,128)(2,1)S(1)} %slice.14), channel_id=1, source_target_pairs={{0,4},{4,8},{8,12},{12,16},{16,20},{20,24},{24,28},{28,32},{32,36}... | collective-permute-start | bytes 786440 | tf_op jit(solution)/shard_map/ppermute | solution.py:197

commit v5 on v4

--- a/solution.py
+++ b/solution.py
@@ -13,7 +13,7 @@
 NL = 128
 KNB = 2
 SLOTS = 2
-CHUNKS = 2
+CHUNKS = (2, 2)
 TAIL = 16
 LOG2E = 1.4426950408889634
 
@@ -33,36 +33,45 @@
     return source, row % local_rows
 
 
+def listed_places(ids_ref, blocks, owners, geometry):
+    lengths = [block.shape[0] for block in blocks[::owners]]
+    me = ids_ref[owners * sum(lengths)]
+    for o, block in enumerate(blocks):
+        start = (me + o % owners) % owners * sum(lengths) + sum(lengths[: o // owners])
+        for k in range(block.shape[0]):
+            yield block, k, place_of(ids_ref[start + k], geometry)
+
+
 def deliver_kernel(ids_ref, held_ref, *out_refs, owners, geometry):
-    length = out_refs[0].shape[0]
-    count = len(out_refs) // owners * length
-    me = ids_ref[owners * count]
-    for o, out_ref in enumerate(out_refs):
-        owner = (me + o % owners) % owners
-        for k in range(length):
-            row = ids_ref[owner * count + o // owners * length + k]
-            source, part = place_of(row, geometry)
-            for slot in range(SLOTS):
-                out_ref[k, slot] = held_ref[source, slot, part]
+    for block, k, (source, part) in listed_places(ids_ref, out_refs, owners, geometry):
+        for slot in range(SLOTS):
+            block[k, slot] = held_ref[source, slot, part]
 
 
 def collect_kernel(ids_ref, *refs, owners, geometry):
-    held_refs, out_ref = refs[:-1], refs[-1]
-    length = held_refs[0].shape[0]
-    count = len(held_refs) // owners * length
-    me = ids_ref[owners * count]
-    for o, held_ref in enumerate(held_refs):
-        owner = (me + o % owners) % owners
-        for k in range(length):
-            row = ids_ref[owner * count + o // owners * length + k]
-            source, part = place_of(row, geometry)
-            for slot in range(SLOTS):
-                out_ref[source, slot, part] = held_ref[k, slot]
+    *held_refs, out_ref, sem = refs
+    copies = [
+        pltpu.make_async_copy(block.at[k], out_ref.at[source, :, part], sem.at[i])
+        for i, (block, k, (source, part)) in enumerate(
+            listed_places(ids_ref, held_refs, owners, geometry)
+        )
+    ]
+    for copy in copies:
+        copy.start()
+    for copy in copies:
+        copy.wait()
 
 
 def attention_kernel(q_ref, g_ref, *refs, parts, halo, first):
     if halo:
-        halo_q_ref, halo_g_ref, *refs = refs
+        *sources, refs = refs[0], refs[1], refs[2:]
+        *refs, halo_q_ref, halo_g_ref, sem = refs
+        copies = [
+            pltpu.make_async_copy(source, target, sem.at[i])
+            for i, (source, target) in enumerate(zip(sources, (halo_q_ref, halo_g_ref)))
+        ]
+        for copy in copies:
+            copy.start()
     kv_refs, out_ref, grad_refs = refs[:parts], refs[parts], refs[parts + 1 :]
     rows = kv_refs[0].shape[2]
     kv_heads = kv_refs[0].shape[3] // HD
@@ -92,6 +101,9 @@
         return places, lanes, heads, key, value, query, grad
 
     for span in range(spans):
+        if halo and span == spans - 1:
+            for copy in copies:
+                copy.wait()
         loaded = [load(span, h) for h in range(kv_heads)]
         all_scores = [nt(key, query) for _, _, _, key, _, query, _ in loaded]
         slopes = [nt(value, grad) for _, _, _, _, value, _, grad in loaded]
@@ -151,21 +163,23 @@
     forth = [(i, i + 1) for i in range(context_size - 1)]
     halo = [lax.ppermute(values[:SPAN], "context", back) for values in (query, grad)]
 
-    chunks = CHUNKS
-    length = count // chunks
-    chunk_rows = row_count // chunks
-    part = jax.ShapeDtypeStruct((length, SLOTS, rows, width), jnp.bfloat16)
+    chunks = CHUNKS if sum(CHUNKS) == spans else (spans,)
+    parts = [
+        jax.ShapeDtypeStruct((n * KNB, SLOTS, rows, width), jnp.bfloat16)
+        for n in chunks
+        for _ in range(dp_size)
+    ]
     delivered = pl.pallas_call(
         functools.partial(deliver_kernel, owners=dp_size, geometry=geometry),
-        out_shape=(part,) * (dp_size * chunks),
+        out_shape=parts,
         in_specs=[smem, vmem],
-        out_specs=(vmem,) * (dp_size * chunks),
+        out_specs=[vmem] * len(parts),
         compiler_params=params,
         name="deliver",
     )(ids, held)
     order = sorted(range(1, dp_size), key=lambda s: -min(s, dp_size - s))
     kv = []
-    for c in range(chunks):
+    for c in range(len(chunks)):
         mine = delivered[c * dp_size : (c + 1) * dp_size]
         arrived = {0: mine[0]}
         for s in order:
@@ -173,20 +187,24 @@
         kv.append([arrived[s] for s in range(dp_size)])
     out_parts = []
     returned = []
-    for c in range(chunks):
-        ends = c == chunks - 1
-        operands = [query, grad] + (halo if ends else []) + kv[c]
+    for c, n in enumerate(chunks):
+        ends = c == len(chunks) - 1
+        halo_rows = halo if ends else []
+        anywhere = pl.BlockSpec(memory_space=pl.ANY)
+        scratch = [pltpu.VMEM((SPAN, query_width), jnp.bfloat16)] * 2
+        scratch.append(pltpu.SemaphoreType.DMA((2,)))
         out_rows, *kv_grads = pl.pallas_call(
             functools.partial(
-                attention_kernel, parts=dp_size, halo=ends, first=c * spans // chunks
+                attention_kernel, parts=dp_size, halo=ends, first=sum(chunks[:c])
             ),
-            out_shape=(jax.ShapeDtypeStruct((chunk_rows, query_width), jnp.bfloat16),)
-            + (part,) * dp_size,
-            in_specs=[vmem] * len(operands),
-            out_specs=(vmem,) * (1 + dp_size),
+            out_shape=[jax.ShapeDtypeStruct((n * SPAN, query_width), jnp.bfloat16)]
+            + parts[c * dp_size : (c + 1) * dp_size],
+            in_specs=[vmem] * 2 + [anywhere] * len(halo_rows) + [vmem] * dp_size,
+            out_specs=[vmem] * (1 + dp_size),
+            scratch_shapes=scratch if ends else [],
             compiler_params=pltpu.CompilerParams(vmem_limit_bytes=16 * 1024 * 1024),
             name="attention",
-        )(*operands)
+        )(query, grad, *halo_rows, *kv[c])
         out_parts.append(out_rows)
         arrived = {0: kv_grads[0]}
         for s in order:
@@ -204,8 +222,9 @@
     collected = pl.pallas_call(
         functools.partial(collect_kernel, owners=dp_size, geometry=geometry),
         out_shape=jax.ShapeDtypeStruct(held.shape, jnp.bfloat16),
-        in_specs=[smem] + [vmem] * (dp_size * chunks),
-        out_specs=vmem,
+        in_specs=[smem] + [vmem] * len(returned),
+        out_specs=pl.BlockSpec(memory_space=pl.ANY),
+        scratch_shapes=[pltpu.SemaphoreType.DMA((dp_size * count,))],
         compiler_params=params,
         name="collect",
     )(ids, *returned)

time: 81.8 us -> 80.9 us (0.989)
  Pallas kernels: 8.44 us -> 7.56 us
  transfers between devices with their start and end apart: 17 -> 17, of which waited for: 9 -> 9; matrix products, arithmetic and copies ran while one was open for 4% -> 4% of each run, Pallas kernels for 8% -> 7%
where the time goes in v5:
time: 80.9 us; the launch traced here: 80.5 us
  starting transfers between devices  32.1 us (40%)
  waiting for transfers between devices  31.9 us (39%)
  Pallas kernels  7.56 us (9%)
  local copies, waits for them, and re-layouts  6.76 us (8%)
  other arithmetic  1.46 us (2%)
    ppermute x12, starting transfers between devices, ring(): lax.ppermute(array, 'dp', [(i, (i + by) % dp_size) for i in range(dp_size)])  14.3 us
    ppermute x12, waiting for transfers between devices, ring(): lax.ppermute(array, 'dp', [(i, (i + by) % dp_size) for i in range(dp_size)])  11.4 us
    all_to_all x1, waiting for transfers between devices, shards(): held = lax.all_to_all(spread, group, 0, 0, tiled=True)  10.9 us
    all_to_all x1, starting transfers between devices, shards(): held = lax.all_to_all(spread, group, 0, 0, tiled=True)  7.17 us
    ppermute x1, waiting for transfers between devices, shards(): before = lax.ppermute(windows[row_count - SPAN:], 'context', forth)  5.68 us
    ppermute x2, starting transfers between devices, shards(): lax.ppermute(values[:SPAN], 'context', back)  4.92 us
    pallas_call x2, Pallas kernels, shards(): pl.pallas_call(functools.partial(attention_kernel, parts=dp_size, halo=en...  4.66 us
    all_to_all x1, waiting for transfers between devices, shards(): final = lax.all_to_all(collected, group, 0, 0, tiled=True)  3.87 us
  transfers between devices with their start and end apart: 17, of which 9 were waited for; matrix products, arithmetic and copies ran while one was open for 4% of the time, Pallas kernels for 7%

profile of v5, /device:TPU:224, one launch (start us, length us, event | category | flops | bytes accessed | tf_op | source)
XLA Modules:
  0.0 80.5 jit_solution(14283546067103553651)
XLA Ops:
  0.6 0.0 copy-start
  0.6 1.7 %reshape.132 = bf16[2,2,4,32,4,256]{5,4,0,3,2,1:T(4,128)(2,1)S(1)} reshape(bf16[2,2,128,1024]{3,0,2,1:T(2,128)(2,1)} %bitcast.27) | data formatting | bytes 2097152 | tf_op jit(solution)/shard_map/reshape | solution.py:152
  2.4 1.2 %copy.9 = bf16[2,2,4,32,4,256]{5,3,1,0,2,4:T(8,128)(2,1)} copy(bf16[2,2,4,32,4,256]{5,4,0,3,2,1:T(4,128)(2,1)S(1)} %reshape.132) | data formatting | bytes 2097152 | tf_op jit(solution)/shard_map/reshape | solution.py:152
  3.6 0.0 copy-start.2
  3.6 0.0 copy-start.1
  3.6 7.2 %all-to-all-start = ((bf16[16,2,2,32,256]{4,3,2,1,0:T(8,128)(2,1)}), bf16[16,2,2,32,256]{4,3,2,1,0:T(8,128)(2,1)S(1)}, u32[]{:S(2)}, u32[]{:S(2)}) async-start(bf16[16,2,2,32,256]{4,3,2,1,0:T(8,128)(2,1)} %bitcast.25), calls=%async_computation | async-start | bytes 2097152 | tf_op jit(solution)/shard_map/all_to_all | solution.py:160
  10.8 0.0 copy-done.2
  10.8 0.7 slice.13
  11.5 2.1 %collective-permute-start.4 = (bf16[64,2048]{1,0:T(8,128)(2,1)}, bf16[64,2048]{1,0:T(8,128)(2,1)S(1)}, u32[]{:S(2)}, u32[]{:S(2)}) collective-permute-start(bf16[64,2048]{1,0:T(8,128)(2,1)} %slice.13), channel_id=1, source_target_pairs={{4,0},{8,4},{12,8},{16,12},{20,16},{24,20},{28,24},{32,28},{36,32}... | collective-permute-start | bytes 786440 | tf_op jit(solution)/shard_map/ppermute | solution.py:164
  13.6 0.0 copy-done.1
  13.6 0.7 slice.12
  14.3 2.9 %collective-permute-start.3 = (bf16[64,2048]{1,0:T(8,128)(2,1)}, bf16[64,2048]{1,0:T(8,128)(2,1)}, u32[]{:S(2)}, u32[]{:S(2)}) collective-permute-start(bf16[64,2048]{1,0:T(8,128)(2,1)} %slice.12), channel_id=1, source_target_pairs={{4,0},{8,4},{12,8},{16,12},{20,16},{24,20},{28,24},{32,28},{36,32}... | collective-permute-start | bytes 786440 | tf_op jit(solution)/shard_map/ppermute | solution.py:164
  17.2 0.0 copy-done
  17.2 0.1 constant_dynamic-slice_fusion
  17.3 0.1 copy.10
  17.4 0.1 reshape.134
  17.5 0.1 pad_add_fusion.ids_ref
  17.6 10.9 %all-to-all-done.held_ref = bf16[16,2,2,32,256]{4,3,2,1,0:T(8,128)(2,1)S(1)} async-done(((bf16[16,2,2,32,256]{4,3,2,1,0:T(8,128)(2,1)}), bf16[16,2,2,32,256]{4,3,2,1,0:T(8,128)(2,1)S(1)}, u32[]{:S(2)}, u32[]{:S(2)}) %all-to-all-start) | async-done | bytes 1048608 | tf_op jit(solution)/shard_map/all_to_all | solution.py:160
  28.5 1.0 %deliver.1 = (bf16[4,2,32,256]{3,2,1,0:T(8,128)(2,1)S(1)}, bf16[4,2,32,256]{3,2,1,0:T(8,128)(2,1)S(1)}, bf16[4,2,32,256]{3,2,1,0:T(8,128)(2,1)S(1)}, bf16[4,2,32...) custom-call(s32[33]{0:T(128)S(1)} %pad_add_fusion.ids_ref, ...), custom_call_target="tpu_custom_call" | custom-call | tf_op jit(solution)/shard_map/deliver/pallas_call | solution.py:172
  29.5 0.6 collective-permute-start.5
  30.1 1.1 %collective-permute-start.6 = (bf16[4,2,32,256]{3,2,1,0:T(8,128)(2,1)S(1)}, bf16[4,2,32,256]{3,2,1,0:T(8,128)(2,1)S(1)}, u32[]{:S(2)}, u32[]{:S(2)}) collective-permute-start(bf16[4,2,32,256]{3,2,1,0:T(8,128)(2,1)S(1)} %get-tuple-element.33), channel_id=1, source_target_pairs={{0,128},{64,192},{128,0},{192,64},{1,129},{65,193},{129,1},{193,65... | collective-permute-start | bytes 393224 | tf_op jit(solution)/shard_map/ppermute | solution.py:149
  31.2 1.8 %collective-permute-start.7 = (bf16[4,2,32,256]{3,2,1,0:T(8,128)(2,1)S(1)}, bf16[4,2,32,256]{3,2,1,0:T(8,128)(2,1)S(1)}, u32[]{:S(2)}, u32[]{:S(2)}) collective-permute-start(bf16[4,2,32,256]{3,2,1,0:T(8,128)(2,1)S(1)} %get-tuple-element.34), channel_id=1, source_target_pairs={{0,192},{64,0},{128,64},{192,128},{1,193},{65,1},{129,65},{193,129... | collective-permute-start | bytes 393224 | tf_op jit(solution)/shard_map/ppermute | solution.py:149
  32.9 0.0 collective-permute-done.4.refs_1_
  33.0 0.7 collective-permute-start
  33.7 0.0 collective-permute-done.3.refs_0_
  33.7 2.2 %collective-permute-start.1 = (bf16[4,2,32,256]{3,2,1,0:T(8,128)(2,1)S(1)}, bf16[4,2,32,256]{3,2,1,0:T(8,128)(2,1)S(1)}, u32[]{:S(2)}, u32[]{:S(2)}) collective-permute-start(bf16[4,2,32,256]{3,2,1,0:T(8,128)(2,1)S(1)} %get-tuple-element.28), channel_id=1, source_target_pairs={{0,128},{64,192},{128,0},{192,64},{1,129},{65,193},{129,1},{193,65... | collective-permute-start | bytes 393224 | tf_op jit(solution)/shard_map/ppermute | solution.py:149
  35.8 4.0 %collective-permute-done.5.refs_3_ = bf16[4,2,32,256]{3,2,1,0:T(8,128)(2,1)S(1)} collective-permute-done((bf16[4,2,32,256]{3,2,1,0:T(8,128)(2,1)S(1)}, bf16[4,2,32,256]{3,2,1,0:T(8,128)(2,1)S(1)}, u32[]{:S(2)}, u32[]{:S(2)}) %collective-permute-start.5) | collective-permute-done | bytes 131104 | tf_op jit(solution)/shard_map/ppermute | solution.py:149
  39.8 0.0 collective-permute-start.2
  39.8 0.0 collective-permute-done.6.refs_4_
  39.9 0.9 %collective-permute-done.7.refs_5_ = bf16[4,2,32,256]{3,2,1,0:T(8,128)(2,1)S(1)} collective-permute-done((bf16[4,2,32,256]{3,2,1,0:T(8,128)(2,1)S(1)}, bf16[4,2,32,256]{3,2,1,0:T(8,128)(2,1)S(1)}, u32[]{:S(2)}, u32[]{:S(2)}) %collective-permute-start.7) | collective-permute-done | bytes 131104 | tf_op jit(solution)/shard_map/ppermute | solution.py:149
  40.8 2.4 %attention.3 = (bf16[128,2048]{1,0:T(8,128)(2,1)S(1)}, bf16[4,2,32,256]{3,2,1,0:T(8,128)(2,1)S(1)}, bf16[4,2,32,256]{3,2,1,0:T(8,128)(2,1)S(1)}, bf16[4,2,32,256...) custom-call(bf16[256,2048]{1,0:T(8,128)(2,1)S(1)} %bitcast.18, bf16[256,2048]{1,0:T(8,128)(2,1)S(1)} %bitcast.21, ...), custom_call_target="tpu_custom_call" | custom-call | tf_op jit(solution)/shard_map/attention/pallas_call | solution.py:196
  43.2 2.4 %collective-permute-start.12 = (bf16[4,2,32,256]{3,2,1,0:T(8,128)(2,1)S(1)}, bf16[4,2,32,256]{3,2,1,0:T(8,128)(2,1)S(1)}, u32[]{:S(2)}, u32[]{:S(2)}) collective-permute-start(bf16[4,2,32,256]{3,2,1,0:T(8,128)(2,1)S(1)} %get-tuple-element.41), channel_id=1, source_target_pairs={{0,192},{64,0},{128,64},{192,128},{1,193},{65,1},{129,65},{193,129... | collective-permute-start | bytes 393224 | tf_op jit(solution)/shard_map/ppermute | solution.py:149
  45.5 0.9 %collective-permute-start.13 = (bf16[4,2,32,256]{3,2,1,0:T(8,128)(2,1)S(1)}, bf16[4,2,32,256]{3,2,1,0:T(8,128)(2,1)S(1)}, u32[]{:S(2)}, u32[]{:S(2)}) collective-permute-start(bf16[4,2,32,256]{3,2,1,0:T(8,128)(2,1)S(1)} %get-tuple-element.42), channel_id=1, source_target_pairs={{0,128},{64,192},{128,0},{192,64},{1,129},{65,193},{129,1},{193,65... | collective-permute-start | bytes 393224 | tf_op jit(solution)/shard_map/ppermute | solution.py:149
  46.4 0.0 collective-permute-done.refs_1_
  46.5 0.1 collective-permute-start.14
  46.5 0.0 collective-permute-done.1.refs_2_
  46.5 0.0 collective-permute-done.2.refs_3_
  46.5 2.2 %attention.2 = (bf16[128,2048]{1,0:T(8,128)(2,1)S(1)}, bf16[4,2,32,256]{3,2,1,0:T(8,128)(2,1)S(1)}, bf16[4,2,32,256]{3,2,1,0:T(8,128)(2,1)S(1)}, bf16[4,2,32,256...) custom-call(bf16[256,2048]{1,0:T(8,128)(2,1)S(1)} %bitcast.19, bf16[256,2048]{1,0:T(8,128)(2,1)S(1)} %bitcast.22, ...), custom_call_target="tpu_custom_call" | custom-call | tf_op jit(solution)/shard_map/attention/pallas_call | solution.py:196
  48.8 3.3 %collective-permute-start.9 = (bf16[4,2,32,256]{3,2,1,0:T(8,128)(2,1)S(1)}, bf16[4,2,32,256]{3,2,1,0:T(8,128)(2,1)S(1)}, u32[]{:S(2)}, u32[]{:S(2)}) collective-permute-start(bf16[4,2,32,256]{3,2,1,0:T(8,128)(2,1)S(1)} %get-tuple-element.37), channel_id=1, source_target_pairs={{0,192},{64,0},{128,64},{192,128},{1,193},{65,1},{129,65},{193,129... | collective-permute-start | bytes 393224 | tf_op jit(solution)/shard_map/ppermute | solution.py:149
  52.0 1.4 %collective-permute-start.10 = (bf16[4,2,32,256]{3,2,1,0:T(8,128)(2,1)S(1)}, bf16[4,2,32,256]{3,2,1,0:T(8,128)(2,1)S(1)}, u32[]{:S(2)}, u32[]{:S(2)}) collective-permute-start(bf16[4,2,32,256]{3,2,1,0:T(8,128)(2,1)S(1)} %get-tuple-element.38), channel_id=1, source_target_pairs={{0,128},{64,192},{128,0},{192,64},{1,129},{65,193},{129,1},{193,65... | collective-permute-start | bytes 393224 | tf_op jit(solution)/shard_map/ppermute | solution.py:149
  53.4 0.0 collective-permute-done.12.refs_5_
  53.5 0.0 collective-permute-start.11
  53.5 0.0 collective-permute-done.13.refs_6_
  53.5 1.5 %collective-permute-done.14.refs_7_ = bf16[4,2,32,256]{3,2,1,0:T(8,128)(2,1)S(1)} collective-permute-done((bf16[4,2,32,256]{3,2,1,0:T(8,128)(2,1)S(1)}, bf16[4,2,32,256]{3,2,1,0:T(8,128)(2,1)S(1)}, u32[]{:S(2)}, u32[]{:S(2)}) %collective-permute-start.14) | collective-permute-done | bytes 131104 | tf_op jit(solution)/shard_map/ppermute | solution.py:149
  54.9 1.0 %collective-permute-done.9.refs_1_ = bf16[4,2,32,256]{3,2,1,0:T(8,128)(2,1)S(1)} collective-permute-done((bf16[4,2,32,256]{3,2,1,0:T(8,128)(2,1)S(1)}, bf16[4,2,32,256]{3,2,1,0:T(8,128)(2,1)S(1)}, u32[]{:S(2)}, u32[]{:S(2)}) %collective-permute-start.9) | collective-permute-done | bytes 131104 | tf_op jit(solution)/shard_map/ppermute | solution.py:149
  56.0 2.6 %collective-permute-done.10.refs_2_ = bf16[4,2,32,256]{3,2,1,0:T(8,128)(2,1)S(1)} collective-permute-done((bf16[4,2,32,256]{3,2,1,0:T(8,128)(2,1)S(1)}, bf16[4,2,32,256]{3,2,1,0:T(8,128)(2,1)S(1)}, u32[]{:S(2)}, u32[]{:S(2)}) %collective-permute-start.10) | collective-permute-done | bytes 131104 | tf_op jit(solution)/shard_map/ppermute | solution.py:149
  58.5 1.4 %collective-permute-done.11.refs_3_ = bf16[4,2,32,256]{3,2,1,0:T(8,128)(2,1)S(1)} collective-permute-done((bf16[4,2,32,256]{3,2,1,0:T(8,128)(2,1)S(1)}, bf16[4,2,32,256]{3,2,1,0:T(8,128)(2,1)S(1)}, u32[]{:S(2)}, u32[]{:S(2)}) %collective-permute-start.11) | collective-permute-done | bytes 131104 | tf_op jit(solution)/shard_map/ppermute | solution.py:149
  59.9 1.9 %collect.1 = bf16[16,2,2,32,256]{4,3,2,1,0:T(8,128)(2,1)} custom-call(s32[33]{0:T(128)S(1)} %pad_add_fusion.ids_ref, bf16[4,2,32,256]{3,2,1,0:T(8,128)(2,1)S(1)} %get-tuple-element.36.refs_0_, bf16[4,2,32,256]{3,2,1,0:T(8,128)(2,1)S(1)} %collective-permute-done.9.refs_1_, bf16[4,2,32,256]{3,2,1,0:T(8,128)(2,1)S(1)} %collective-permute-done.10.refs_2_, ...), custom_call_target="tpu_custom_call" | custom-call | tf_op jit(solution)/shard_map/collect/pallas_call | solution.py:222
  61.8 3.7 %all-to-all-start.1 = ((bf16[16,2,2,32,256]{4,3,2,1,0:T(8,128)(2,1)}), bf16[16,2,2,32,256]{4,3,2,1,0:T(8,128)(2,1)S(1)}, u32[]{:S(2)}, u32[]{:S(2)}) async-start(bf16[16,2,2,32,256]{4,3,2,1,0:T(8,128)(2,1)} %collect.1), calls=%async_computation.1 | async-start | bytes 2097152 | tf_op jit(solution)/shard_map/all_to_all | solution.py:231
  65.6 1.9 %collective-permute-start.8 = (bf16[64,2048]{1,0:T(8,128)(2,1)S(1)}, bf16[64,2048]{1,0:T(8,128)(2,1)S(1)}, u32[]{:S(2)}, u32[]{:S(2)}) collective-permute-start(bf16[64,2048]{1,0:T(8,128)(2,1)S(1)} %slice.14), channel_id=1, source_target_pairs={{0,4},{4,8},{8,12},{12,16},{16,20},{20,24},{24,28},{28,32},{32,36}... | collective-permute-start | bytes 786440 | tf_op jit(solution)/shard_map/ppermute | solution.py:215
  67.5 0.1 fusion.1
  67.6 5.7 %collective-permute-done.8 = bf16[64,2048]{1,0:T(8,128)(2,1)S(1)} collective-permute-done((bf16[64,2048]{1,0:T(8,128)(2,1)S(1)}, bf16[64,2048]{1,0:T(8,128)(2,1)S(1)}, u32[]{:S(2)}, u32[]{:S(2)}) %collective-permute-start.8) | collective-permute-done | bytes 262176 | tf_op jit(solution)/shard_map/ppermute | solution.py:215
  73.3 1.3 %fusion = bf16[1,256,2048]{2,1,0:T(8,128)(2,1)} fusion(bf16[1,128,2048]{2,1,0:T(8,128)(2,1)S(1)} %bitcast.23, bf16[1,128,2048]{2,1,0:T(8,128)(2,1)S(1)} %bitcast.24, bf16[1,192,2048]{2,1,0:T(8,128)(2,1)S(1)} %fusion.1, bf16[1,64,2048]{2,1,0:T(8,128)(2,1)S(1)} %bitcast.28, s32[256]{0:T(256)S(1)} %get-tuple-element.44, s32[256]{0:T(256)S(1)} %get-tuple-element.45, ...), kind=kLoop, calls=%fused_computation.1 | loop fusion | flops 5767168 | bytes 3148032 | tf_op jit(solution)/shard_map/jit(_where)/select_n | solution.py:217
  74.6 3.9 %all-to-all-done.1 = bf16[16,2,2,32,256]{4,3,2,1,0:T(8,128)(2,1)S(1)} async-done(((bf16[16,2,2,32,256]{4,3,2,1,0:T(8,128)(2,1)}), bf16[16,2,2,32,256]{4,3,2,1,0:T(8,128)(2,1)S(1)}, u32[]{:S(2)}, u32[]{:S(2)}) %all-to-all-start.1) | async-done | bytes 1048608 | tf_op jit(solution)/shard_map/all_to_all | solution.py:231
  78.5 0.8 %copy.11 = bf16[2,4,32,2,4,256]{5,4,3,2,1,0:T(4,128)(2,1)S(1)} copy(bf16[2,4,32,2,4,256]{5,2,0,3,1,4:T(8,128)(2,1)S(1)} %bitcast.26) | data formatting | bytes 2097152 | tf_op jit(solution)/shard_map/transpose | solution.py:233
  79.3 1.2 %reshape.136 = bf16[2,128,2,1024]{3,2,1,0:T(2,128)(2,1)} reshape(bf16[2,4,32,2,4,256]{5,4,3,2,1,0:T(4,128)(2,1)S(1)} %copy.11) | data formatting | bytes 2097152 | tf_op jit(solution)/shard_map/reshape | solution.py:234
  (3 shorter events, 0.0 us)
Async XLA Ops:
  0.6 16.6 %copy-start = (s32[4,64,2]{1,2,0:T(2,128)S(1)}, s32[4,64,2]{1,2,0:T(2,128)}, u32[]{:S(2)}) copy-start(s32[4,64,2]{1,2,0:T(2,128)} %param.7) | copy-start | bytes 6148
  3.6 7.2 %copy-start.2 = (bf16[1,256,2048]{2,1,0:T(8,128)(2,1)S(1)}, bf16[1,256,2048]{2,1,0:T(8,128)(2,1)}, u32[]{:S(2)}) copy-start(bf16[1,256,2048]{2,1,0:T(8,128)(2,1)} %param.5) | copy-start | bytes 3145732
  3.6 10.0 %copy-start.1 = (bf16[1,256,2048]{2,1,0:T(8,128)(2,1)S(1)}, bf16[1,256,2048]{2,1,0:T(8,128)(2,1)}, u32[]{:S(2)}) copy-start(bf16[1,256,2048]{2,1,0:T(8,128)(2,1)} %param.4) | copy-start | bytes 3145732
  3.6 24.9 %all-to-all-start = ((bf16[16,2,2,32,256]{4,3,2,1,0:T(8,128)(2,1)}), bf16[16,2,2,32,256]{4,3,2,1,0:T(8,128)(2,1)S(1)}, u32[]{:S(2)}, u32[]{:S(2)}) async-start(bf16[16,2,2,32,256]{4,3,2,1,0:T(8,128)(2,1)} %bitcast.25), calls=%async_computation | async-start | bytes 2097152 | tf_op jit(solution)/shard_map/all_to_all | solution.py:160
  11.5 21.4 %collective-permute-start.4 = (bf16[64,2048]{1,0:T(8,128)(2,1)}, bf16[64,2048]{1,0:T(8,128)(2,1)S(1)}, u32[]{:S(2)}, u32[]{:S(2)}) collective-permute-start(bf16[64,2048]{1,0:T(8,128)(2,1)} %slice.13), channel_id=1, source_target_pairs={{4,0},{8,4},{12,8},{16,12},{20,16},{24,20},{28,24},{32,28},{36,32}... | collective-permute-start | bytes 786440 | tf_op jit(solution)/shard_map/ppermute | solution.py:164
  14.3 19.3 %collective-permute-start.3 = (bf16[64,2048]{1,0:T(8,128)(2,1)}, bf16[64,2048]{1,0:T(8,128)(2,1)}, u32[]{:S(2)}, u32[]{:S(2)}) collective-permute-start(bf16[64,2048]{1,0:T(8,128)(2,1)} %slice.12), channel_id=1, source_target_pairs={{4,0},{8,4},{12,8},{16,12},{20,16},{24,20},{28,24},{32,28},{36,32}... | collective-permute-start | bytes 786440 | tf_op jit(solution)/shard_map/ppermute | solution.py:164
  29.5 10.4 %collective-permute-start.5 = (bf16[4,2,32,256]{3,2,1,0:T(8,128)(2,1)S(1)}, bf16[4,2,32,256]{3,2,1,0:T(8,128)(2,1)S(1)}, u32[]{:S(2)}, u32[]{:S(2)}) collective-permute-start(bf16[4,2,32,256]{3,2,1,0:T(8,128)(2,1)S(1)} %get-tuple-element.32), channel_id=1, source_target_pairs={{0,64},{64,128},{128,192},{192,0},{1,65},{65,129},{129,193},{193,1... | collective-permute-start | bytes 393224 | tf_op jit(solution)/shard_map/ppermute | solution.py:149
  30.1 9.7 %collective-permute-start.6 = (bf16[4,2,32,256]{3,2,1,0:T(8,128)(2,1)S(1)}, bf16[4,2,32,256]{3,2,1,0:T(8,128)(2,1)S(1)}, u32[]{:S(2)}, u32[]{:S(2)}) collective-permute-start(bf16[4,2,32,256]{3,2,1,0:T(8,128)(2,1)S(1)} %get-tuple-element.33), channel_id=1, source_target_pairs={{0,128},{64,192},{128,0},{192,64},{1,129},{65,193},{129,1},{193,65... | collective-permute-start | bytes 393224 | tf_op jit(solution)/shard_map/ppermute | solution.py:149
  31.2 9.6 %collective-permute-start.7 = (bf16[4,2,32,256]{3,2,1,0:T(8,128)(2,1)S(1)}, bf16[4,2,32,256]{3,2,1,0:T(8,128)(2,1)S(1)}, u32[]{:S(2)}, u32[]{:S(2)}) collective-permute-start(bf16[4,2,32,256]{3,2,1,0:T(8,128)(2,1)S(1)} %get-tuple-element.34), channel_id=1, source_target_pairs={{0,192},{64,0},{128,64},{192,128},{1,193},{65,1},{129,65},{193,129... | collective-permute-start | bytes 393224 | tf_op jit(solution)/shard_map/ppermute | solution.py:149
  33.0 13.5 %collective-permute-start = (bf16[4,2,32,256]{3,2,1,0:T(8,128)(2,1)S(1)}, bf16[4,2,32,256]{3,2,1,0:T(8,128)(2,1)S(1)}, u32[]{:S(2)}, u32[]{:S(2)}) collective-permute-start(bf16[4,2,32,256]{3,2,1,0:T(8,128)(2,1)S(1)} %get-tuple-element.27), channel_id=1, source_target_pairs={{0,64},{64,128},{128,192},{192,0},{1,65},{65,129},{129,193},{193,1... | collective-permute-start | bytes 393224 | tf_op jit(solution)/shard_map/ppermute | solution.py:149
  33.7 12.9 %collective-permute-start.1 = (bf16[4,2,32,256]{3,2,1,0:T(8,128)(2,1)S(1)}, bf16[4,2,32,256]{3,2,1,0:T(8,128)(2,1)S(1)}, u32[]{:S(2)}, u32[]{:S(2)}) collective-permute-start(bf16[4,2,32,256]{3,2,1,0:T(8,128)(2,1)S(1)} %get-tuple-element.28), channel_id=1, source_target_pairs={{0,128},{64,192},{128,0},{192,64},{1,129},{65,193},{129,1},{193,65... | collective-permute-start | bytes 393224 | tf_op jit(solution)/shard_map/ppermute | solution.py:149
  39.8 6.7 %collective-permute-start.2 = (bf16[4,2,32,256]{3,2,1,0:T(8,128)(2,1)S(1)}, bf16[4,2,32,256]{3,2,1,0:T(8,128)(2,1)S(1)}, u32[]{:S(2)}, u32[]{:S(2)}) collective-permute-start(bf16[4,2,32,256]{3,2,1,0:T(8,128)(2,1)S(1)} %get-tuple-element.29), channel_id=1, source_target_pairs={{0,192},{64,0},{128,64},{192,128},{1,193},{65,1},{129,65},{193,129... | collective-permute-start | bytes 393224 | tf_op jit(solution)/shard_map/ppermute | solution.py:149
  43.2 10.3 %collective-permute-start.12 = (bf16[4,2,32,256]{3,2,1,0:T(8,128)(2,1)S(1)}, bf16[4,2,32,256]{3,2,1,0:T(8,128)(2,1)S(1)}, u32[]{:S(2)}, u32[]{:S(2)}) collective-permute-start(bf16[4,2,32,256]{3,2,1,0:T(8,128)(2,1)S(1)} %get-tuple-element.41), channel_id=1, source_target_pairs={{0,192},{64,0},{128,64},{192,128},{1,193},{65,1},{129,65},{193,129... | collective-permute-start | bytes 393224 | tf_op jit(solution)/shard_map/ppermute | solution.py:149
  45.5 7.9 %collective-permute-start.13 = (bf16[4,2,32,256]{3,2,1,0:T(8,128)(2,1)S(1)}, bf16[4,2,32,256]{3,2,1,0:T(8,128)(2,1)S(1)}, u32[]{:S(2)}, u32[]{:S(2)}) collective-permute-start(bf16[4,2,32,256]{3,2,1,0:T(8,128)(2,1)S(1)} %get-tuple-element.42), channel_id=1, source_target_pairs={{0,128},{64,192},{128,0},{192,64},{1,129},{65,193},{129,1},{193,65... | collective-permute-start | bytes 393224 | tf_op jit(solution)/shard_map/ppermute | solution.py:149
  46.5 8.5 %collective-permute-start.14 = (bf16[4,2,32,256]{3,2,1,0:T(8,128)(2,1)S(1)}, bf16[4,2,32,256]{3,2,1,0:T(8,128)(2,1)S(1)}, u32[]{:S(2)}, u32[]{:S(2)}) collective-permute-start(bf16[4,2,32,256]{3,2,1,0:T(8,128)(2,1)S(1)} %get-tuple-element.43), channel_id=1, source_target_pairs={{0,64},{64,128},{128,192},{192,0},{1,65},{65,129},{129,193},{193,1... | collective-permute-start | bytes 393224 | tf_op jit(solution)/shard_map/ppermute | solution.py:149
  48.8 7.2 %collective-permute-start.9 = (bf16[4,2,32,256]{3,2,1,0:T(8,128)(2,1)S(1)}, bf16[4,2,32,256]{3,2,1,0:T(8,128)(2,1)S(1)}, u32[]{:S(2)}, u32[]{:S(2)}) collective-permute-start(bf16[4,2,32,256]{3,2,1,0:T(8,128)(2,1)S(1)} %get-tuple-element.37), channel_id=1, source_target_pairs={{0,192},{64,0},{128,64},{192,128},{1,193},{65,1},{129,65},{193,129... | collective-permute-start | bytes 393224 | tf_op jit(solution)/shard_map/ppermute | solution.py:149
  52.0 6.5 %collective-permute-start.10 = (bf16[4,2,32,256]{3,2,1,0:T(8,128)(2,1)S(1)}, bf16[4,2,32,256]{3,2,1,0:T(8,128)(2,1)S(1)}, u32[]{:S(2)}, u32[]{:S(2)}) collective-permute-start(bf16[4,2,32,256]{3,2,1,0:T(8,128)(2,1)S(1)} %get-tuple-element.38), channel_id=1, source_target_pairs={{0,128},{64,192},{128,0},{192,64},{1,129},{65,193},{129,1},{193,65... | collective-permute-start | bytes 393224 | tf_op jit(solution)/shard_map/ppermute | solution.py:149
  53.5 6.5 %collective-permute-start.11 = (bf16[4,2,32,256]{3,2,1,0:T(8,128)(2,1)S(1)}, bf16[4,2,32,256]{3,2,1,0:T(8,128)(2,1)S(1)}, u32[]{:S(2)}, u32[]{:S(2)}) collective-permute-start(bf16[4,2,32,256]{3,2,1,0:T(8,128)(2,1)S(1)} %get-tuple-element.39), channel_id=1, source_target_pairs={{0,64},{64,128},{128,192},{192,0},{1,65},{65,129},{129,193},{193,1... | collective-permute-start | bytes 393224 | tf_op jit(solution)/shard_map/ppermute | solution.py:149
  61.8 16.6 %all-to-all-start.1 = ((bf16[16,2,2,32,256]{4,3,2,1,0:T(8,128)(2,1)}), bf16[16,2,2,32,256]{4,3,2,1,0:T(8,128)(2,1)S(1)}, u32[]{:S(2)}, u32[]{:S(2)}) async-start(bf16[16,2,2,32,256]{4,3,2,1,0:T(8,128)(2,1)} %collect.1), calls=%async_computation.1 | async-start | bytes 2097152 | tf_op jit(solution)/shard_map/all_to_all | solution.py:231
  65.6 7.7 %collective-permute-start.8 = (bf16[64,2048]{1,0:T(8,128)(2,1)S(1)}, bf16[64,2048]{1,0:T(8,128)(2,1)S(1)}, u32[]{:S(2)}, u32[]{:S(2)}) collective-permute-start(bf16[64,2048]{1,0:T(8,128)(2,1)S(1)} %slice.14), channel_id=1, source_target_pairs={{0,4},{4,8},{8,12},{12,16},{16,20},{20,24},{24,28},{28,32},{32,36}... | collective-permute-start | bytes 786440 | tf_op jit(solution)/shard_map/ppermute | solution.py:215

commit v6 on v5

--- a/solution.py
+++ b/solution.py
@@ -33,27 +33,29 @@
     return source, row % local_rows
 
 
-def listed_places(ids_ref, blocks, owners, geometry):
+def listed_places(ids_ref, blocks, owners, geometry, first, count):
     lengths = [block.shape[0] for block in blocks[::owners]]
-    me = ids_ref[owners * sum(lengths)]
+    me = ids_ref[owners * count]
     for o, block in enumerate(blocks):
-        start = (me + o % owners) % owners * sum(lengths) + sum(lengths[: o // owners])
+        start = (me + o % owners) % owners * count + first + sum(lengths[: o // owners])
         for k in range(block.shape[0]):
             yield block, k, place_of(ids_ref[start + k], geometry)
 
 
-def deliver_kernel(ids_ref, held_ref, *out_refs, owners, geometry):
-    for block, k, (source, part) in listed_places(ids_ref, out_refs, owners, geometry):
+def deliver_kernel(ids_ref, held_ref, *out_refs, owners, geometry, count):
+    for block, k, (source, part) in listed_places(
+        ids_ref, out_refs, owners, geometry, 0, count
+    ):
         for slot in range(SLOTS):
             block[k, slot] = held_ref[source, slot, part]
 
 
-def collect_kernel(ids_ref, *refs, owners, geometry):
-    *held_refs, out_ref, sem = refs
+def collect_kernel(ids_ref, *refs, owners, geometry, first, count):
+    held_refs, (out_ref, sem) = refs[:owners], refs[-2:]
     copies = [
         pltpu.make_async_copy(block.at[k], out_ref.at[source, :, part], sem.at[i])
         for i, (block, k, (source, part)) in enumerate(
-            listed_places(ids_ref, held_refs, owners, geometry)
+            listed_places(ids_ref, held_refs, owners, geometry, first, count)
         )
     ]
     for copy in copies:
@@ -100,28 +102,29 @@
         )
         return places, lanes, heads, key, value, query, grad
 
-    for span in range(spans):
-        if halo and span == spans - 1:
+    stages = [range(spans - 1), range(spans - 1, spans)] if halo else [range(spans)]
+    for stage in stages:
+        if halo and spans - 1 in stage:
             for copy in copies:
                 copy.wait()
-        loaded = [load(span, h) for h in range(kv_heads)]
-        all_scores = [nt(key, query) for _, _, _, key, _, query, _ in loaded]
-        slopes = [nt(value, grad) for _, _, _, _, value, _, grad in loaded]
-        all_weights = []
-        for scores in all_scores:
-            scores = scores * (scale * LOG2E)
-            raised = jnp.exp2(scores - jnp.max(scores, axis=0, keepdims=True))
-            all_weights.append(raised * (1.0 / jnp.sum(raised, axis=0, keepdims=True)))
-        for (places, lanes, heads, key, value, query, grad), weights, slope in zip(
-            loaded, all_weights, slopes
+        loaded = [(span,) + load(span, h) for span in stage for h in range(kv_heads)]
+        all_scores = [nt(key, query) for *_, key, _, query, _ in loaded]
+        slopes = [nt(value, grad) for *_, value, _, grad in loaded]
+        all_raised = [
+            jnp.exp2((scores - jnp.max(scores, axis=0, keepdims=True)) * (scale * LOG2E))
+            for scores in all_scores
+        ]
+        shares = [1.0 / jnp.sum(raised, axis=0, keepdims=True) for raised in all_raised]
+        for (span, places, lanes, heads, _, value, query, grad), raised, share, slope in zip(
+            loaded, all_raised, shares, slopes
         ):
-            low = weights.astype(jnp.bfloat16)
+            low = (raised * share).astype(jnp.bfloat16)
             out = nn(value.T, low).T.astype(jnp.bfloat16)
             for g, s in enumerate(heads):
                 out_ref[span * SPAN : (span + 1) * SPAN, s] = out[g * SPAN : (g + 1) * SPAN]
             value_grad = nn(low, grad).astype(jnp.bfloat16)
-            centre = jnp.sum(weights * slope, axis=0, keepdims=True)
-            score_grad = (weights * (slope - centre) * scale).astype(jnp.bfloat16)
+            centre = jnp.sum(raised * slope, axis=0, keepdims=True) * share
+            score_grad = (raised * (share * scale) * (slope - centre)).astype(jnp.bfloat16)
             key_grad = nn(score_grad, query).astype(jnp.bfloat16)
             for b, (p, n) in enumerate(places):
                 grad_refs[p][n, 0, :, lanes] = key_grad[b * rows : (b + 1) * rows]
@@ -170,7 +173,7 @@
         for _ in range(dp_size)
     ]
     delivered = pl.pallas_call(
-        functools.partial(deliver_kernel, owners=dp_size, geometry=geometry),
+        functools.partial(deliver_kernel, owners=dp_size, geometry=geometry, count=count),
         out_shape=parts,
         in_specs=[smem, vmem],
         out_specs=[vmem] * len(parts),
@@ -209,7 +212,7 @@
         arrived = {0: kv_grads[0]}
         for s in order:
             arrived[s] = ring(kv_grads[s], -s)
-        returned += [arrived[s] for s in range(dp_size)]
+        returned.append([arrived[s] for s in range(dp_size)])
 
     windows = jnp.concatenate(out_parts, 0)
     before = lax.ppermute(windows[row_count - SPAN :], "context", forth)
@@ -219,16 +222,27 @@
         windows,
         jnp.concatenate([before, windows[: row_count - SPAN]], 0),
     )
-    collected = pl.pallas_call(
-        functools.partial(collect_kernel, owners=dp_size, geometry=geometry),
-        out_shape=jax.ShapeDtypeStruct(held.shape, jnp.bfloat16),
-        in_specs=[smem] + [vmem] * len(returned),
-        out_specs=pl.BlockSpec(memory_space=pl.ANY),
-        scratch_shapes=[pltpu.SemaphoreType.DMA((dp_size * count,))],
-        compiler_params=params,
-        name="collect",
-    )(ids, *returned)
-    final = lax.all_to_all(collected, group, 0, 0, tiled=True)
+    collected = []
+    for c in reversed(range(len(chunks))):
+        collected = [
+            pl.pallas_call(
+                functools.partial(
+                    collect_kernel,
+                    owners=dp_size,
+                    geometry=geometry,
+                    first=sum(chunks[:c]) * KNB,
+                    count=count,
+                ),
+                out_shape=jax.ShapeDtypeStruct(held.shape, jnp.bfloat16),
+                in_specs=[smem] + [vmem] * dp_size + [anywhere] * len(collected),
+                out_specs=anywhere,
+                scratch_shapes=[pltpu.SemaphoreType.DMA((dp_size * chunks[c] * KNB,))],
+                input_output_aliases={1 + dp_size: 0} if collected else {},
+                compiler_params=params,
+                name="collect",
+            )(ids, *returned[c], *collected)
+        ]
+    final = lax.all_to_all(collected[0], group, 0, 0, tiled=True)
     final = final.reshape(tensor_size, dp_size, SLOTS, local_rows, rows, width)
     final = final.transpose(3, 1, 4, 2, 0, 5)
     return (cross_out[None], final.reshape(neighbour_kv.shape))

time: 80.9 us -> 80.4 us (level)
  waiting for transfers between devices: 31.9 us -> 30.3 us
  Pallas kernels: 7.56 us -> 8.51 us
    ppermute x12, waiting for transfers between devices: 11.4 us -> 9.82 us  [ring(): lax.ppermute(array, 'dp', [(i, (i + by) % dp_size) for i in range(dp_size)])]
    pallas_call x1 -> x2, Pallas kernels: 1.92 us -> 3.08 us  [shards(): pl.pallas_call(functools.partial(collect_kernel, owners=dp_size, geometry...]
  transfers between devices with their start and end apart: 17 -> 17, of which waited for: 9 -> 8; matrix products, arithmetic and copies ran while one was open for 4% -> 4% of each run, Pallas kernels for 7% -> 9%
where the time goes in v6:
time: 80.4 us; the launch traced here: 80.1 us
  starting transfers between devices  32.3 us (40%)
  waiting for transfers between devices  30.3 us (38%)
  Pallas kernels  8.51 us (11%)
  local copies, waits for them, and re-layouts  6.76 us (8%)
  other arithmetic  1.46 us (2%)
  between operations  0.82 us (1%)
    ppermute x12, starting transfers between devices, ring(): lax.ppermute(array, 'dp', [(i, (i + by) % dp_size) for i in range(dp_size)])  14.5 us
    all_to_all x1, waiting for transfers between devices, shards(): held = lax.all_to_all(spread, group, 0, 0, tiled=True)  10.9 us
    ppermute x12, waiting for transfers between devices, ring(): lax.ppermute(array, 'dp', [(i, (i + by) % dp_size) for i in range(dp_size)])  9.82 us
    all_to_all x1, starting transfers between devices, shards(): held = lax.all_to_all(spread, group, 0, 0, tiled=True)  7.17 us
    ppermute x1, waiting for transfers between devices, shards(): before = lax.ppermute(windows[row_count - SPAN:], 'context', forth)  5.68 us
    ppermute x2, starting transfers between devices, shards(): lax.ppermute(values[:SPAN], 'context', back)  4.92 us
    pallas_call x2, Pallas kernels, shards(): pl.pallas_call(functools.partial(attention_kernel, parts=dp_size, halo=en...  4.44 us
    all_to_all x1, waiting for transfers between devices, shards(): final = lax.all_to_all(collected[0], group, 0, 0, tiled=True)  3.87 us
  transfers between devices with their start and end apart: 17, of which 8 were waited for; matrix products, arithmetic and copies ran while one was open for 4% of the time, Pallas kernels for 9%

profile of v6, /device:TPU:224, one launch (start us, length us, event | category | flops | bytes accessed | tf_op | source)
XLA Modules:
  0.0 80.1 jit_solution(11142104251051198403)
XLA Ops:
  0.6 0.0 copy-start
  0.6 1.7 %reshape.132 = bf16[2,2,4,32,4,256]{5,4,0,3,2,1:T(4,128)(2,1)S(1)} reshape(bf16[2,2,128,1024]{3,0,2,1:T(2,128)(2,1)} %bitcast.27) | data formatting | bytes 2097152 | tf_op jit(solution)/shard_map/reshape | solution.py:155
  2.4 1.2 %copy.10 = bf16[2,2,4,32,4,256]{5,3,1,0,2,4:T(8,128)(2,1)} copy(bf16[2,2,4,32,4,256]{5,4,0,3,2,1:T(4,128)(2,1)S(1)} %reshape.132) | data formatting | bytes 2097152 | tf_op jit(solution)/shard_map/reshape | solution.py:155
  3.6 0.0 copy-start.2
  3.6 0.0 copy-start.1
  3.6 7.2 %all-to-all-start = ((bf16[16,2,2,32,256]{4,3,2,1,0:T(8,128)(2,1)}), bf16[16,2,2,32,256]{4,3,2,1,0:T(8,128)(2,1)S(1)}, u32[]{:S(2)}, u32[]{:S(2)}) async-start(bf16[16,2,2,32,256]{4,3,2,1,0:T(8,128)(2,1)} %bitcast.25), calls=%async_computation | async-start | bytes 2097152 | tf_op jit(solution)/shard_map/all_to_all | solution.py:163
  10.8 0.0 copy-done.2
  10.8 0.7 slice.13
  11.5 2.1 %collective-permute-start.4 = (bf16[64,2048]{1,0:T(8,128)(2,1)}, bf16[64,2048]{1,0:T(8,128)(2,1)S(1)}, u32[]{:S(2)}, u32[]{:S(2)}) collective-permute-start(bf16[64,2048]{1,0:T(8,128)(2,1)} %slice.13), channel_id=1, source_target_pairs={{4,0},{8,4},{12,8},{16,12},{20,16},{24,20},{28,24},{32,28},{36,32}... | collective-permute-start | bytes 786440 | tf_op jit(solution)/shard_map/ppermute | solution.py:167
  13.6 0.0 copy-done.1
  13.6 0.7 slice.12
  14.3 2.9 %collective-permute-start.3 = (bf16[64,2048]{1,0:T(8,128)(2,1)}, bf16[64,2048]{1,0:T(8,128)(2,1)}, u32[]{:S(2)}, u32[]{:S(2)}) collective-permute-start(bf16[64,2048]{1,0:T(8,128)(2,1)} %slice.12), channel_id=1, source_target_pairs={{4,0},{8,4},{12,8},{16,12},{20,16},{24,20},{28,24},{32,28},{36,32}... | collective-permute-start | bytes 786440 | tf_op jit(solution)/shard_map/ppermute | solution.py:167
  17.2 0.0 copy-done
  17.2 0.1 constant_dynamic-slice_fusion
  17.3 0.1 copy.11
  17.4 0.1 reshape.134
  17.5 0.1 pad_add_fusion.ids_ref
  17.6 10.9 %all-to-all-done.held_ref = bf16[16,2,2,32,256]{4,3,2,1,0:T(8,128)(2,1)S(1)} async-done(((bf16[16,2,2,32,256]{4,3,2,1,0:T(8,128)(2,1)}), bf16[16,2,2,32,256]{4,3,2,1,0:T(8,128)(2,1)S(1)}, u32[]{:S(2)}, u32[]{:S(2)}) %all-to-all-start) | async-done | bytes 1048608 | tf_op jit(solution)/shard_map/all_to_all | solution.py:163
  28.5 1.0 %deliver.1 = (bf16[4,2,32,256]{3,2,1,0:T(8,128)(2,1)S(1)}, bf16[4,2,32,256]{3,2,1,0:T(8,128)(2,1)S(1)}, bf16[4,2,32,256]{3,2,1,0:T(8,128)(2,1)S(1)}, bf16[4,2,32...) custom-call(s32[33]{0:T(128)S(1)} %pad_add_fusion.ids_ref, ...), custom_call_target="tpu_custom_call" | custom-call | tf_op jit(solution)/shard_map/deliver/pallas_call | solution.py:175
  29.5 0.6 collective-permute-start.5
  30.1 1.1 %collective-permute-start.6 = (bf16[4,2,32,256]{3,2,1,0:T(8,128)(2,1)S(1)}, bf16[4,2,32,256]{3,2,1,0:T(8,128)(2,1)S(1)}, u32[]{:S(2)}, u32[]{:S(2)}) collective-permute-start(bf16[4,2,32,256]{3,2,1,0:T(8,128)(2,1)S(1)} %get-tuple-element.33), channel_id=1, source_target_pairs={{0,128},{64,192},{128,0},{192,64},{1,129},{65,193},{129,1},{193,65... | collective-permute-start | bytes 393224 | tf_op jit(solution)/shard_map/ppermute | solution.py:152
  31.2 1.8 %collective-permute-start.7 = (bf16[4,2,32,256]{3,2,1,0:T(8,128)(2,1)S(1)}, bf16[4,2,32,256]{3,2,1,0:T(8,128)(2,1)S(1)}, u32[]{:S(2)}, u32[]{:S(2)}) collective-permute-start(bf16[4,2,32,256]{3,2,1,0:T(8,128)(2,1)S(1)} %get-tuple-element.34), channel_id=1, source_target_pairs={{0,192},{64,0},{128,64},{192,128},{1,193},{65,1},{129,65},{193,129... | collective-permute-start | bytes 393224 | tf_op jit(solution)/shard_map/ppermute | solution.py:152
  32.9 0.0 collective-permute-done.4.refs_1_
  33.0 0.7 collective-permute-start
  33.7 0.0 collective-permute-done.3.refs_0_
  33.7 2.2 %collective-permute-start.1 = (bf16[4,2,32,256]{3,2,1,0:T(8,128)(2,1)S(1)}, bf16[4,2,32,256]{3,2,1,0:T(8,128)(2,1)S(1)}, u32[]{:S(2)}, u32[]{:S(2)}) collective-permute-start(bf16[4,2,32,256]{3,2,1,0:T(8,128)(2,1)S(1)} %get-tuple-element.28), channel_id=1, source_target_pairs={{0,128},{64,192},{128,0},{192,64},{1,129},{65,193},{129,1},{193,65... | collective-permute-start | bytes 393224 | tf_op jit(solution)/shard_map/ppermute | solution.py:152
  35.8 4.0 %collective-permute-done.5.refs_3_ = bf16[4,2,32,256]{3,2,1,0:T(8,128)(2,1)S(1)} collective-permute-done((bf16[4,2,32,256]{3,2,1,0:T(8,128)(2,1)S(1)}, bf16[4,2,32,256]{3,2,1,0:T(8,128)(2,1)S(1)}, u32[]{:S(2)}, u32[]{:S(2)}) %collective-permute-start.5) | collective-permute-done | bytes 131104 | tf_op jit(solution)/shard_map/ppermute | solution.py:152
  39.8 0.0 collective-permute-start.2
  39.8 0.0 collective-permute-done.6.refs_4_
  39.9 0.9 %collective-permute-done.7.refs_5_ = bf16[4,2,32,256]{3,2,1,0:T(8,128)(2,1)S(1)} collective-permute-done((bf16[4,2,32,256]{3,2,1,0:T(8,128)(2,1)S(1)}, bf16[4,2,32,256]{3,2,1,0:T(8,128)(2,1)S(1)}, u32[]{:S(2)}, u32[]{:S(2)}) %collective-permute-start.7) | collective-permute-done | bytes 131104 | tf_op jit(solution)/shard_map/ppermute | solution.py:152
  40.8 2.4 %attention.3 = (bf16[128,2048]{1,0:T(8,128)(2,1)S(1)}, bf16[4,2,32,256]{3,2,1,0:T(8,128)(2,1)S(1)}, bf16[4,2,32,256]{3,2,1,0:T(8,128)(2,1)S(1)}, bf16[4,2,32,256...) custom-call(bf16[256,2048]{1,0:T(8,128)(2,1)S(1)} %bitcast.18, bf16[256,2048]{1,0:T(8,128)(2,1)S(1)} %bitcast.21, ...), custom_call_target="tpu_custom_call" | custom-call | tf_op jit(solution)/shard_map/attention/pallas_call | solution.py:199
  43.1 2.4 %collective-permute-start.12 = (bf16[4,2,32,256]{3,2,1,0:T(8,128)(2,1)S(1)}, bf16[4,2,32,256]{3,2,1,0:T(8,128)(2,1)S(1)}, u32[]{:S(2)}, u32[]{:S(2)}) collective-permute-start(bf16[4,2,32,256]{3,2,1,0:T(8,128)(2,1)S(1)} %get-tuple-element.41), channel_id=1, source_target_pairs={{0,192},{64,0},{128,64},{192,128},{1,193},{65,1},{129,65},{193,129... | collective-permute-start | bytes 393224 | tf_op jit(solution)/shard_map/ppermute | solution.py:152
  45.5 0.9 %collective-permute-start.13 = (bf16[4,2,32,256]{3,2,1,0:T(8,128)(2,1)S(1)}, bf16[4,2,32,256]{3,2,1,0:T(8,128)(2,1)S(1)}, u32[]{:S(2)}, u32[]{:S(2)}) collective-permute-start(bf16[4,2,32,256]{3,2,1,0:T(8,128)(2,1)S(1)} %get-tuple-element.42), channel_id=1, source_target_pairs={{0,128},{64,192},{128,0},{192,64},{1,129},{65,193},{129,1},{193,65... | collective-permute-start | bytes 393224 | tf_op jit(solution)/shard_map/ppermute | solution.py:152
  46.4 0.0 collective-permute-done.refs_1_
  46.4 0.1 collective-permute-start.14
  46.5 0.0 collective-permute-done.1.refs_2_
  46.5 0.0 collective-permute-done.2.refs_3_
  46.5 2.1 %attention.2 = (bf16[128,2048]{1,0:T(8,128)(2,1)S(1)}, bf16[4,2,32,256]{3,2,1,0:T(8,128)(2,1)S(1)}, bf16[4,2,32,256]{3,2,1,0:T(8,128)(2,1)S(1)}, bf16[4,2,32,256...) custom-call(bf16[256,2048]{1,0:T(8,128)(2,1)S(1)} %bitcast.19, bf16[256,2048]{1,0:T(8,128)(2,1)S(1)} %bitcast.22, ...), custom_call_target="tpu_custom_call" | custom-call | tf_op jit(solution)/shard_map/attention/pallas_call | solution.py:199
  48.6 3.4 %collective-permute-start.9 = (bf16[4,2,32,256]{3,2,1,0:T(8,128)(2,1)S(1)}, bf16[4,2,32,256]{3,2,1,0:T(8,128)(2,1)S(1)}, u32[]{:S(2)}, u32[]{:S(2)}) collective-permute-start(bf16[4,2,32,256]{3,2,1,0:T(8,128)(2,1)S(1)} %get-tuple-element.37), channel_id=1, source_target_pairs={{0,192},{64,0},{128,64},{192,128},{1,193},{65,1},{129,65},{193,129... | collective-permute-start | bytes 393224 | tf_op jit(solution)/shard_map/ppermute | solution.py:152
  52.0 1.4 %collective-permute-start.10 = (bf16[4,2,32,256]{3,2,1,0:T(8,128)(2,1)S(1)}, bf16[4,2,32,256]{3,2,1,0:T(8,128)(2,1)S(1)}, u32[]{:S(2)}, u32[]{:S(2)}) collective-permute-start(bf16[4,2,32,256]{3,2,1,0:T(8,128)(2,1)S(1)} %get-tuple-element.38), channel_id=1, source_target_pairs={{0,128},{64,192},{128,0},{192,64},{1,129},{65,193},{129,1},{193,65... | collective-permute-start | bytes 393224 | tf_op jit(solution)/shard_map/ppermute | solution.py:152
  53.4 0.0 collective-permute-done.12.refs_1_
  53.4 0.0 collective-permute-start.11
  53.4 0.0 collective-permute-done.13.refs_2_
  53.4 1.5 %collective-permute-done.14.refs_3_ = bf16[4,2,32,256]{3,2,1,0:T(8,128)(2,1)S(1)} collective-permute-done((bf16[4,2,32,256]{3,2,1,0:T(8,128)(2,1)S(1)}, bf16[4,2,32,256]{3,2,1,0:T(8,128)(2,1)S(1)}, u32[]{:S(2)}, u32[]{:S(2)}) %collective-permute-start.14) | collective-permute-done | bytes 131104 | tf_op jit(solution)/shard_map/ppermute | solution.py:152
  54.9 1.5 %collect.2.refs_4_ = bf16[16,2,2,32,256]{4,3,2,1,0:T(8,128)(2,1)} custom-call(s32[33]{0:T(128)S(1)} %pad_add_fusion.ids_ref, bf16[4,2,32,256]{3,2,1,0:T(8,128)(2,1)S(1)} %get-tuple-element.40.refs_0_, bf16[4,2,32,256]{3,2,1,0:T(8,128)(2,1)S(1)} %collective-permute-done.12.refs_1_, bf16[4,2,32,256]{3,2,1,0:T(8,128)(2,1)S(1)} %collective-permute-done.13.refs_2_, ...), custom_call_target="tpu_custom_call" | custom-call | tf_op jit(solution)/shard_map/collect/pallas_call | solution.py:228
  56.5 0.0 collective-permute-done.9.refs_1_
  56.5 2.0 %collective-permute-done.10.refs_2_ = bf16[4,2,32,256]{3,2,1,0:T(8,128)(2,1)S(1)} collective-permute-done((bf16[4,2,32,256]{3,2,1,0:T(8,128)(2,1)S(1)}, bf16[4,2,32,256]{3,2,1,0:T(8,128)(2,1)S(1)}, u32[]{:S(2)}, u32[]{:S(2)}) %collective-permute-start.10) | collective-permute-done | bytes 131104 | tf_op jit(solution)/shard_map/ppermute | solution.py:152
  58.5 1.4 %collective-permute-done.11.refs_3_ = bf16[4,2,32,256]{3,2,1,0:T(8,128)(2,1)S(1)} collective-permute-done((bf16[4,2,32,256]{3,2,1,0:T(8,128)(2,1)S(1)}, bf16[4,2,32,256]{3,2,1,0:T(8,128)(2,1)S(1)}, u32[]{:S(2)}, u32[]{:S(2)}) %collective-permute-start.11) | collective-permute-done | bytes 131104 | tf_op jit(solution)/shard_map/ppermute | solution.py:152
  59.9 1.5 %collect.3 = bf16[16,2,2,32,256]{4,3,2,1,0:T(8,128)(2,1)} custom-call(s32[33]{0:T(128)S(1)} %pad_add_fusion.ids_ref, bf16[4,2,32,256]{3,2,1,0:T(8,128)(2,1)S(1)} %get-tuple-element.36.refs_0_, bf16[4,2,32,256]{3,2,1,0:T(8,128)(2,1)S(1)} %collective-permute-done.9.refs_1_, ...), custom_call_target="tpu_custom_call", output_to_operand_aliasing={{}: (5, {})} | custom-call | tf_op jit(solution)/shard_map/collect/pallas_call | solution.py:228
  61.4 3.7 %all-to-all-start.1 = ((bf16[16,2,2,32,256]{4,3,2,1,0:T(8,128)(2,1)}), bf16[16,2,2,32,256]{4,3,2,1,0:T(8,128)(2,1)S(1)}, u32[]{:S(2)}, u32[]{:S(2)}) async-start(bf16[16,2,2,32,256]{4,3,2,1,0:T(8,128)(2,1)} %collect.3), calls=%async_computation.1 | async-start | bytes 2097152 | tf_op jit(solution)/shard_map/all_to_all | solution.py:245
  65.2 1.9 %collective-permute-start.8 = (bf16[64,2048]{1,0:T(8,128)(2,1)S(1)}, bf16[64,2048]{1,0:T(8,128)(2,1)S(1)}, u32[]{:S(2)}, u32[]{:S(2)}) collective-permute-start(bf16[64,2048]{1,0:T(8,128)(2,1)S(1)} %slice.14), channel_id=1, source_target_pairs={{0,4},{4,8},{8,12},{12,16},{16,20},{20,24},{24,28},{28,32},{32,36}... | collective-permute-start | bytes 786440 | tf_op jit(solution)/shard_map/ppermute | solution.py:218
  67.1 0.1 fusion.1
  67.2 5.7 %collective-permute-done.8 = bf16[64,2048]{1,0:T(8,128)(2,1)S(1)} collective-permute-done((bf16[64,2048]{1,0:T(8,128)(2,1)S(1)}, bf16[64,2048]{1,0:T(8,128)(2,1)S(1)}, u32[]{:S(2)}, u32[]{:S(2)}) %collective-permute-start.8) | collective-permute-done | bytes 262176 | tf_op jit(solution)/shard_map/ppermute | solution.py:218
  72.9 1.3 %fusion = bf16[1,256,2048]{2,1,0:T(8,128)(2,1)} fusion(bf16[1,128,2048]{2,1,0:T(8,128)(2,1)S(1)} %bitcast.23, bf16[1,128,2048]{2,1,0:T(8,128)(2,1)S(1)} %bitcast.24, bf16[1,192,2048]{2,1,0:T(8,128)(2,1)S(1)} %fusion.1, bf16[1,64,2048]{2,1,0:T(8,128)(2,1)S(1)} %bitcast.28, s32[256]{0:T(256)S(1)} %get-tuple-element.44, s32[256]{0:T(256)S(1)} %get-tuple-element.45, ...), kind=kLoop, calls=%fused_computation.1 | loop fusion | flops 5767168 | bytes 3148032 | tf_op jit(solution)/shard_map/jit(_where)/select_n | solution.py:220
  74.2 3.9 %all-to-all-done.1 = bf16[16,2,2,32,256]{4,3,2,1,0:T(8,128)(2,1)S(1)} async-done(((bf16[16,2,2,32,256]{4,3,2,1,0:T(8,128)(2,1)}), bf16[16,2,2,32,256]{4,3,2,1,0:T(8,128)(2,1)S(1)}, u32[]{:S(2)}, u32[]{:S(2)}) %all-to-all-start.1) | async-done | bytes 1048608 | tf_op jit(solution)/shard_map/all_to_all | solution.py:245
  78.0 0.8 %copy.12 = bf16[2,4,32,2,4,256]{5,4,3,2,1,0:T(4,128)(2,1)S(1)} copy(bf16[2,4,32,2,4,256]{5,2,0,3,1,4:T(8,128)(2,1)S(1)} %bitcast.26) | data formatting | bytes 2097152 | tf_op jit(solution)/shard_map/transpose | solution.py:247
  78.9 1.2 %reshape.136 = bf16[2,128,2,1024]{3,2,1,0:T(2,128)(2,1)} reshape(bf16[2,4,32,2,4,256]{5,4,3,2,1,0:T(4,128)(2,1)S(1)} %copy.12) | data formatting | bytes 2097152 | tf_op jit(solution)/shard_map/reshape | solution.py:248
  (3 shorter events, 0.0 us)
Async XLA Ops:
  0.6 16.6 %copy-start = (s32[4,64,2]{1,2,0:T(2,128)S(1)}, s32[4,64,2]{1,2,0:T(2,128)}, u32[]{:S(2)}) copy-start(s32[4,64,2]{1,2,0:T(2,128)} %param.7) | copy-start | bytes 6148
  3.6 7.2 %copy-start.2 = (bf16[1,256,2048]{2,1,0:T(8,128)(2,1)S(1)}, bf16[1,256,2048]{2,1,0:T(8,128)(2,1)}, u32[]{:S(2)}) copy-start(bf16[1,256,2048]{2,1,0:T(8,128)(2,1)} %param.5) | copy-start | bytes 3145732
  3.6 10.0 %copy-start.1 = (bf16[1,256,2048]{2,1,0:T(8,128)(2,1)S(1)}, bf16[1,256,2048]{2,1,0:T(8,128)(2,1)}, u32[]{:S(2)}) copy-start(bf16[1,256,2048]{2,1,0:T(8,128)(2,1)} %param.4) | copy-start | bytes 3145732
  3.6 24.9 %all-to-all-start = ((bf16[16,2,2,32,256]{4,3,2,1,0:T(8,128)(2,1)}), bf16[16,2,2,32,256]{4,3,2,1,0:T(8,128)(2,1)S(1)}, u32[]{:S(2)}, u32[]{:S(2)}) async-start(bf16[16,2,2,32,256]{4,3,2,1,0:T(8,128)(2,1)} %bitcast.25), calls=%async_computation | async-start | bytes 2097152 | tf_op jit(solution)/shard_map/all_to_all | solution.py:163
  11.5 21.4 %collective-permute-start.4 = (bf16[64,2048]{1,0:T(8,128)(2,1)}, bf16[64,2048]{1,0:T(8,128)(2,1)S(1)}, u32[]{:S(2)}, u32[]{:S(2)}) collective-permute-start(bf16[64,2048]{1,0:T(8,128)(2,1)} %slice.13), channel_id=1, source_target_pairs={{4,0},{8,4},{12,8},{16,12},{20,16},{24,20},{28,24},{32,28},{36,32}... | collective-permute-start | bytes 786440 | tf_op jit(solution)/shard_map/ppermute | solution.py:167
  14.3 19.3 %collective-permute-start.3 = (bf16[64,2048]{1,0:T(8,128)(2,1)}, bf16[64,2048]{1,0:T(8,128)(2,1)}, u32[]{:S(2)}, u32[]{:S(2)}) collective-permute-start(bf16[64,2048]{1,0:T(8,128)(2,1)} %slice.12), channel_id=1, source_target_pairs={{4,0},{8,4},{12,8},{16,12},{20,16},{24,20},{28,24},{32,28},{36,32}... | collective-permute-start | bytes 786440 | tf_op jit(solution)/shard_map/ppermute | solution.py:167
  29.5 10.4 %collective-permute-start.5 = (bf16[4,2,32,256]{3,2,1,0:T(8,128)(2,1)S(1)}, bf16[4,2,32,256]{3,2,1,0:T(8,128)(2,1)S(1)}, u32[]{:S(2)}, u32[]{:S(2)}) collective-permute-start(bf16[4,2,32,256]{3,2,1,0:T(8,128)(2,1)S(1)} %get-tuple-element.32), channel_id=1, source_target_pairs={{0,64},{64,128},{128,192},{192,0},{1,65},{65,129},{129,193},{193,1... | collective-permute-start | bytes 393224 | tf_op jit(solution)/shard_map/ppermute | solution.py:152
  30.1 9.7 %collective-permute-start.6 = (bf16[4,2,32,256]{3,2,1,0:T(8,128)(2,1)S(1)}, bf16[4,2,32,256]{3,2,1,0:T(8,128)(2,1)S(1)}, u32[]{:S(2)}, u32[]{:S(2)}) collective-permute-start(bf16[4,2,32,256]{3,2,1,0:T(8,128)(2,1)S(1)} %get-tuple-element.33), channel_id=1, source_target_pairs={{0,128},{64,192},{128,0},{192,64},{1,129},{65,193},{129,1},{193,65... | collective-permute-start | bytes 393224 | tf_op jit(solution)/shard_map/ppermute | solution.py:152
  31.2 9.6 %collective-permute-start.7 = (bf16[4,2,32,256]{3,2,1,0:T(8,128)(2,1)S(1)}, bf16[4,2,32,256]{3,2,1,0:T(8,128)(2,1)S(1)}, u32[]{:S(2)}, u32[]{:S(2)}) collective-permute-start(bf16[4,2,32,256]{3,2,1,0:T(8,128)(2,1)S(1)} %get-tuple-element.34), channel_id=1, source_target_pairs={{0,192},{64,0},{128,64},{192,128},{1,193},{65,1},{129,65},{193,129... | collective-permute-start | bytes 393224 | tf_op jit(solution)/shard_map/ppermute | solution.py:152
  33.0 13.4 %collective-permute-start = (bf16[4,2,32,256]{3,2,1,0:T(8,128)(2,1)S(1)}, bf16[4,2,32,256]{3,2,1,0:T(8,128)(2,1)S(1)}, u32[]{:S(2)}, u32[]{:S(2)}) collective-permute-start(bf16[4,2,32,256]{3,2,1,0:T(8,128)(2,1)S(1)} %get-tuple-element.27), channel_id=1, source_target_pairs={{0,64},{64,128},{128,192},{192,0},{1,65},{65,129},{129,193},{193,1... | collective-permute-start | bytes 393224 | tf_op jit(solution)/shard_map/ppermute | solution.py:152
  33.7 12.8 %collective-permute-start.1 = (bf16[4,2,32,256]{3,2,1,0:T(8,128)(2,1)S(1)}, bf16[4,2,32,256]{3,2,1,0:T(8,128)(2,1)S(1)}, u32[]{:S(2)}, u32[]{:S(2)}) collective-permute-start(bf16[4,2,32,256]{3,2,1,0:T(8,128)(2,1)S(1)} %get-tuple-element.28), channel_id=1, source_target_pairs={{0,128},{64,192},{128,0},{192,64},{1,129},{65,193},{129,1},{193,65... | collective-permute-start | bytes 393224 | tf_op jit(solution)/shard_map/ppermute | solution.py:152
  39.8 6.6 %collective-permute-start.2 = (bf16[4,2,32,256]{3,2,1,0:T(8,128)(2,1)S(1)}, bf16[4,2,32,256]{3,2,1,0:T(8,128)(2,1)S(1)}, u32[]{:S(2)}, u32[]{:S(2)}) collective-permute-start(bf16[4,2,32,256]{3,2,1,0:T(8,128)(2,1)S(1)} %get-tuple-element.29), channel_id=1, source_target_pairs={{0,192},{64,0},{128,64},{192,128},{1,193},{65,1},{129,65},{193,129... | collective-permute-start | bytes 393224 | tf_op jit(solution)/shard_map/ppermute | solution.py:152
  43.1 10.3 %collective-permute-start.12 = (bf16[4,2,32,256]{3,2,1,0:T(8,128)(2,1)S(1)}, bf16[4,2,32,256]{3,2,1,0:T(8,128)(2,1)S(1)}, u32[]{:S(2)}, u32[]{:S(2)}) collective-permute-start(bf16[4,2,32,256]{3,2,1,0:T(8,128)(2,1)S(1)} %get-tuple-element.41), channel_id=1, source_target_pairs={{0,192},{64,0},{128,64},{192,128},{1,193},{65,1},{129,65},{193,129... | collective-permute-start | bytes 393224 | tf_op jit(solution)/shard_map/ppermute | solution.py:152
  45.5 7.9 %collective-permute-start.13 = (bf16[4,2,32,256]{3,2,1,0:T(8,128)(2,1)S(1)}, bf16[4,2,32,256]{3,2,1,0:T(8,128)(2,1)S(1)}, u32[]{:S(2)}, u32[]{:S(2)}) collective-permute-start(bf16[4,2,32,256]{3,2,1,0:T(8,128)(2,1)S(1)} %get-tuple-element.42), channel_id=1, source_target_pairs={{0,128},{64,192},{128,0},{192,64},{1,129},{65,193},{129,1},{193,65... | collective-permute-start | bytes 393224 | tf_op jit(solution)/shard_map/ppermute | solution.py:152
  46.4 8.6 %collective-permute-start.14 = (bf16[4,2,32,256]{3,2,1,0:T(8,128)(2,1)S(1)}, bf16[4,2,32,256]{3,2,1,0:T(8,128)(2,1)S(1)}, u32[]{:S(2)}, u32[]{:S(2)}) collective-permute-start(bf16[4,2,32,256]{3,2,1,0:T(8,128)(2,1)S(1)} %get-tuple-element.43), channel_id=1, source_target_pairs={{0,64},{64,128},{128,192},{192,0},{1,65},{65,129},{129,193},{193,1... | collective-permute-start | bytes 393224 | tf_op jit(solution)/shard_map/ppermute | solution.py:152
  48.6 7.9 %collective-permute-start.9 = (bf16[4,2,32,256]{3,2,1,0:T(8,128)(2,1)S(1)}, bf16[4,2,32,256]{3,2,1,0:T(8,128)(2,1)S(1)}, u32[]{:S(2)}, u32[]{:S(2)}) collective-permute-start(bf16[4,2,32,256]{3,2,1,0:T(8,128)(2,1)S(1)} %get-tuple-element.37), channel_id=1, source_target_pairs={{0,192},{64,0},{128,64},{192,128},{1,193},{65,1},{129,65},{193,129... | collective-permute-start | bytes 393224 | tf_op jit(solution)/shard_map/ppermute | solution.py:152
  52.0 6.5 %collective-permute-start.10 = (bf16[4,2,32,256]{3,2,1,0:T(8,128)(2,1)S(1)}, bf16[4,2,32,256]{3,2,1,0:T(8,128)(2,1)S(1)}, u32[]{:S(2)}, u32[]{:S(2)}) collective-permute-start(bf16[4,2,32,256]{3,2,1,0:T(8,128)(2,1)S(1)} %get-tuple-element.38), channel_id=1, source_target_pairs={{0,128},{64,192},{128,0},{192,64},{1,129},{65,193},{129,1},{193,65... | collective-permute-start | bytes 393224 | tf_op jit(solution)/shard_map/ppermute | solution.py:152
  53.4 6.4 %collective-permute-start.11 = (bf16[4,2,32,256]{3,2,1,0:T(8,128)(2,1)S(1)}, bf16[4,2,32,256]{3,2,1,0:T(8,128)(2,1)S(1)}, u32[]{:S(2)}, u32[]{:S(2)}) collective-permute-start(bf16[4,2,32,256]{3,2,1,0:T(8,128)(2,1)S(1)} %get-tuple-element.39), channel_id=1, source_target_pairs={{0,64},{64,128},{128,192},{192,0},{1,65},{65,129},{129,193},{193,1... | collective-permute-start | bytes 393224 | tf_op jit(solution)/shard_map/ppermute | solution.py:152
  61.4 16.6 %all-to-all-start.1 = ((bf16[16,2,2,32,256]{4,3,2,1,0:T(8,128)(2,1)}), bf16[16,2,2,32,256]{4,3,2,1,0:T(8,128)(2,1)S(1)}, u32[]{:S(2)}, u32[]{:S(2)}) async-start(bf16[16,2,2,32,256]{4,3,2,1,0:T(8,128)(2,1)} %collect.3), calls=%async_computation.1 | async-start | bytes 2097152 | tf_op jit(solution)/shard_map/all_to_all | solution.py:245
  65.2 7.7 %collective-permute-start.8 = (bf16[64,2048]{1,0:T(8,128)(2,1)S(1)}, bf16[64,2048]{1,0:T(8,128)(2,1)S(1)}, u32[]{:S(2)}, u32[]{:S(2)}) collective-permute-start(bf16[64,2048]{1,0:T(8,128)(2,1)S(1)} %slice.14), channel_id=1, source_target_pairs={{0,4},{4,8},{8,12},{12,16},{16,20},{20,24},{24,28},{28,32},{32,36}... | collective-permute-start | bytes 786440 | tf_op jit(solution)/shard_map/ppermute | solution.py:218

commit v7 on v6

--- a/solution.py
+++ b/solution.py
@@ -26,18 +26,25 @@
     return lax.dot_general(a, b, (((1,), (0,)), ((), ())), preferred_element_type=jnp.float32)
 
 
+def split(value, size):
+    if size & (size - 1) == 0:
+        return lax.shift_right_logical(value, size.bit_length() - 1), value & (size - 1)
+    return lax.div(value, size), lax.rem(value, size)
+
+
 def place_of(row, geometry):
     local_rows, dp_size, context_size, tensor_size = geometry
-    device = row // local_rows
-    source = device % tensor_size * dp_size + device // (context_size * tensor_size)
-    return source, row % local_rows
+    device, part = split(row, local_rows)
+    tensor = split(device, tensor_size)[1]
+    dp = split(device, context_size * tensor_size)[0]
+    return tensor * dp_size + dp, part
 
 
 def listed_places(ids_ref, blocks, owners, geometry, first, count):
     lengths = [block.shape[0] for block in blocks[::owners]]
     me = ids_ref[owners * count]
     for o, block in enumerate(blocks):
-        start = (me + o % owners) % owners * count + first + sum(lengths[: o // owners])
+        start = split(me + o % owners, owners)[1] * count + first + sum(lengths[: o // owners])
         for k in range(block.shape[0]):
             yield block, k, place_of(ids_ref[start + k], geometry)
 

time: 80.4 us -> 80 us (level)
  transfers between devices with their start and end apart: 17 -> 17, of which waited for: 8 -> 8; matrix products, arithmetic and copies ran while one was open for 4% -> 4% of each run, Pallas kernels for 9% -> 8%
where the time goes in v7:
time: 80 us; the launch traced here: 79.7 us
  starting transfers between devices  32.3 us (40%)
  waiting for transfers between devices  30.3 us (38%)
  Pallas kernels  8.04 us (10%)
  local copies, waits for them, and re-layouts  6.76 us (8%)
  other arithmetic  1.46 us (2%)
  between operations  0.82 us (1%)
    ppermute x12, starting transfers between devices, ring(): lax.ppermute(array, 'dp', [(i, (i + by) % dp_size) for i in range(dp_size)])  14.5 us
    all_to_all x1, waiting for transfers between devices, shards(): held = lax.all_to_all(spread, group, 0, 0, tiled=True)  10.9 us
    ppermute x12, waiting for transfers between devices, ring(): lax.ppermute(array, 'dp', [(i, (i + by) % dp_size) for i in range(dp_size)])  9.88 us
    all_to_all x1, starting transfers between devices, shards(): held = lax.all_to_all(spread, group, 0, 0, tiled=True)  7.17 us
    ppermute x1, waiting for transfers between devices, shards(): before = lax.ppermute(windows[row_count - SPAN:], 'context', forth)  5.68 us
    ppermute x2, starting transfers between devices, shards(): lax.ppermute(values[:SPAN], 'context', back)  4.92 us
    pallas_call x2, Pallas kernels, shards(): pl.pallas_call(functools.partial(attention_kernel, parts=dp_size, halo=en...  4.44 us
    all_to_all x1, waiting for transfers between devices, shards(): final = lax.all_to_all(collected[0], group, 0, 0, tiled=True)  3.87 us
  transfers between devices with their start and end apart: 17, of which 8 were waited for; matrix products, arithmetic and copies ran while one was open for 4% of the time, Pallas kernels for 8%

profile of v7, /device:TPU:224, one launch (start us, length us, event | category | flops | bytes accessed | tf_op | source)
XLA Modules:
  0.0 79.7 jit_solution(7910863036285820464)
XLA Ops:
  0.6 0.0 copy-start
  0.6 1.7 %reshape.132 = bf16[2,2,4,32,4,256]{5,4,0,3,2,1:T(4,128)(2,1)S(1)} reshape(bf16[2,2,128,1024]{3,0,2,1:T(2,128)(2,1)} %bitcast.27) | data formatting | bytes 2097152 | tf_op jit(solution)/shard_map/reshape | solution.py:162
  2.4 1.2 %copy.10 = bf16[2,2,4,32,4,256]{5,3,1,0,2,4:T(8,128)(2,1)} copy(bf16[2,2,4,32,4,256]{5,4,0,3,2,1:T(4,128)(2,1)S(1)} %reshape.132) | data formatting | bytes 2097152 | tf_op jit(solution)/shard_map/reshape | solution.py:162
  3.6 0.0 copy-start.2
  3.6 0.0 copy-start.1
  3.6 7.2 %all-to-all-start = ((bf16[16,2,2,32,256]{4,3,2,1,0:T(8,128)(2,1)}), bf16[16,2,2,32,256]{4,3,2,1,0:T(8,128)(2,1)S(1)}, u32[]{:S(2)}, u32[]{:S(2)}) async-start(bf16[16,2,2,32,256]{4,3,2,1,0:T(8,128)(2,1)} %bitcast.25), calls=%async_computation | async-start | bytes 2097152 | tf_op jit(solution)/shard_map/all_to_all | solution.py:170
  10.8 0.0 copy-done.2
  10.8 0.7 slice.13
  11.5 2.1 %collective-permute-start.4 = (bf16[64,2048]{1,0:T(8,128)(2,1)}, bf16[64,2048]{1,0:T(8,128)(2,1)S(1)}, u32[]{:S(2)}, u32[]{:S(2)}) collective-permute-start(bf16[64,2048]{1,0:T(8,128)(2,1)} %slice.13), channel_id=1, source_target_pairs={{4,0},{8,4},{12,8},{16,12},{20,16},{24,20},{28,24},{32,28},{36,32}... | collective-permute-start | bytes 786440 | tf_op jit(solution)/shard_map/ppermute | solution.py:174
  13.6 0.0 copy-done.1
  13.6 0.7 slice.12
  14.3 2.9 %collective-permute-start.3 = (bf16[64,2048]{1,0:T(8,128)(2,1)}, bf16[64,2048]{1,0:T(8,128)(2,1)}, u32[]{:S(2)}, u32[]{:S(2)}) collective-permute-start(bf16[64,2048]{1,0:T(8,128)(2,1)} %slice.12), channel_id=1, source_target_pairs={{4,0},{8,4},{12,8},{16,12},{20,16},{24,20},{28,24},{32,28},{36,32}... | collective-permute-start | bytes 786440 | tf_op jit(solution)/shard_map/ppermute | solution.py:174
  17.2 0.0 copy-done
  17.2 0.1 constant_dynamic-slice_fusion
  17.3 0.1 copy.11
  17.4 0.1 reshape.134
  17.5 0.1 pad_add_fusion.ids_ref
  17.6 10.9 %all-to-all-done.held_ref = bf16[16,2,2,32,256]{4,3,2,1,0:T(8,128)(2,1)S(1)} async-done(((bf16[16,2,2,32,256]{4,3,2,1,0:T(8,128)(2,1)}), bf16[16,2,2,32,256]{4,3,2,1,0:T(8,128)(2,1)S(1)}, u32[]{:S(2)}, u32[]{:S(2)}) %all-to-all-start) | async-done | bytes 1048608 | tf_op jit(solution)/shard_map/all_to_all | solution.py:170
  28.5 0.7 deliver.1
  29.2 0.6 collective-permute-start.5
  29.8 1.1 %collective-permute-start.6 = (bf16[4,2,32,256]{3,2,1,0:T(8,128)(2,1)S(1)}, bf16[4,2,32,256]{3,2,1,0:T(8,128)(2,1)S(1)}, u32[]{:S(2)}, u32[]{:S(2)}) collective-permute-start(bf16[4,2,32,256]{3,2,1,0:T(8,128)(2,1)S(1)} %get-tuple-element.33), channel_id=1, source_target_pairs={{0,128},{64,192},{128,0},{192,64},{1,129},{65,193},{129,1},{193,65... | collective-permute-start | bytes 393224 | tf_op jit(solution)/shard_map/ppermute | solution.py:159
  30.8 1.8 %collective-permute-start.7 = (bf16[4,2,32,256]{3,2,1,0:T(8,128)(2,1)S(1)}, bf16[4,2,32,256]{3,2,1,0:T(8,128)(2,1)S(1)}, u32[]{:S(2)}, u32[]{:S(2)}) collective-permute-start(bf16[4,2,32,256]{3,2,1,0:T(8,128)(2,1)S(1)} %get-tuple-element.34), channel_id=1, source_target_pairs={{0,192},{64,0},{128,64},{192,128},{1,193},{65,1},{129,65},{193,129... | collective-permute-start | bytes 393224 | tf_op jit(solution)/shard_map/ppermute | solution.py:159
  32.6 0.0 collective-permute-done.4.refs_1_
  32.6 0.7 collective-permute-start
  33.3 0.0 collective-permute-done.3.refs_0_
  33.3 2.2 %collective-permute-start.1 = (bf16[4,2,32,256]{3,2,1,0:T(8,128)(2,1)S(1)}, bf16[4,2,32,256]{3,2,1,0:T(8,128)(2,1)S(1)}, u32[]{:S(2)}, u32[]{:S(2)}) collective-permute-start(bf16[4,2,32,256]{3,2,1,0:T(8,128)(2,1)S(1)} %get-tuple-element.28), channel_id=1, source_target_pairs={{0,128},{64,192},{128,0},{192,64},{1,129},{65,193},{129,1},{193,65... | collective-permute-start | bytes 393224 | tf_op jit(solution)/shard_map/ppermute | solution.py:159
  35.5 4.0 %collective-permute-done.5.refs_3_ = bf16[4,2,32,256]{3,2,1,0:T(8,128)(2,1)S(1)} collective-permute-done((bf16[4,2,32,256]{3,2,1,0:T(8,128)(2,1)S(1)}, bf16[4,2,32,256]{3,2,1,0:T(8,128)(2,1)S(1)}, u32[]{:S(2)}, u32[]{:S(2)}) %collective-permute-start.5) | collective-permute-done | bytes 131104 | tf_op jit(solution)/shard_map/ppermute | solution.py:159
  39.5 0.0 collective-permute-start.2
  39.5 0.0 collective-permute-done.6.refs_4_
  39.5 0.9 %collective-permute-done.7.refs_5_ = bf16[4,2,32,256]{3,2,1,0:T(8,128)(2,1)S(1)} collective-permute-done((bf16[4,2,32,256]{3,2,1,0:T(8,128)(2,1)S(1)}, bf16[4,2,32,256]{3,2,1,0:T(8,128)(2,1)S(1)}, u32[]{:S(2)}, u32[]{:S(2)}) %collective-permute-start.7) | collective-permute-done | bytes 131104 | tf_op jit(solution)/shard_map/ppermute | solution.py:159
  40.4 2.4 %attention.3 = (bf16[128,2048]{1,0:T(8,128)(2,1)S(1)}, bf16[4,2,32,256]{3,2,1,0:T(8,128)(2,1)S(1)}, bf16[4,2,32,256]{3,2,1,0:T(8,128)(2,1)S(1)}, bf16[4,2,32,256...) custom-call(bf16[256,2048]{1,0:T(8,128)(2,1)S(1)} %bitcast.18, bf16[256,2048]{1,0:T(8,128)(2,1)S(1)} %bitcast.21, ...), custom_call_target="tpu_custom_call" | custom-call | tf_op jit(solution)/shard_map/attention/pallas_call | solution.py:206
  42.8 2.4 %collective-permute-start.12 = (bf16[4,2,32,256]{3,2,1,0:T(8,128)(2,1)S(1)}, bf16[4,2,32,256]{3,2,1,0:T(8,128)(2,1)S(1)}, u32[]{:S(2)}, u32[]{:S(2)}) collective-permute-start(bf16[4,2,32,256]{3,2,1,0:T(8,128)(2,1)S(1)} %get-tuple-element.41), channel_id=1, source_target_pairs={{0,192},{64,0},{128,64},{192,128},{1,193},{65,1},{129,65},{193,129... | collective-permute-start | bytes 393224 | tf_op jit(solution)/shard_map/ppermute | solution.py:159
  45.2 0.9 %collective-permute-start.13 = (bf16[4,2,32,256]{3,2,1,0:T(8,128)(2,1)S(1)}, bf16[4,2,32,256]{3,2,1,0:T(8,128)(2,1)S(1)}, u32[]{:S(2)}, u32[]{:S(2)}) collective-permute-start(bf16[4,2,32,256]{3,2,1,0:T(8,128)(2,1)S(1)} %get-tuple-element.42), channel_id=1, source_target_pairs={{0,128},{64,192},{128,0},{192,64},{1,129},{65,193},{129,1},{193,65... | collective-permute-start | bytes 393224 | tf_op jit(solution)/shard_map/ppermute | solution.py:159
  46.1 0.0 collective-permute-done.refs_1_
  46.1 0.1 collective-permute-start.14
  46.1 0.0 collective-permute-done.1.refs_2_
  46.1 0.0 collective-permute-done.2.refs_3_
  46.1 2.1 %attention.2 = (bf16[128,2048]{1,0:T(8,128)(2,1)S(1)}, bf16[4,2,32,256]{3,2,1,0:T(8,128)(2,1)S(1)}, bf16[4,2,32,256]{3,2,1,0:T(8,128)(2,1)S(1)}, bf16[4,2,32,256...) custom-call(bf16[256,2048]{1,0:T(8,128)(2,1)S(1)} %bitcast.19, bf16[256,2048]{1,0:T(8,128)(2,1)S(1)} %bitcast.22, ...), custom_call_target="tpu_custom_call" | custom-call | tf_op jit(solution)/shard_map/attention/pallas_call | solution.py:206
  48.2 3.4 %collective-permute-start.9 = (bf16[4,2,32,256]{3,2,1,0:T(8,128)(2,1)S(1)}, bf16[4,2,32,256]{3,2,1,0:T(8,128)(2,1)S(1)}, u32[]{:S(2)}, u32[]{:S(2)}) collective-permute-start(bf16[4,2,32,256]{3,2,1,0:T(8,128)(2,1)S(1)} %get-tuple-element.37), channel_id=1, source_target_pairs={{0,192},{64,0},{128,64},{192,128},{1,193},{65,1},{129,65},{193,129... | collective-permute-start | bytes 393224 | tf_op jit(solution)/shard_map/ppermute | solution.py:159
  51.6 1.4 %collective-permute-start.10 = (bf16[4,2,32,256]{3,2,1,0:T(8,128)(2,1)S(1)}, bf16[4,2,32,256]{3,2,1,0:T(8,128)(2,1)S(1)}, u32[]{:S(2)}, u32[]{:S(2)}) collective-permute-start(bf16[4,2,32,256]{3,2,1,0:T(8,128)(2,1)S(1)} %get-tuple-element.38), channel_id=1, source_target_pairs={{0,128},{64,192},{128,0},{192,64},{1,129},{65,193},{129,1},{193,65... | collective-permute-start | bytes 393224 | tf_op jit(solution)/shard_map/ppermute | solution.py:159
  53.1 0.0 collective-permute-done.12.refs_1_
  53.1 0.0 collective-permute-start.11
  53.1 0.0 collective-permute-done.13.refs_2_
  53.1 1.5 %collective-permute-done.14.refs_3_ = bf16[4,2,32,256]{3,2,1,0:T(8,128)(2,1)S(1)} collective-permute-done((bf16[4,2,32,256]{3,2,1,0:T(8,128)(2,1)S(1)}, bf16[4,2,32,256]{3,2,1,0:T(8,128)(2,1)S(1)}, u32[]{:S(2)}, u32[]{:S(2)}) %collective-permute-start.14) | collective-permute-done | bytes 131104 | tf_op jit(solution)/shard_map/ppermute | solution.py:159
  54.6 1.5 %collect.2.refs_4_ = bf16[16,2,2,32,256]{4,3,2,1,0:T(8,128)(2,1)} custom-call(s32[33]{0:T(128)S(1)} %pad_add_fusion.ids_ref, bf16[4,2,32,256]{3,2,1,0:T(8,128)(2,1)S(1)} %get-tuple-element.40.refs_0_, bf16[4,2,32,256]{3,2,1,0:T(8,128)(2,1)S(1)} %collective-permute-done.12.refs_1_, bf16[4,2,32,256]{3,2,1,0:T(8,128)(2,1)S(1)} %collective-permute-done.13.refs_2_, ...), custom_call_target="tpu_custom_call" | custom-call | tf_op jit(solution)/shard_map/collect/pallas_call | solution.py:235
  56.1 0.0 collective-permute-done.9.refs_1_
  56.1 2.0 %collective-permute-done.10.refs_2_ = bf16[4,2,32,256]{3,2,1,0:T(8,128)(2,1)S(1)} collective-permute-done((bf16[4,2,32,256]{3,2,1,0:T(8,128)(2,1)S(1)}, bf16[4,2,32,256]{3,2,1,0:T(8,128)(2,1)S(1)}, u32[]{:S(2)}, u32[]{:S(2)}) %collective-permute-start.10) | collective-permute-done | bytes 131104 | tf_op jit(solution)/shard_map/ppermute | solution.py:159
  58.1 1.4 %collective-permute-done.11.refs_3_ = bf16[4,2,32,256]{3,2,1,0:T(8,128)(2,1)S(1)} collective-permute-done((bf16[4,2,32,256]{3,2,1,0:T(8,128)(2,1)S(1)}, bf16[4,2,32,256]{3,2,1,0:T(8,128)(2,1)S(1)}, u32[]{:S(2)}, u32[]{:S(2)}) %collective-permute-start.11) | collective-permute-done | bytes 131104 | tf_op jit(solution)/shard_map/ppermute | solution.py:159
  59.5 1.5 %collect.3 = bf16[16,2,2,32,256]{4,3,2,1,0:T(8,128)(2,1)} custom-call(s32[33]{0:T(128)S(1)} %pad_add_fusion.ids_ref, bf16[4,2,32,256]{3,2,1,0:T(8,128)(2,1)S(1)} %get-tuple-element.36.refs_0_, bf16[4,2,32,256]{3,2,1,0:T(8,128)(2,1)S(1)} %collective-permute-done.9.refs_1_, ...), custom_call_target="tpu_custom_call", output_to_operand_aliasing={{}: (5, {})} | custom-call | tf_op jit(solution)/shard_map/collect/pallas_call | solution.py:235
  61.0 3.7 %all-to-all-start.1 = ((bf16[16,2,2,32,256]{4,3,2,1,0:T(8,128)(2,1)}), bf16[16,2,2,32,256]{4,3,2,1,0:T(8,128)(2,1)S(1)}, u32[]{:S(2)}, u32[]{:S(2)}) async-start(bf16[16,2,2,32,256]{4,3,2,1,0:T(8,128)(2,1)} %collect.3), calls=%async_computation.1 | async-start | bytes 2097152 | tf_op jit(solution)/shard_map/all_to_all | solution.py:252
  64.8 1.9 %collective-permute-start.8 = (bf16[64,2048]{1,0:T(8,128)(2,1)S(1)}, bf16[64,2048]{1,0:T(8,128)(2,1)S(1)}, u32[]{:S(2)}, u32[]{:S(2)}) collective-permute-start(bf16[64,2048]{1,0:T(8,128)(2,1)S(1)} %slice.14), channel_id=1, source_target_pairs={{0,4},{4,8},{8,12},{12,16},{16,20},{20,24},{24,28},{28,32},{32,36}... | collective-permute-start | bytes 786440 | tf_op jit(solution)/shard_map/ppermute | solution.py:225
  66.7 0.1 fusion.1
  66.8 5.7 %collective-permute-done.8 = bf16[64,2048]{1,0:T(8,128)(2,1)S(1)} collective-permute-done((bf16[64,2048]{1,0:T(8,128)(2,1)S(1)}, bf16[64,2048]{1,0:T(8,128)(2,1)S(1)}, u32[]{:S(2)}, u32[]{:S(2)}) %collective-permute-start.8) | collective-permute-done | bytes 262176 | tf_op jit(solution)/shard_map/ppermute | solution.py:225
  72.5 1.3 %fusion = bf16[1,256,2048]{2,1,0:T(8,128)(2,1)} fusion(bf16[1,128,2048]{2,1,0:T(8,128)(2,1)S(1)} %bitcast.23, bf16[1,128,2048]{2,1,0:T(8,128)(2,1)S(1)} %bitcast.24, bf16[1,192,2048]{2,1,0:T(8,128)(2,1)S(1)} %fusion.1, bf16[1,64,2048]{2,1,0:T(8,128)(2,1)S(1)} %bitcast.28, s32[256]{0:T(256)S(1)} %get-tuple-element.44, s32[256]{0:T(256)S(1)} %get-tuple-element.45, ...), kind=kLoop, calls=%fused_computation.1 | loop fusion | flops 5767168 | bytes 3148032 | tf_op jit(solution)/shard_map/jit(_where)/select_n | solution.py:227
  73.8 3.9 %all-to-all-done.1 = bf16[16,2,2,32,256]{4,3,2,1,0:T(8,128)(2,1)S(1)} async-done(((bf16[16,2,2,32,256]{4,3,2,1,0:T(8,128)(2,1)}), bf16[16,2,2,32,256]{4,3,2,1,0:T(8,128)(2,1)S(1)}, u32[]{:S(2)}, u32[]{:S(2)}) %all-to-all-start.1) | async-done | bytes 1048608 | tf_op jit(solution)/shard_map/all_to_all | solution.py:252
  77.7 0.8 %copy.12 = bf16[2,4,32,2,4,256]{5,4,3,2,1,0:T(4,128)(2,1)S(1)} copy(bf16[2,4,32,2,4,256]{5,2,0,3,1,4:T(8,128)(2,1)S(1)} %bitcast.26) | data formatting | bytes 2097152 | tf_op jit(solution)/shard_map/transpose | solution.py:254
  78.5 1.2 %reshape.136 = bf16[2,128,2,1024]{3,2,1,0:T(2,128)(2,1)} reshape(bf16[2,4,32,2,4,256]{5,4,3,2,1,0:T(4,128)(2,1)S(1)} %copy.12) | data formatting | bytes 2097152 | tf_op jit(solution)/shard_map/reshape | solution.py:255
  (3 shorter events, 0.0 us)
Async XLA Ops:
  0.6 16.6 %copy-start = (s32[4,64,2]{1,2,0:T(2,128)S(1)}, s32[4,64,2]{1,2,0:T(2,128)}, u32[]{:S(2)}) copy-start(s32[4,64,2]{1,2,0:T(2,128)} %param.7) | copy-start | bytes 6148
  3.6 7.2 %copy-start.2 = (bf16[1,256,2048]{2,1,0:T(8,128)(2,1)S(1)}, bf16[1,256,2048]{2,1,0:T(8,128)(2,1)}, u32[]{:S(2)}) copy-start(bf16[1,256,2048]{2,1,0:T(8,128)(2,1)} %param.5) | copy-start | bytes 3145732
  3.6 10.0 %copy-start.1 = (bf16[1,256,2048]{2,1,0:T(8,128)(2,1)S(1)}, bf16[1,256,2048]{2,1,0:T(8,128)(2,1)}, u32[]{:S(2)}) copy-start(bf16[1,256,2048]{2,1,0:T(8,128)(2,1)} %param.4) | copy-start | bytes 3145732
  3.6 24.9 %all-to-all-start = ((bf16[16,2,2,32,256]{4,3,2,1,0:T(8,128)(2,1)}), bf16[16,2,2,32,256]{4,3,2,1,0:T(8,128)(2,1)S(1)}, u32[]{:S(2)}, u32[]{:S(2)}) async-start(bf16[16,2,2,32,256]{4,3,2,1,0:T(8,128)(2,1)} %bitcast.25), calls=%async_computation | async-start | bytes 2097152 | tf_op jit(solution)/shard_map/all_to_all | solution.py:170
  11.5 21.1 %collective-permute-start.4 = (bf16[64,2048]{1,0:T(8,128)(2,1)}, bf16[64,2048]{1,0:T(8,128)(2,1)S(1)}, u32[]{:S(2)}, u32[]{:S(2)}) collective-permute-start(bf16[64,2048]{1,0:T(8,128)(2,1)} %slice.13), channel_id=1, source_target_pairs={{4,0},{8,4},{12,8},{16,12},{20,16},{24,20},{28,24},{32,28},{36,32}... | collective-permute-start | bytes 786440 | tf_op jit(solution)/shard_map/ppermute | solution.py:174
  14.3 19.0 %collective-permute-start.3 = (bf16[64,2048]{1,0:T(8,128)(2,1)}, bf16[64,2048]{1,0:T(8,128)(2,1)}, u32[]{:S(2)}, u32[]{:S(2)}) collective-permute-start(bf16[64,2048]{1,0:T(8,128)(2,1)} %slice.12), channel_id=1, source_target_pairs={{4,0},{8,4},{12,8},{16,12},{20,16},{24,20},{28,24},{32,28},{36,32}... | collective-permute-start | bytes 786440 | tf_op jit(solution)/shard_map/ppermute | solution.py:174
  29.2 10.4 %collective-permute-start.5 = (bf16[4,2,32,256]{3,2,1,0:T(8,128)(2,1)S(1)}, bf16[4,2,32,256]{3,2,1,0:T(8,128)(2,1)S(1)}, u32[]{:S(2)}, u32[]{:S(2)}) collective-permute-start(bf16[4,2,32,256]{3,2,1,0:T(8,128)(2,1)S(1)} %get-tuple-element.32), channel_id=1, source_target_pairs={{0,64},{64,128},{128,192},{192,0},{1,65},{65,129},{129,193},{193,1... | collective-permute-start | bytes 393224 | tf_op jit(solution)/shard_map/ppermute | solution.py:159
  29.8 9.7 %collective-permute-start.6 = (bf16[4,2,32,256]{3,2,1,0:T(8,128)(2,1)S(1)}, bf16[4,2,32,256]{3,2,1,0:T(8,128)(2,1)S(1)}, u32[]{:S(2)}, u32[]{:S(2)}) collective-permute-start(bf16[4,2,32,256]{3,2,1,0:T(8,128)(2,1)S(1)} %get-tuple-element.33), channel_id=1, source_target_pairs={{0,128},{64,192},{128,0},{192,64},{1,129},{65,193},{129,1},{193,65... | collective-permute-start | bytes 393224 | tf_op jit(solution)/shard_map/ppermute | solution.py:159
  30.8 9.6 %collective-permute-start.7 = (bf16[4,2,32,256]{3,2,1,0:T(8,128)(2,1)S(1)}, bf16[4,2,32,256]{3,2,1,0:T(8,128)(2,1)S(1)}, u32[]{:S(2)}, u32[]{:S(2)}) collective-permute-start(bf16[4,2,32,256]{3,2,1,0:T(8,128)(2,1)S(1)} %get-tuple-element.34), channel_id=1, source_target_pairs={{0,192},{64,0},{128,64},{192,128},{1,193},{65,1},{129,65},{193,129... | collective-permute-start | bytes 393224 | tf_op jit(solution)/shard_map/ppermute | solution.py:159
  32.6 13.4 %collective-permute-start = (bf16[4,2,32,256]{3,2,1,0:T(8,128)(2,1)S(1)}, bf16[4,2,32,256]{3,2,1,0:T(8,128)(2,1)S(1)}, u32[]{:S(2)}, u32[]{:S(2)}) collective-permute-start(bf16[4,2,32,256]{3,2,1,0:T(8,128)(2,1)S(1)} %get-tuple-element.27), channel_id=1, source_target_pairs={{0,64},{64,128},{128,192},{192,0},{1,65},{65,129},{129,193},{193,1... | collective-permute-start | bytes 393224 | tf_op jit(solution)/shard_map/ppermute | solution.py:159
  33.3 12.8 %collective-permute-start.1 = (bf16[4,2,32,256]{3,2,1,0:T(8,128)(2,1)S(1)}, bf16[4,2,32,256]{3,2,1,0:T(8,128)(2,1)S(1)}, u32[]{:S(2)}, u32[]{:S(2)}) collective-permute-start(bf16[4,2,32,256]{3,2,1,0:T(8,128)(2,1)S(1)} %get-tuple-element.28), channel_id=1, source_target_pairs={{0,128},{64,192},{128,0},{192,64},{1,129},{65,193},{129,1},{193,65... | collective-permute-start | bytes 393224 | tf_op jit(solution)/shard_map/ppermute | solution.py:159
  39.5 6.6 %collective-permute-start.2 = (bf16[4,2,32,256]{3,2,1,0:T(8,128)(2,1)S(1)}, bf16[4,2,32,256]{3,2,1,0:T(8,128)(2,1)S(1)}, u32[]{:S(2)}, u32[]{:S(2)}) collective-permute-start(bf16[4,2,32,256]{3,2,1,0:T(8,128)(2,1)S(1)} %get-tuple-element.29), channel_id=1, source_target_pairs={{0,192},{64,0},{128,64},{192,128},{1,193},{65,1},{129,65},{193,129... | collective-permute-start | bytes 393224 | tf_op jit(solution)/shard_map/ppermute | solution.py:159
  42.8 10.3 %collective-permute-start.12 = (bf16[4,2,32,256]{3,2,1,0:T(8,128)(2,1)S(1)}, bf16[4,2,32,256]{3,2,1,0:T(8,128)(2,1)S(1)}, u32[]{:S(2)}, u32[]{:S(2)}) collective-permute-start(bf16[4,2,32,256]{3,2,1,0:T(8,128)(2,1)S(1)} %get-tuple-element.41), channel_id=1, source_target_pairs={{0,192},{64,0},{128,64},{192,128},{1,193},{65,1},{129,65},{193,129... | collective-permute-start | bytes 393224 | tf_op jit(solution)/shard_map/ppermute | solution.py:159
  45.2 7.9 %collective-permute-start.13 = (bf16[4,2,32,256]{3,2,1,0:T(8,128)(2,1)S(1)}, bf16[4,2,32,256]{3,2,1,0:T(8,128)(2,1)S(1)}, u32[]{:S(2)}, u32[]{:S(2)}) collective-permute-start(bf16[4,2,32,256]{3,2,1,0:T(8,128)(2,1)S(1)} %get-tuple-element.42), channel_id=1, source_target_pairs={{0,128},{64,192},{128,0},{192,64},{1,129},{65,193},{129,1},{193,65... | collective-permute-start | bytes 393224 | tf_op jit(solution)/shard_map/ppermute | solution.py:159
  46.1 8.6 %collective-permute-start.14 = (bf16[4,2,32,256]{3,2,1,0:T(8,128)(2,1)S(1)}, bf16[4,2,32,256]{3,2,1,0:T(8,128)(2,1)S(1)}, u32[]{:S(2)}, u32[]{:S(2)}) collective-permute-start(bf16[4,2,32,256]{3,2,1,0:T(8,128)(2,1)S(1)} %get-tuple-element.43), channel_id=1, source_target_pairs={{0,64},{64,128},{128,192},{192,0},{1,65},{65,129},{129,193},{193,1... | collective-permute-start | bytes 393224 | tf_op jit(solution)/shard_map/ppermute | solution.py:159
  48.2 7.9 %collective-permute-start.9 = (bf16[4,2,32,256]{3,2,1,0:T(8,128)(2,1)S(1)}, bf16[4,2,32,256]{3,2,1,0:T(8,128)(2,1)S(1)}, u32[]{:S(2)}, u32[]{:S(2)}) collective-permute-start(bf16[4,2,32,256]{3,2,1,0:T(8,128)(2,1)S(1)} %get-tuple-element.37), channel_id=1, source_target_pairs={{0,192},{64,0},{128,64},{192,128},{1,193},{65,1},{129,65},{193,129... | collective-permute-start | bytes 393224 | tf_op jit(solution)/shard_map/ppermute | solution.py:159
  51.6 6.5 %collective-permute-start.10 = (bf16[4,2,32,256]{3,2,1,0:T(8,128)(2,1)S(1)}, bf16[4,2,32,256]{3,2,1,0:T(8,128)(2,1)S(1)}, u32[]{:S(2)}, u32[]{:S(2)}) collective-permute-start(bf16[4,2,32,256]{3,2,1,0:T(8,128)(2,1)S(1)} %get-tuple-element.38), channel_id=1, source_target_pairs={{0,128},{64,192},{128,0},{192,64},{1,129},{65,193},{129,1},{193,65... | collective-permute-start | bytes 393224 | tf_op jit(solution)/shard_map/ppermute | solution.py:159
  53.1 6.4 %collective-permute-start.11 = (bf16[4,2,32,256]{3,2,1,0:T(8,128)(2,1)S(1)}, bf16[4,2,32,256]{3,2,1,0:T(8,128)(2,1)S(1)}, u32[]{:S(2)}, u32[]{:S(2)}) collective-permute-start(bf16[4,2,32,256]{3,2,1,0:T(8,128)(2,1)S(1)} %get-tuple-element.39), channel_id=1, source_target_pairs={{0,64},{64,128},{128,192},{192,0},{1,65},{65,129},{129,193},{193,1... | collective-permute-start | bytes 393224 | tf_op jit(solution)/shard_map/ppermute | solution.py:159
  61.0 16.7 %all-to-all-start.1 = ((bf16[16,2,2,32,256]{4,3,2,1,0:T(8,128)(2,1)}), bf16[16,2,2,32,256]{4,3,2,1,0:T(8,128)(2,1)S(1)}, u32[]{:S(2)}, u32[]{:S(2)}) async-start(bf16[16,2,2,32,256]{4,3,2,1,0:T(8,128)(2,1)} %collect.3), calls=%async_computation.1 | async-start | bytes 2097152 | tf_op jit(solution)/shard_map/all_to_all | solution.py:252
  64.8 7.7 %collective-permute-start.8 = (bf16[64,2048]{1,0:T(8,128)(2,1)S(1)}, bf16[64,2048]{1,0:T(8,128)(2,1)S(1)}, u32[]{:S(2)}, u32[]{:S(2)}) collective-permute-start(bf16[64,2048]{1,0:T(8,128)(2,1)S(1)} %slice.14), channel_id=1, source_target_pairs={{0,4},{4,8},{8,12},{12,16},{16,20},{20,24},{24,28},{28,32},{32,36}... | collective-permute-start | bytes 786440 | tf_op jit(solution)/shard_map/ppermute | solution.py:225

commit v8 on v7

--- a/solution.py
+++ b/solution.py
@@ -40,29 +40,26 @@
     return tensor * dp_size + dp, part
 
 
-def listed_places(ids_ref, blocks, owners, geometry, first, count):
-    lengths = [block.shape[0] for block in blocks[::owners]]
+def listed_places(ids_ref, blocks, spots, owners, geometry, count):
     me = ids_ref[owners * count]
-    for o, block in enumerate(blocks):
-        start = split(me + o % owners, owners)[1] * count + first + sum(lengths[: o // owners])
+    for block, (s, first) in zip(blocks, spots):
+        start = split(me + s, owners)[1] * count + first
         for k in range(block.shape[0]):
             yield block, k, place_of(ids_ref[start + k], geometry)
 
 
-def deliver_kernel(ids_ref, held_ref, *out_refs, owners, geometry, count):
-    for block, k, (source, part) in listed_places(
-        ids_ref, out_refs, owners, geometry, 0, count
-    ):
+def deliver_kernel(ids_ref, held_ref, *out_refs, **listing):
+    for block, k, (source, part) in listed_places(ids_ref, out_refs, **listing):
         for slot in range(SLOTS):
             block[k, slot] = held_ref[source, slot, part]
 
 
-def collect_kernel(ids_ref, *refs, owners, geometry, first, count):
-    held_refs, (out_ref, sem) = refs[:owners], refs[-2:]
+def collect_kernel(ids_ref, *refs, spots, **listing):
+    held_refs, (out_ref, sem) = refs[: len(spots)], refs[-2:]
     copies = [
         pltpu.make_async_copy(block.at[k], out_ref.at[source, :, part], sem.at[i])
         for i, (block, k, (source, part)) in enumerate(
-            listed_places(ids_ref, held_refs, owners, geometry, first, count)
+            listed_places(ids_ref, held_refs, spots, **listing)
         )
     ]
     for copy in copies:
@@ -179,8 +176,12 @@
         for n in chunks
         for _ in range(dp_size)
     ]
+    listing = dict(owners=dp_size, geometry=geometry, count=count)
+    spots = [
+        [(s, sum(chunks[:c]) * KNB) for s in range(dp_size)] for c in range(len(chunks))
+    ]
     delivered = pl.pallas_call(
-        functools.partial(deliver_kernel, owners=dp_size, geometry=geometry, count=count),
+        functools.partial(deliver_kernel, spots=sum(spots, []), **listing),
         out_shape=parts,
         in_specs=[smem, vmem],
         out_specs=[vmem] * len(parts),
@@ -229,25 +230,25 @@
         windows,
         jnp.concatenate([before, windows[: row_count - SPAN]], 0),
     )
+    half = dp_size // 2
+    groups = [(c, range(dp_size)) for c in reversed(range(1, len(chunks)))]
+    groups += [(0, range(half)), (0, range(half, dp_size))]
     collected = []
-    for c in reversed(range(len(chunks))):
+    for c, shifts in groups:
+        arrays = [returned[c][s] for s in shifts]
         collected = [
             pl.pallas_call(
                 functools.partial(
-                    collect_kernel,
-                    owners=dp_size,
-                    geometry=geometry,
-                    first=sum(chunks[:c]) * KNB,
-                    count=count,
+                    collect_kernel, spots=[spots[c][s] for s in shifts], **listing
                 ),
                 out_shape=jax.ShapeDtypeStruct(held.shape, jnp.bfloat16),
-                in_specs=[smem] + [vmem] * dp_size + [anywhere] * len(collected),
+                in_specs=[smem] + [vmem] * len(arrays) + [anywhere] * len(collected),
                 out_specs=anywhere,
-                scratch_shapes=[pltpu.SemaphoreType.DMA((dp_size * chunks[c] * KNB,))],
-                input_output_aliases={1 + dp_size: 0} if collected else {},
+                scratch_shapes=[pltpu.SemaphoreType.DMA((len(arrays) * chunks[c] * KNB,))],
+                input_output_aliases={1 + len(arrays): 0} if collected else {},
                 compiler_params=params,
                 name="collect",
-            )(ids, *returned[c], *collected)
+            )(ids, *arrays, *collected)
         ]
     final = lax.all_to_all(collected[0], group, 0, 0, tiled=True)
     final = final.reshape(tensor_size, dp_size, SLOTS, local_rows, rows, width)

time: 80 us -> 79.9 us (level)
  waiting for transfers between devices: 30.3 us -> 29 us
  Pallas kernels: 8.04 us -> 9.2 us
    ppermute x12, waiting for transfers between devices: 9.88 us -> 8.56 us  [ring(): lax.ppermute(array, 'dp', [(i, (i + by) % dp_size) for i in range(dp_size)])]
    pallas_call x3 -> x4, Pallas kernels: 3.59 us -> 4.75 us  [the longest x3 4.09 us: shards(): pl.pallas_call(functools.partial(collect_kernel, spots=[spots[c][s] for s...]
  transfers between devices with their start and end apart: 17 -> 17, of which waited for: 8 -> 8; matrix products, arithmetic and copies ran while one was open for 4% -> 4% of each run, Pallas kernels for 8% -> 10%
where the time goes in v8:
time: 79.9 us; the launch traced here: 79.5 us
  starting transfers between devices  32.3 us (40%)
  waiting for transfers between devices  29 us (36%)
  Pallas kernels  9.2 us (12%)
  local copies, waits for them, and re-layouts  6.76 us (8%)
  other arithmetic  1.46 us (2%)
  between operations  0.82 us (1%)
    ppermute x12, starting transfers between devices, ring(): lax.ppermute(array, 'dp', [(i, (i + by) % dp_size) for i in range(dp_size)])  14.5 us
    all_to_all x1, waiting for transfers between devices, shards(): held = lax.all_to_all(spread, group, 0, 0, tiled=True)  10.9 us
    ppermute x12, waiting for transfers between devices, ring(): lax.ppermute(array, 'dp', [(i, (i + by) % dp_size) for i in range(dp_size)])  8.56 us
    all_to_all x1, starting transfers between devices, shards(): held = lax.all_to_all(spread, group, 0, 0, tiled=True)  7.17 us
    ppermute x1, waiting for transfers between devices, shards(): before = lax.ppermute(windows[row_count - SPAN:], 'context', forth)  5.68 us
    ppermute x2, starting transfers between devices, shards(): lax.ppermute(values[:SPAN], 'context', back)  4.92 us
    pallas_call x2, Pallas kernels, shards(): pl.pallas_call(functools.partial(attention_kernel, parts=dp_size, halo=en...  4.44 us
    pallas_call x3, Pallas kernels, shards(): pl.pallas_call(functools.partial(collect_kernel, spots=[spots[c][s] for s...  4.09 us
  transfers between devices with their start and end apart: 17, of which 8 were waited for; matrix products, arithmetic and copies ran while one was open for 4% of the time, Pallas kernels for 10%

profile of v8, /device:TPU:224, one launch (start us, length us, event | category | flops | bytes accessed | tf_op | source)
XLA Modules:
  0.0 79.5 jit_solution(17664335371714854835)
XLA Ops:
  0.6 0.0 copy-start
  0.6 1.7 %reshape.132 = bf16[2,2,4,32,4,256]{5,4,0,3,2,1:T(4,128)(2,1)S(1)} reshape(bf16[2,2,128,1024]{3,0,2,1:T(2,128)(2,1)} %bitcast.27) | data formatting | bytes 2097152 | tf_op jit(solution)/shard_map/reshape | solution.py:159
  2.4 1.2 %copy.11 = bf16[2,2,4,32,4,256]{5,3,1,0,2,4:T(8,128)(2,1)} copy(bf16[2,2,4,32,4,256]{5,4,0,3,2,1:T(4,128)(2,1)S(1)} %reshape.132) | data formatting | bytes 2097152 | tf_op jit(solution)/shard_map/reshape | solution.py:159
  3.6 0.0 copy-start.2
  3.6 0.0 copy-start.1
  3.6 7.2 %all-to-all-start = ((bf16[16,2,2,32,256]{4,3,2,1,0:T(8,128)(2,1)}), bf16[16,2,2,32,256]{4,3,2,1,0:T(8,128)(2,1)S(1)}, u32[]{:S(2)}, u32[]{:S(2)}) async-start(bf16[16,2,2,32,256]{4,3,2,1,0:T(8,128)(2,1)} %bitcast.25), calls=%async_computation | async-start | bytes 2097152 | tf_op jit(solution)/shard_map/all_to_all | solution.py:167
  10.8 0.0 copy-done.2
  10.8 0.7 slice.13
  11.5 2.1 %collective-permute-start.4 = (bf16[64,2048]{1,0:T(8,128)(2,1)}, bf16[64,2048]{1,0:T(8,128)(2,1)S(1)}, u32[]{:S(2)}, u32[]{:S(2)}) collective-permute-start(bf16[64,2048]{1,0:T(8,128)(2,1)} %slice.13), channel_id=1, source_target_pairs={{4,0},{8,4},{12,8},{16,12},{20,16},{24,20},{28,24},{32,28},{36,32}... | collective-permute-start | bytes 786440 | tf_op jit(solution)/shard_map/ppermute | solution.py:171
  13.6 0.0 copy-done.1
  13.6 0.7 slice.12
  14.3 2.9 %collective-permute-start.3 = (bf16[64,2048]{1,0:T(8,128)(2,1)}, bf16[64,2048]{1,0:T(8,128)(2,1)}, u32[]{:S(2)}, u32[]{:S(2)}) collective-permute-start(bf16[64,2048]{1,0:T(8,128)(2,1)} %slice.12), channel_id=1, source_target_pairs={{4,0},{8,4},{12,8},{16,12},{20,16},{24,20},{28,24},{32,28},{36,32}... | collective-permute-start | bytes 786440 | tf_op jit(solution)/shard_map/ppermute | solution.py:171
  17.2 0.0 copy-done
  17.2 0.1 constant_dynamic-slice_fusion
  17.3 0.1 copy.12
  17.4 0.1 reshape.134
  17.5 0.1 pad_add_fusion.ids_ref
  17.6 10.9 %all-to-all-done.held_ref = bf16[16,2,2,32,256]{4,3,2,1,0:T(8,128)(2,1)S(1)} async-done(((bf16[16,2,2,32,256]{4,3,2,1,0:T(8,128)(2,1)}), bf16[16,2,2,32,256]{4,3,2,1,0:T(8,128)(2,1)S(1)}, u32[]{:S(2)}, u32[]{:S(2)}) %all-to-all-start) | async-done | bytes 1048608 | tf_op jit(solution)/shard_map/all_to_all | solution.py:167
  28.5 0.7 deliver.1
  29.2 0.6 collective-permute-start.5
  29.8 1.1 %collective-permute-start.6 = (bf16[4,2,32,256]{3,2,1,0:T(8,128)(2,1)S(1)}, bf16[4,2,32,256]{3,2,1,0:T(8,128)(2,1)S(1)}, u32[]{:S(2)}, u32[]{:S(2)}) collective-permute-start(bf16[4,2,32,256]{3,2,1,0:T(8,128)(2,1)S(1)} %get-tuple-element.33), channel_id=1, source_target_pairs={{0,128},{64,192},{128,0},{192,64},{1,129},{65,193},{129,1},{193,65... | collective-permute-start | bytes 393224 | tf_op jit(solution)/shard_map/ppermute | solution.py:156
  30.8 1.8 %collective-permute-start.7 = (bf16[4,2,32,256]{3,2,1,0:T(8,128)(2,1)S(1)}, bf16[4,2,32,256]{3,2,1,0:T(8,128)(2,1)S(1)}, u32[]{:S(2)}, u32[]{:S(2)}) collective-permute-start(bf16[4,2,32,256]{3,2,1,0:T(8,128)(2,1)S(1)} %get-tuple-element.34), channel_id=1, source_target_pairs={{0,192},{64,0},{128,64},{192,128},{1,193},{65,1},{129,65},{193,129... | collective-permute-start | bytes 393224 | tf_op jit(solution)/shard_map/ppermute | solution.py:156
  32.6 0.0 collective-permute-done.4.refs_1_
  32.6 0.7 collective-permute-start
  33.3 0.0 collective-permute-done.3.refs_0_
  33.3 2.2 %collective-permute-start.1 = (bf16[4,2,32,256]{3,2,1,0:T(8,128)(2,1)S(1)}, bf16[4,2,32,256]{3,2,1,0:T(8,128)(2,1)S(1)}, u32[]{:S(2)}, u32[]{:S(2)}) collective-permute-start(bf16[4,2,32,256]{3,2,1,0:T(8,128)(2,1)S(1)} %get-tuple-element.28), channel_id=1, source_target_pairs={{0,128},{64,192},{128,0},{192,64},{1,129},{65,193},{129,1},{193,65... | collective-permute-start | bytes 393224 | tf_op jit(solution)/shard_map/ppermute | solution.py:156
  35.5 4.0 %collective-permute-done.5.refs_3_ = bf16[4,2,32,256]{3,2,1,0:T(8,128)(2,1)S(1)} collective-permute-done((bf16[4,2,32,256]{3,2,1,0:T(8,128)(2,1)S(1)}, bf16[4,2,32,256]{3,2,1,0:T(8,128)(2,1)S(1)}, u32[]{:S(2)}, u32[]{:S(2)}) %collective-permute-start.5) | collective-permute-done | bytes 131104 | tf_op jit(solution)/shard_map/ppermute | solution.py:156
  39.5 0.0 collective-permute-start.2
  39.5 0.0 collective-permute-done.6.refs_4_
  39.5 0.9 %collective-permute-done.7.refs_5_ = bf16[4,2,32,256]{3,2,1,0:T(8,128)(2,1)S(1)} collective-permute-done((bf16[4,2,32,256]{3,2,1,0:T(8,128)(2,1)S(1)}, bf16[4,2,32,256]{3,2,1,0:T(8,128)(2,1)S(1)}, u32[]{:S(2)}, u32[]{:S(2)}) %collective-permute-start.7) | collective-permute-done | bytes 131104 | tf_op jit(solution)/shard_map/ppermute | solution.py:156
  40.4 2.4 %attention.3 = (bf16[128,2048]{1,0:T(8,128)(2,1)S(1)}, bf16[4,2,32,256]{3,2,1,0:T(8,128)(2,1)S(1)}, bf16[4,2,32,256]{3,2,1,0:T(8,128)(2,1)S(1)}, bf16[4,2,32,256...) custom-call(bf16[256,2048]{1,0:T(8,128)(2,1)S(1)} %bitcast.18, bf16[256,2048]{1,0:T(8,128)(2,1)S(1)} %bitcast.21, ...), custom_call_target="tpu_custom_call" | custom-call | tf_op jit(solution)/shard_map/attention/pallas_call | solution.py:207
  42.8 2.4 %collective-permute-start.12 = (bf16[4,2,32,256]{3,2,1,0:T(8,128)(2,1)S(1)}, bf16[4,2,32,256]{3,2,1,0:T(8,128)(2,1)S(1)}, u32[]{:S(2)}, u32[]{:S(2)}) collective-permute-start(bf16[4,2,32,256]{3,2,1,0:T(8,128)(2,1)S(1)} %get-tuple-element.41), channel_id=1, source_target_pairs={{0,192},{64,0},{128,64},{192,128},{1,193},{65,1},{129,65},{193,129... | collective-permute-start | bytes 393224 | tf_op jit(solution)/shard_map/ppermute | solution.py:156
  45.2 0.9 %collective-permute-start.13 = (bf16[4,2,32,256]{3,2,1,0:T(8,128)(2,1)S(1)}, bf16[4,2,32,256]{3,2,1,0:T(8,128)(2,1)S(1)}, u32[]{:S(2)}, u32[]{:S(2)}) collective-permute-start(bf16[4,2,32,256]{3,2,1,0:T(8,128)(2,1)S(1)} %get-tuple-element.42), channel_id=1, source_target_pairs={{0,128},{64,192},{128,0},{192,64},{1,129},{65,193},{129,1},{193,65... | collective-permute-start | bytes 393224 | tf_op jit(solution)/shard_map/ppermute | solution.py:156
  46.1 0.0 collective-permute-done.refs_1_
  46.1 0.1 collective-permute-start.14
  46.1 0.0 collective-permute-done.1.refs_2_
  46.1 0.0 collective-permute-done.2.refs_3_
  46.1 2.1 %attention.2 = (bf16[128,2048]{1,0:T(8,128)(2,1)S(1)}, bf16[4,2,32,256]{3,2,1,0:T(8,128)(2,1)S(1)}, bf16[4,2,32,256]{3,2,1,0:T(8,128)(2,1)S(1)}, bf16[4,2,32,256...) custom-call(bf16[256,2048]{1,0:T(8,128)(2,1)S(1)} %bitcast.19, bf16[256,2048]{1,0:T(8,128)(2,1)S(1)} %bitcast.22, ...), custom_call_target="tpu_custom_call" | custom-call | tf_op jit(solution)/shard_map/attention/pallas_call | solution.py:207
  48.2 3.4 %collective-permute-start.11 = (bf16[4,2,32,256]{3,2,1,0:T(8,128)(2,1)S(1)}, bf16[4,2,32,256]{3,2,1,0:T(8,128)(2,1)S(1)}, u32[]{:S(2)}, u32[]{:S(2)}) collective-permute-start(bf16[4,2,32,256]{3,2,1,0:T(8,128)(2,1)S(1)} %get-tuple-element.39), channel_id=1, source_target_pairs={{0,192},{64,0},{128,64},{192,128},{1,193},{65,1},{129,65},{193,129... | collective-permute-start | bytes 393224 | tf_op jit(solution)/shard_map/ppermute | solution.py:156
  51.6 1.4 %collective-permute-start.9 = (bf16[4,2,32,256]{3,2,1,0:T(8,128)(2,1)S(1)}, bf16[4,2,32,256]{3,2,1,0:T(8,128)(2,1)S(1)}, u32[]{:S(2)}, u32[]{:S(2)}) collective-permute-start(bf16[4,2,32,256]{3,2,1,0:T(8,128)(2,1)S(1)} %get-tuple-element.36), channel_id=1, source_target_pairs={{0,128},{64,192},{128,0},{192,64},{1,129},{65,193},{129,1},{193,65... | collective-permute-start | bytes 393224 | tf_op jit(solution)/shard_map/ppermute | solution.py:156
  53.1 0.0 collective-permute-done.12.refs_1_
  53.1 0.0 collective-permute-start.10
  53.1 0.0 collective-permute-done.13.refs_2_
  53.1 1.5 %collective-permute-done.14.refs_3_ = bf16[4,2,32,256]{3,2,1,0:T(8,128)(2,1)S(1)} collective-permute-done((bf16[4,2,32,256]{3,2,1,0:T(8,128)(2,1)S(1)}, bf16[4,2,32,256]{3,2,1,0:T(8,128)(2,1)S(1)}, u32[]{:S(2)}, u32[]{:S(2)}) %collective-permute-start.14) | collective-permute-done | bytes 131104 | tf_op jit(solution)/shard_map/ppermute | solution.py:156
  54.6 1.5 %collect.3.refs_2_ = bf16[16,2,2,32,256]{4,3,2,1,0:T(8,128)(2,1)} custom-call(s32[33]{0:T(128)S(1)} %pad_add_fusion.ids_ref, bf16[4,2,32,256]{3,2,1,0:T(8,128)(2,1)S(1)} %get-tuple-element.40.refs_0_, bf16[4,2,32,256]{3,2,1,0:T(8,128)(2,1)S(1)} %collective-permute-done.12.refs_1_, bf16[4,2,32,256]{3,2,1,0:T(8,128)(2,1)S(1)} %collective-permute-done.13.refs_2_, ...), custom_call_target="tpu_custom_call" | custom-call | tf_op jit(solution)/shard_map/collect/pallas_call | solution.py:240
  56.1 0.0 collective-permute-done.11.refs_1_
  56.1 1.3 %collect.4.refs_2_ = bf16[16,2,2,32,256]{4,3,2,1,0:T(8,128)(2,1)} custom-call(s32[33]{0:T(128)S(1)} %pad_add_fusion.ids_ref, bf16[4,2,32,256]{3,2,1,0:T(8,128)(2,1)S(1)} %get-tuple-element.38.refs_0_, bf16[4,2,32,256]{3,2,1,0:T(8,128)(2,1)S(1)} %collective-permute-done.11.refs_1_, ...), custom_call_target="tpu_custom_call", output_to_operand_aliasing={{}: (3, {})} | custom-call | tf_op jit(solution)/shard_map/collect/pallas_call | solution.py:240
  57.4 0.7 collective-permute-done.9.refs_0_
  58.1 1.4 %collective-permute-done.10.refs_1_ = bf16[4,2,32,256]{3,2,1,0:T(8,128)(2,1)S(1)} collective-permute-done((bf16[4,2,32,256]{3,2,1,0:T(8,128)(2,1)S(1)}, bf16[4,2,32,256]{3,2,1,0:T(8,128)(2,1)S(1)}, u32[]{:S(2)}, u32[]{:S(2)}) %collective-permute-start.10) | collective-permute-done | bytes 131104 | tf_op jit(solution)/shard_map/ppermute | solution.py:156
  59.5 1.3 %collect.5 = bf16[16,2,2,32,256]{4,3,2,1,0:T(8,128)(2,1)} custom-call(s32[33]{0:T(128)S(1)} %pad_add_fusion.ids_ref, bf16[4,2,32,256]{3,2,1,0:T(8,128)(2,1)S(1)} %collective-permute-done.9.refs_0_, bf16[4,2,32,256]{3,2,1,0:T(8,128)(2,1)S(1)} %collective-permute-done.10.refs_1_, ...), custom_call_target="tpu_custom_call", output_to_operand_aliasing={{}: (3, {})} | custom-call | tf_op jit(solution)/shard_map/collect/pallas_call | solution.py:240
  60.8 3.7 %all-to-all-start.1 = ((bf16[16,2,2,32,256]{4,3,2,1,0:T(8,128)(2,1)}), bf16[16,2,2,32,256]{4,3,2,1,0:T(8,128)(2,1)S(1)}, u32[]{:S(2)}, u32[]{:S(2)}) async-start(bf16[16,2,2,32,256]{4,3,2,1,0:T(8,128)(2,1)} %collect.5), calls=%async_computation.1 | async-start | bytes 2097152 | tf_op jit(solution)/shard_map/all_to_all | solution.py:253
  64.6 1.9 %collective-permute-start.8 = (bf16[64,2048]{1,0:T(8,128)(2,1)S(1)}, bf16[64,2048]{1,0:T(8,128)(2,1)S(1)}, u32[]{:S(2)}, u32[]{:S(2)}) collective-permute-start(bf16[64,2048]{1,0:T(8,128)(2,1)S(1)} %slice.14), channel_id=1, source_target_pairs={{0,4},{4,8},{8,12},{12,16},{16,20},{20,24},{24,28},{28,32},{32,36}... | collective-permute-start | bytes 786440 | tf_op jit(solution)/shard_map/ppermute | solution.py:226
  66.6 0.1 fusion.1
  66.6 5.7 %collective-permute-done.8 = bf16[64,2048]{1,0:T(8,128)(2,1)S(1)} collective-permute-done((bf16[64,2048]{1,0:T(8,128)(2,1)S(1)}, bf16[64,2048]{1,0:T(8,128)(2,1)S(1)}, u32[]{:S(2)}, u32[]{:S(2)}) %collective-permute-start.8) | collective-permute-done | bytes 262176 | tf_op jit(solution)/shard_map/ppermute | solution.py:226
  72.3 1.3 %fusion = bf16[1,256,2048]{2,1,0:T(8,128)(2,1)} fusion(bf16[1,128,2048]{2,1,0:T(8,128)(2,1)S(1)} %bitcast.23, bf16[1,128,2048]{2,1,0:T(8,128)(2,1)S(1)} %bitcast.24, bf16[1,192,2048]{2,1,0:T(8,128)(2,1)S(1)} %fusion.1, bf16[1,64,2048]{2,1,0:T(8,128)(2,1)S(1)} %bitcast.28, s32[256]{0:T(256)S(1)} %get-tuple-element.44, s32[256]{0:T(256)S(1)} %get-tuple-element.45, ...), kind=kLoop, calls=%fused_computation.1 | loop fusion | flops 5767168 | bytes 3148032 | tf_op jit(solution)/shard_map/jit(_where)/select_n | solution.py:228
  73.6 3.9 %all-to-all-done.1 = bf16[16,2,2,32,256]{4,3,2,1,0:T(8,128)(2,1)S(1)} async-done(((bf16[16,2,2,32,256]{4,3,2,1,0:T(8,128)(2,1)}), bf16[16,2,2,32,256]{4,3,2,1,0:T(8,128)(2,1)S(1)}, u32[]{:S(2)}, u32[]{:S(2)}) %all-to-all-start.1) | async-done | bytes 1048608 | tf_op jit(solution)/shard_map/all_to_all | solution.py:253
  77.5 0.8 %copy.13 = bf16[2,4,32,2,4,256]{5,4,3,2,1,0:T(4,128)(2,1)S(1)} copy(bf16[2,4,32,2,4,256]{5,2,0,3,1,4:T(8,128)(2,1)S(1)} %bitcast.26) | data formatting | bytes 2097152 | tf_op jit(solution)/shard_map/transpose | solution.py:255
  78.3 1.2 %reshape.136 = bf16[2,128,2,1024]{3,2,1,0:T(2,128)(2,1)} reshape(bf16[2,4,32,2,4,256]{5,4,3,2,1,0:T(4,128)(2,1)S(1)} %copy.13) | data formatting | bytes 2097152 | tf_op jit(solution)/shard_map/reshape | solution.py:256
  (3 shorter events, 0.0 us)
Async XLA Ops:
  0.6 16.6 %copy-start = (s32[4,64,2]{1,2,0:T(2,128)S(1)}, s32[4,64,2]{1,2,0:T(2,128)}, u32[]{:S(2)}) copy-start(s32[4,64,2]{1,2,0:T(2,128)} %param.7) | copy-start | bytes 6148
  3.6 7.2 %copy-start.2 = (bf16[1,256,2048]{2,1,0:T(8,128)(2,1)S(1)}, bf16[1,256,2048]{2,1,0:T(8,128)(2,1)}, u32[]{:S(2)}) copy-start(bf16[1,256,2048]{2,1,0:T(8,128)(2,1)} %param.5) | copy-start | bytes 3145732
  3.6 10.0 %copy-start.1 = (bf16[1,256,2048]{2,1,0:T(8,128)(2,1)S(1)}, bf16[1,256,2048]{2,1,0:T(8,128)(2,1)}, u32[]{:S(2)}) copy-start(bf16[1,256,2048]{2,1,0:T(8,128)(2,1)} %param.4) | copy-start | bytes 3145732
  3.6 24.9 %all-to-all-start = ((bf16[16,2,2,32,256]{4,3,2,1,0:T(8,128)(2,1)}), bf16[16,2,2,32,256]{4,3,2,1,0:T(8,128)(2,1)S(1)}, u32[]{:S(2)}, u32[]{:S(2)}) async-start(bf16[16,2,2,32,256]{4,3,2,1,0:T(8,128)(2,1)} %bitcast.25), calls=%async_computation | async-start | bytes 2097152 | tf_op jit(solution)/shard_map/all_to_all | solution.py:167
  11.5 21.1 %collective-permute-start.4 = (bf16[64,2048]{1,0:T(8,128)(2,1)}, bf16[64,2048]{1,0:T(8,128)(2,1)S(1)}, u32[]{:S(2)}, u32[]{:S(2)}) collective-permute-start(bf16[64,2048]{1,0:T(8,128)(2,1)} %slice.13), channel_id=1, source_target_pairs={{4,0},{8,4},{12,8},{16,12},{20,16},{24,20},{28,24},{32,28},{36,32}... | collective-permute-start | bytes 786440 | tf_op jit(solution)/shard_map/ppermute | solution.py:171
  14.3 19.0 %collective-permute-start.3 = (bf16[64,2048]{1,0:T(8,128)(2,1)}, bf16[64,2048]{1,0:T(8,128)(2,1)}, u32[]{:S(2)}, u32[]{:S(2)}) collective-permute-start(bf16[64,2048]{1,0:T(8,128)(2,1)} %slice.12), channel_id=1, source_target_pairs={{4,0},{8,4},{12,8},{16,12},{20,16},{24,20},{28,24},{32,28},{36,32}... | collective-permute-start | bytes 786440 | tf_op jit(solution)/shard_map/ppermute | solution.py:171
  29.2 10.4 %collective-permute-start.5 = (bf16[4,2,32,256]{3,2,1,0:T(8,128)(2,1)S(1)}, bf16[4,2,32,256]{3,2,1,0:T(8,128)(2,1)S(1)}, u32[]{:S(2)}, u32[]{:S(2)}) collective-permute-start(bf16[4,2,32,256]{3,2,1,0:T(8,128)(2,1)S(1)} %get-tuple-element.32), channel_id=1, source_target_pairs={{0,64},{64,128},{128,192},{192,0},{1,65},{65,129},{129,193},{193,1... | collective-permute-start | bytes 393224 | tf_op jit(solution)/shard_map/ppermute | solution.py:156
  29.8 9.7 %collective-permute-start.6 = (bf16[4,2,32,256]{3,2,1,0:T(8,128)(2,1)S(1)}, bf16[4,2,32,256]{3,2,1,0:T(8,128)(2,1)S(1)}, u32[]{:S(2)}, u32[]{:S(2)}) collective-permute-start(bf16[4,2,32,256]{3,2,1,0:T(8,128)(2,1)S(1)} %get-tuple-element.33), channel_id=1, source_target_pairs={{0,128},{64,192},{128,0},{192,64},{1,129},{65,193},{129,1},{193,65... | collective-permute-start | bytes 393224 | tf_op jit(solution)/shard_map/ppermute | solution.py:156
  30.8 9.6 %collective-permute-start.7 = (bf16[4,2,32,256]{3,2,1,0:T(8,128)(2,1)S(1)}, bf16[4,2,32,256]{3,2,1,0:T(8,128)(2,1)S(1)}, u32[]{:S(2)}, u32[]{:S(2)}) collective-permute-start(bf16[4,2,32,256]{3,2,1,0:T(8,128)(2,1)S(1)} %get-tuple-element.34), channel_id=1, source_target_pairs={{0,192},{64,0},{128,64},{192,128},{1,193},{65,1},{129,65},{193,129... | collective-permute-start | bytes 393224 | tf_op jit(solution)/shard_map/ppermute | solution.py:156
  32.6 13.4 %collective-permute-start = (bf16[4,2,32,256]{3,2,1,0:T(8,128)(2,1)S(1)}, bf16[4,2,32,256]{3,2,1,0:T(8,128)(2,1)S(1)}, u32[]{:S(2)}, u32[]{:S(2)}) collective-permute-start(bf16[4,2,32,256]{3,2,1,0:T(8,128)(2,1)S(1)} %get-tuple-element.27), channel_id=1, source_target_pairs={{0,64},{64,128},{128,192},{192,0},{1,65},{65,129},{129,193},{193,1... | collective-permute-start | bytes 393224 | tf_op jit(solution)/shard_map/ppermute | solution.py:156
  33.3 12.8 %collective-permute-start.1 = (bf16[4,2,32,256]{3,2,1,0:T(8,128)(2,1)S(1)}, bf16[4,2,32,256]{3,2,1,0:T(8,128)(2,1)S(1)}, u32[]{:S(2)}, u32[]{:S(2)}) collective-permute-start(bf16[4,2,32,256]{3,2,1,0:T(8,128)(2,1)S(1)} %get-tuple-element.28), channel_id=1, source_target_pairs={{0,128},{64,192},{128,0},{192,64},{1,129},{65,193},{129,1},{193,65... | collective-permute-start | bytes 393224 | tf_op jit(solution)/shard_map/ppermute | solution.py:156
  39.5 6.6 %collective-permute-start.2 = (bf16[4,2,32,256]{3,2,1,0:T(8,128)(2,1)S(1)}, bf16[4,2,32,256]{3,2,1,0:T(8,128)(2,1)S(1)}, u32[]{:S(2)}, u32[]{:S(2)}) collective-permute-start(bf16[4,2,32,256]{3,2,1,0:T(8,128)(2,1)S(1)} %get-tuple-element.29), channel_id=1, source_target_pairs={{0,192},{64,0},{128,64},{192,128},{1,193},{65,1},{129,65},{193,129... | collective-permute-start | bytes 393224 | tf_op jit(solution)/shard_map/ppermute | solution.py:156
  42.8 10.3 %collective-permute-start.12 = (bf16[4,2,32,256]{3,2,1,0:T(8,128)(2,1)S(1)}, bf16[4,2,32,256]{3,2,1,0:T(8,128)(2,1)S(1)}, u32[]{:S(2)}, u32[]{:S(2)}) collective-permute-start(bf16[4,2,32,256]{3,2,1,0:T(8,128)(2,1)S(1)} %get-tuple-element.41), channel_id=1, source_target_pairs={{0,192},{64,0},{128,64},{192,128},{1,193},{65,1},{129,65},{193,129... | collective-permute-start | bytes 393224 | tf_op jit(solution)/shard_map/ppermute | solution.py:156
  45.2 7.9 %collective-permute-start.13 = (bf16[4,2,32,256]{3,2,1,0:T(8,128)(2,1)S(1)}, bf16[4,2,32,256]{3,2,1,0:T(8,128)(2,1)S(1)}, u32[]{:S(2)}, u32[]{:S(2)}) collective-permute-start(bf16[4,2,32,256]{3,2,1,0:T(8,128)(2,1)S(1)} %get-tuple-element.42), channel_id=1, source_target_pairs={{0,128},{64,192},{128,0},{192,64},{1,129},{65,193},{129,1},{193,65... | collective-permute-start | bytes 393224 | tf_op jit(solution)/shard_map/ppermute | solution.py:156
  46.1 8.6 %collective-permute-start.14 = (bf16[4,2,32,256]{3,2,1,0:T(8,128)(2,1)S(1)}, bf16[4,2,32,256]{3,2,1,0:T(8,128)(2,1)S(1)}, u32[]{:S(2)}, u32[]{:S(2)}) collective-permute-start(bf16[4,2,32,256]{3,2,1,0:T(8,128)(2,1)S(1)} %get-tuple-element.43), channel_id=1, source_target_pairs={{0,64},{64,128},{128,192},{192,0},{1,65},{65,129},{129,193},{193,1... | collective-permute-start | bytes 393224 | tf_op jit(solution)/shard_map/ppermute | solution.py:156
  48.2 7.9 %collective-permute-start.11 = (bf16[4,2,32,256]{3,2,1,0:T(8,128)(2,1)S(1)}, bf16[4,2,32,256]{3,2,1,0:T(8,128)(2,1)S(1)}, u32[]{:S(2)}, u32[]{:S(2)}) collective-permute-start(bf16[4,2,32,256]{3,2,1,0:T(8,128)(2,1)S(1)} %get-tuple-element.39), channel_id=1, source_target_pairs={{0,192},{64,0},{128,64},{192,128},{1,193},{65,1},{129,65},{193,129... | collective-permute-start | bytes 393224 | tf_op jit(solution)/shard_map/ppermute | solution.py:156
  51.6 6.5 %collective-permute-start.9 = (bf16[4,2,32,256]{3,2,1,0:T(8,128)(2,1)S(1)}, bf16[4,2,32,256]{3,2,1,0:T(8,128)(2,1)S(1)}, u32[]{:S(2)}, u32[]{:S(2)}) collective-permute-start(bf16[4,2,32,256]{3,2,1,0:T(8,128)(2,1)S(1)} %get-tuple-element.36), channel_id=1, source_target_pairs={{0,128},{64,192},{128,0},{192,64},{1,129},{65,193},{129,1},{193,65... | collective-permute-start | bytes 393224 | tf_op jit(solution)/shard_map/ppermute | solution.py:156
  53.1 6.4 %collective-permute-start.10 = (bf16[4,2,32,256]{3,2,1,0:T(8,128)(2,1)S(1)}, bf16[4,2,32,256]{3,2,1,0:T(8,128)(2,1)S(1)}, u32[]{:S(2)}, u32[]{:S(2)}) collective-permute-start(bf16[4,2,32,256]{3,2,1,0:T(8,128)(2,1)S(1)} %get-tuple-element.37), channel_id=1, source_target_pairs={{0,64},{64,128},{128,192},{192,0},{1,65},{65,129},{129,193},{193,1... | collective-permute-start | bytes 393224 | tf_op jit(solution)/shard_map/ppermute | solution.py:156
  60.8 16.7 %all-to-all-start.1 = ((bf16[16,2,2,32,256]{4,3,2,1,0:T(8,128)(2,1)}), bf16[16,2,2,32,256]{4,3,2,1,0:T(8,128)(2,1)S(1)}, u32[]{:S(2)}, u32[]{:S(2)}) async-start(bf16[16,2,2,32,256]{4,3,2,1,0:T(8,128)(2,1)} %collect.5), calls=%async_computation.1 | async-start | bytes 2097152 | tf_op jit(solution)/shard_map/all_to_all | solution.py:253
  64.6 7.7 %collective-permute-start.8 = (bf16[64,2048]{1,0:T(8,128)(2,1)S(1)}, bf16[64,2048]{1,0:T(8,128)(2,1)S(1)}, u32[]{:S(2)}, u32[]{:S(2)}) collective-permute-start(bf16[64,2048]{1,0:T(8,128)(2,1)S(1)} %slice.14), channel_id=1, source_target_pairs={{0,4},{4,8},{8,12},{12,16},{16,20},{20,24},{24,28},{28,32},{32,36}... | collective-permute-start | bytes 786440 | tf_op jit(solution)/shard_map/ppermute | solution.py:226

commit v9 on v8

--- a/solution.py
+++ b/solution.py
@@ -51,13 +51,13 @@
 def deliver_kernel(ids_ref, held_ref, *out_refs, **listing):
     for block, k, (source, part) in listed_places(ids_ref, out_refs, **listing):
         for slot in range(SLOTS):
-            block[k, slot] = held_ref[source, slot, part]
+            block[k, slot] = held_ref[source, part, slot]
 
 
 def collect_kernel(ids_ref, *refs, spots, **listing):
     held_refs, (out_ref, sem) = refs[: len(spots)], refs[-2:]
     copies = [
-        pltpu.make_async_copy(block.at[k], out_ref.at[source, :, part], sem.at[i])
+        pltpu.make_async_copy(block.at[k], out_ref.at[source, part], sem.at[i])
         for i, (block, k, (source, part)) in enumerate(
             listed_places(ids_ref, held_refs, spots, **listing)
         )
@@ -157,7 +157,7 @@
 
     spread = neighbour_kv.transpose(2, 0, 1, 3)
     spread = spread.reshape(SLOTS, local_rows, dp_size, rows, tensor_size, width)
-    spread = spread.transpose(4, 2, 0, 1, 3, 5).reshape(peers, SLOTS, local_rows, rows, width)
+    spread = spread.transpose(4, 2, 1, 0, 3, 5).reshape(peers, local_rows, SLOTS, rows, width)
     ids = lax.dynamic_slice_in_dim(
         span_neighbours, lax.axis_index("context") * spans, spans, 1
     ).reshape(-1)
@@ -251,8 +251,8 @@
             )(ids, *arrays, *collected)
         ]
     final = lax.all_to_all(collected[0], group, 0, 0, tiled=True)
-    final = final.reshape(tensor_size, dp_size, SLOTS, local_rows, rows, width)
-    final = final.transpose(3, 1, 4, 2, 0, 5)
+    final = final.reshape(tensor_size, dp_size, local_rows, SLOTS, rows, width)
+    final = final.transpose(2, 1, 4, 3, 0, 5)
     return (cross_out[None], final.reshape(neighbour_kv.shape))
 
 

time: 79.9 us -> 79.9 us (level)
  no operation moved by 1% of the time
where the time goes in v9:
time: 79.9 us; the launch traced here: 79.5 us
  starting transfers between devices  32.3 us (40%)
  waiting for transfers between devices  29 us (36%)
  Pallas kernels  9.19 us (12%)
  local copies, waits for them, and re-layouts  6.76 us (8%)
  other arithmetic  1.46 us (2%)
  between operations  0.82 us (1%)
    ppermute x12, starting transfers between devices, ring(): lax.ppermute(array, 'dp', [(i, (i + by) % dp_size) for i in range(dp_size)])  14.5 us
    all_to_all x1, waiting for transfers between devices, shards(): held = lax.all_to_all(spread, group, 0, 0, tiled=True)  10.9 us
    ppermute x12, waiting for transfers between devices, ring(): lax.ppermute(array, 'dp', [(i, (i + by) % dp_size) for i in range(dp_size)])  8.56 us
    all_to_all x1, starting transfers between devices, shards(): held = lax.all_to_all(spread, group, 0, 0, tiled=True)  7.17 us
    ppermute x1, waiting for transfers between devices, shards(): before = lax.ppermute(windows[row_count - SPAN:], 'context', forth)  5.68 us
    ppermute x2, starting transfers between devices, shards(): lax.ppermute(values[:SPAN], 'context', back)  4.92 us
    pallas_call x2, Pallas kernels, shards(): pl.pallas_call(functools.partial(attention_kernel, parts=dp_size, halo=en...  4.44 us
    pallas_call x3, Pallas kernels, shards(): pl.pallas_call(functools.partial(collect_kernel, spots=[spots[c][s] for s...  4.09 us
  transfers between devices with their start and end apart: 17, of which 8 were waited for; matrix products, arithmetic and copies ran while one was open for 4% of the time, Pallas kernels for 10%

profile of v9, /device:TPU:224, one launch (start us, length us, event | category | flops | bytes accessed | tf_op | source)
XLA Modules:
  0.0 79.5 jit_solution(1023555963230180770)
XLA Ops:
  0.6 0.0 copy-start
  0.6 1.7 %reshape.132 = bf16[2,2,4,32,4,256]{5,4,0,3,2,1:T(4,128)(2,1)S(1)} reshape(bf16[2,2,128,1024]{3,0,2,1:T(2,128)(2,1)} %bitcast.27) | data formatting | bytes 2097152 | tf_op jit(solution)/shard_map/reshape | solution.py:159
  2.4 1.2 %copy.11 = bf16[2,2,4,32,4,256]{5,3,0,1,2,4:T(8,128)(2,1)} copy(bf16[2,2,4,32,4,256]{5,4,0,3,2,1:T(4,128)(2,1)S(1)} %reshape.132) | data formatting | bytes 2097152 | tf_op jit(solution)/shard_map/reshape | solution.py:159
  3.6 0.0 copy-start.2
  3.6 0.0 copy-start.1
  3.6 7.2 %all-to-all-start = ((bf16[16,2,2,32,256]{4,3,2,1,0:T(8,128)(2,1)}), bf16[16,2,2,32,256]{4,3,2,1,0:T(8,128)(2,1)S(1)}, u32[]{:S(2)}, u32[]{:S(2)}) async-start(bf16[16,2,2,32,256]{4,3,2,1,0:T(8,128)(2,1)} %bitcast.25), calls=%async_computation | async-start | bytes 2097152 | tf_op jit(solution)/shard_map/all_to_all | solution.py:167
  10.8 0.0 copy-done.2
  10.8 0.7 slice.13
  11.5 2.1 %collective-permute-start.4 = (bf16[64,2048]{1,0:T(8,128)(2,1)}, bf16[64,2048]{1,0:T(8,128)(2,1)S(1)}, u32[]{:S(2)}, u32[]{:S(2)}) collective-permute-start(bf16[64,2048]{1,0:T(8,128)(2,1)} %slice.13), channel_id=1, source_target_pairs={{4,0},{8,4},{12,8},{16,12},{20,16},{24,20},{28,24},{32,28},{36,32}... | collective-permute-start | bytes 786440 | tf_op jit(solution)/shard_map/ppermute | solution.py:171
  13.6 0.0 copy-done.1
  13.6 0.7 slice.12
  14.3 2.9 %collective-permute-start.3 = (bf16[64,2048]{1,0:T(8,128)(2,1)}, bf16[64,2048]{1,0:T(8,128)(2,1)}, u32[]{:S(2)}, u32[]{:S(2)}) collective-permute-start(bf16[64,2048]{1,0:T(8,128)(2,1)} %slice.12), channel_id=1, source_target_pairs={{4,0},{8,4},{12,8},{16,12},{20,16},{24,20},{28,24},{32,28},{36,32}... | collective-permute-start | bytes 786440 | tf_op jit(solution)/shard_map/ppermute | solution.py:171
  17.2 0.0 copy-done
  17.2 0.1 constant_dynamic-slice_fusion
  17.3 0.1 copy.12
  17.4 0.1 reshape.134
  17.5 0.1 pad_add_fusion.ids_ref
  17.6 10.9 %all-to-all-done.held_ref = bf16[16,2,2,32,256]{4,3,2,1,0:T(8,128)(2,1)S(1)} async-done(((bf16[16,2,2,32,256]{4,3,2,1,0:T(8,128)(2,1)}), bf16[16,2,2,32,256]{4,3,2,1,0:T(8,128)(2,1)S(1)}, u32[]{:S(2)}, u32[]{:S(2)}) %all-to-all-start) | async-done | bytes 1048608 | tf_op jit(solution)/shard_map/all_to_all | solution.py:167
  28.5 0.7 deliver.1
  29.2 0.6 collective-permute-start.5
  29.8 1.1 %collective-permute-start.6 = (bf16[4,2,32,256]{3,2,1,0:T(8,128)(2,1)S(1)}, bf16[4,2,32,256]{3,2,1,0:T(8,128)(2,1)S(1)}, u32[]{:S(2)}, u32[]{:S(2)}) collective-permute-start(bf16[4,2,32,256]{3,2,1,0:T(8,128)(2,1)S(1)} %get-tuple-element.33), channel_id=1, source_target_pairs={{0,128},{64,192},{128,0},{192,64},{1,129},{65,193},{129,1},{193,65... | collective-permute-start | bytes 393224 | tf_op jit(solution)/shard_map/ppermute | solution.py:156
  30.9 1.8 %collective-permute-start.7 = (bf16[4,2,32,256]{3,2,1,0:T(8,128)(2,1)S(1)}, bf16[4,2,32,256]{3,2,1,0:T(8,128)(2,1)S(1)}, u32[]{:S(2)}, u32[]{:S(2)}) collective-permute-start(bf16[4,2,32,256]{3,2,1,0:T(8,128)(2,1)S(1)} %get-tuple-element.34), channel_id=1, source_target_pairs={{0,192},{64,0},{128,64},{192,128},{1,193},{65,1},{129,65},{193,129... | collective-permute-start | bytes 393224 | tf_op jit(solution)/shard_map/ppermute | solution.py:156
  32.6 0.0 collective-permute-done.4.refs_1_
  32.6 0.7 collective-permute-start
  33.3 0.0 collective-permute-done.3.refs_0_
  33.3 2.2 %collective-permute-start.1 = (bf16[4,2,32,256]{3,2,1,0:T(8,128)(2,1)S(1)}, bf16[4,2,32,256]{3,2,1,0:T(8,128)(2,1)S(1)}, u32[]{:S(2)}, u32[]{:S(2)}) collective-permute-start(bf16[4,2,32,256]{3,2,1,0:T(8,128)(2,1)S(1)} %get-tuple-element.28), channel_id=1, source_target_pairs={{0,128},{64,192},{128,0},{192,64},{1,129},{65,193},{129,1},{193,65... | collective-permute-start | bytes 393224 | tf_op jit(solution)/shard_map/ppermute | solution.py:156
  35.5 4.0 %collective-permute-done.5.refs_3_ = bf16[4,2,32,256]{3,2,1,0:T(8,128)(2,1)S(1)} collective-permute-done((bf16[4,2,32,256]{3,2,1,0:T(8,128)(2,1)S(1)}, bf16[4,2,32,256]{3,2,1,0:T(8,128)(2,1)S(1)}, u32[]{:S(2)}, u32[]{:S(2)}) %collective-permute-start.5) | collective-permute-done | bytes 131104 | tf_op jit(solution)/shard_map/ppermute | solution.py:156
  39.5 0.0 collective-permute-start.2
  39.5 0.0 collective-permute-done.6.refs_4_
  39.5 0.9 %collective-permute-done.7.refs_5_ = bf16[4,2,32,256]{3,2,1,0:T(8,128)(2,1)S(1)} collective-permute-done((bf16[4,2,32,256]{3,2,1,0:T(8,128)(2,1)S(1)}, bf16[4,2,32,256]{3,2,1,0:T(8,128)(2,1)S(1)}, u32[]{:S(2)}, u32[]{:S(2)}) %collective-permute-start.7) | collective-permute-done | bytes 131104 | tf_op jit(solution)/shard_map/ppermute | solution.py:156
  40.4 2.4 %attention.3 = (bf16[128,2048]{1,0:T(8,128)(2,1)S(1)}, bf16[4,2,32,256]{3,2,1,0:T(8,128)(2,1)S(1)}, bf16[4,2,32,256]{3,2,1,0:T(8,128)(2,1)S(1)}, bf16[4,2,32,256...) custom-call(bf16[256,2048]{1,0:T(8,128)(2,1)S(1)} %bitcast.18, bf16[256,2048]{1,0:T(8,128)(2,1)S(1)} %bitcast.21, ...), custom_call_target="tpu_custom_call" | custom-call | tf_op jit(solution)/shard_map/attention/pallas_call | solution.py:207
  42.8 2.4 %collective-permute-start.12 = (bf16[4,2,32,256]{3,2,1,0:T(8,128)(2,1)S(1)}, bf16[4,2,32,256]{3,2,1,0:T(8,128)(2,1)S(1)}, u32[]{:S(2)}, u32[]{:S(2)}) collective-permute-start(bf16[4,2,32,256]{3,2,1,0:T(8,128)(2,1)S(1)} %get-tuple-element.41), channel_id=1, source_target_pairs={{0,192},{64,0},{128,64},{192,128},{1,193},{65,1},{129,65},{193,129... | collective-permute-start | bytes 393224 | tf_op jit(solution)/shard_map/ppermute | solution.py:156
  45.2 0.9 %collective-permute-start.13 = (bf16[4,2,32,256]{3,2,1,0:T(8,128)(2,1)S(1)}, bf16[4,2,32,256]{3,2,1,0:T(8,128)(2,1)S(1)}, u32[]{:S(2)}, u32[]{:S(2)}) collective-permute-start(bf16[4,2,32,256]{3,2,1,0:T(8,128)(2,1)S(1)} %get-tuple-element.42), channel_id=1, source_target_pairs={{0,128},{64,192},{128,0},{192,64},{1,129},{65,193},{129,1},{193,65... | collective-permute-start | bytes 393224 | tf_op jit(solution)/shard_map/ppermute | solution.py:156
  46.1 0.0 collective-permute-done.refs_1_
  46.1 0.1 collective-permute-start.14
  46.1 0.0 collective-permute-done.1.refs_2_
  46.1 0.0 collective-permute-done.2.refs_3_
  46.1 2.1 %attention.2 = (bf16[128,2048]{1,0:T(8,128)(2,1)S(1)}, bf16[4,2,32,256]{3,2,1,0:T(8,128)(2,1)S(1)}, bf16[4,2,32,256]{3,2,1,0:T(8,128)(2,1)S(1)}, bf16[4,2,32,256...) custom-call(bf16[256,2048]{1,0:T(8,128)(2,1)S(1)} %bitcast.19, bf16[256,2048]{1,0:T(8,128)(2,1)S(1)} %bitcast.22, ...), custom_call_target="tpu_custom_call" | custom-call | tf_op jit(solution)/shard_map/attention/pallas_call | solution.py:207
  48.2 3.4 %collective-permute-start.11 = (bf16[4,2,32,256]{3,2,1,0:T(8,128)(2,1)S(1)}, bf16[4,2,32,256]{3,2,1,0:T(8,128)(2,1)S(1)}, u32[]{:S(2)}, u32[]{:S(2)}) collective-permute-start(bf16[4,2,32,256]{3,2,1,0:T(8,128)(2,1)S(1)} %get-tuple-element.39), channel_id=1, source_target_pairs={{0,192},{64,0},{128,64},{192,128},{1,193},{65,1},{129,65},{193,129... | collective-permute-start | bytes 393224 | tf_op jit(solution)/shard_map/ppermute | solution.py:156
  51.6 1.4 %collective-permute-start.9 = (bf16[4,2,32,256]{3,2,1,0:T(8,128)(2,1)S(1)}, bf16[4,2,32,256]{3,2,1,0:T(8,128)(2,1)S(1)}, u32[]{:S(2)}, u32[]{:S(2)}) collective-permute-start(bf16[4,2,32,256]{3,2,1,0:T(8,128)(2,1)S(1)} %get-tuple-element.36), channel_id=1, source_target_pairs={{0,128},{64,192},{128,0},{192,64},{1,129},{65,193},{129,1},{193,65... | collective-permute-start | bytes 393224 | tf_op jit(solution)/shard_map/ppermute | solution.py:156
  53.1 0.0 collective-permute-done.12.refs_1_
  53.1 0.0 collective-permute-start.10
  53.1 0.0 collective-permute-done.13.refs_2_
  53.1 1.5 %collective-permute-done.14.refs_3_ = bf16[4,2,32,256]{3,2,1,0:T(8,128)(2,1)S(1)} collective-permute-done((bf16[4,2,32,256]{3,2,1,0:T(8,128)(2,1)S(1)}, bf16[4,2,32,256]{3,2,1,0:T(8,128)(2,1)S(1)}, u32[]{:S(2)}, u32[]{:S(2)}) %collective-permute-start.14) | collective-permute-done | bytes 131104 | tf_op jit(solution)/shard_map/ppermute | solution.py:156
  54.6 1.5 %collect.3.refs_2_ = bf16[16,2,2,32,256]{4,3,2,1,0:T(8,128)(2,1)} custom-call(s32[33]{0:T(128)S(1)} %pad_add_fusion.ids_ref, bf16[4,2,32,256]{3,2,1,0:T(8,128)(2,1)S(1)} %get-tuple-element.40.refs_0_, bf16[4,2,32,256]{3,2,1,0:T(8,128)(2,1)S(1)} %collective-permute-done.12.refs_1_, bf16[4,2,32,256]{3,2,1,0:T(8,128)(2,1)S(1)} %collective-permute-done.13.refs_2_, ...), custom_call_target="tpu_custom_call" | custom-call | tf_op jit(solution)/shard_map/collect/pallas_call | solution.py:240
  56.1 0.0 collective-permute-done.11.refs_1_
  56.1 1.3 %collect.4.refs_2_ = bf16[16,2,2,32,256]{4,3,2,1,0:T(8,128)(2,1)} custom-call(s32[33]{0:T(128)S(1)} %pad_add_fusion.ids_ref, bf16[4,2,32,256]{3,2,1,0:T(8,128)(2,1)S(1)} %get-tuple-element.38.refs_0_, bf16[4,2,32,256]{3,2,1,0:T(8,128)(2,1)S(1)} %collective-permute-done.11.refs_1_, ...), custom_call_target="tpu_custom_call", output_to_operand_aliasing={{}: (3, {})} | custom-call | tf_op jit(solution)/shard_map/collect/pallas_call | solution.py:240
  57.4 0.7 collective-permute-done.9.refs_0_
  58.1 1.4 %collective-permute-done.10.refs_1_ = bf16[4,2,32,256]{3,2,1,0:T(8,128)(2,1)S(1)} collective-permute-done((bf16[4,2,32,256]{3,2,1,0:T(8,128)(2,1)S(1)}, bf16[4,2,32,256]{3,2,1,0:T(8,128)(2,1)S(1)}, u32[]{:S(2)}, u32[]{:S(2)}) %collective-permute-start.10) | collective-permute-done | bytes 131104 | tf_op jit(solution)/shard_map/ppermute | solution.py:156
  59.5 1.3 %collect.5 = bf16[16,2,2,32,256]{4,3,2,1,0:T(8,128)(2,1)} custom-call(s32[33]{0:T(128)S(1)} %pad_add_fusion.ids_ref, bf16[4,2,32,256]{3,2,1,0:T(8,128)(2,1)S(1)} %collective-permute-done.9.refs_0_, bf16[4,2,32,256]{3,2,1,0:T(8,128)(2,1)S(1)} %collective-permute-done.10.refs_1_, ...), custom_call_target="tpu_custom_call", output_to_operand_aliasing={{}: (3, {})} | custom-call | tf_op jit(solution)/shard_map/collect/pallas_call | solution.py:240
  60.8 3.7 %all-to-all-start.1 = ((bf16[16,2,2,32,256]{4,3,2,1,0:T(8,128)(2,1)}), bf16[16,2,2,32,256]{4,3,2,1,0:T(8,128)(2,1)S(1)}, u32[]{:S(2)}, u32[]{:S(2)}) async-start(bf16[16,2,2,32,256]{4,3,2,1,0:T(8,128)(2,1)} %collect.5), calls=%async_computation.1 | async-start | bytes 2097152 | tf_op jit(solution)/shard_map/all_to_all | solution.py:253
  64.6 1.9 %collective-permute-start.8 = (bf16[64,2048]{1,0:T(8,128)(2,1)S(1)}, bf16[64,2048]{1,0:T(8,128)(2,1)S(1)}, u32[]{:S(2)}, u32[]{:S(2)}) collective-permute-start(bf16[64,2048]{1,0:T(8,128)(2,1)S(1)} %slice.14), channel_id=1, source_target_pairs={{0,4},{4,8},{8,12},{12,16},{16,20},{20,24},{24,28},{28,32},{32,36}... | collective-permute-start | bytes 786440 | tf_op jit(solution)/shard_map/ppermute | solution.py:226
  66.6 0.1 fusion.1
  66.6 5.7 %collective-permute-done.8 = bf16[64,2048]{1,0:T(8,128)(2,1)S(1)} collective-permute-done((bf16[64,2048]{1,0:T(8,128)(2,1)S(1)}, bf16[64,2048]{1,0:T(8,128)(2,1)S(1)}, u32[]{:S(2)}, u32[]{:S(2)}) %collective-permute-start.8) | collective-permute-done | bytes 262176 | tf_op jit(solution)/shard_map/ppermute | solution.py:226
  72.3 1.3 %fusion = bf16[1,256,2048]{2,1,0:T(8,128)(2,1)} fusion(bf16[1,128,2048]{2,1,0:T(8,128)(2,1)S(1)} %bitcast.23, bf16[1,128,2048]{2,1,0:T(8,128)(2,1)S(1)} %bitcast.24, bf16[1,192,2048]{2,1,0:T(8,128)(2,1)S(1)} %fusion.1, bf16[1,64,2048]{2,1,0:T(8,128)(2,1)S(1)} %bitcast.28, s32[256]{0:T(256)S(1)} %get-tuple-element.44, s32[256]{0:T(256)S(1)} %get-tuple-element.45, ...), kind=kLoop, calls=%fused_computation.1 | loop fusion | flops 5767168 | bytes 3148032 | tf_op jit(solution)/shard_map/jit(_where)/select_n | solution.py:228
  73.6 3.9 %all-to-all-done.1 = bf16[16,2,2,32,256]{4,3,2,1,0:T(8,128)(2,1)S(1)} async-done(((bf16[16,2,2,32,256]{4,3,2,1,0:T(8,128)(2,1)}), bf16[16,2,2,32,256]{4,3,2,1,0:T(8,128)(2,1)S(1)}, u32[]{:S(2)}, u32[]{:S(2)}) %all-to-all-start.1) | async-done | bytes 1048608 | tf_op jit(solution)/shard_map/all_to_all | solution.py:253
  77.5 0.8 %copy.13 = bf16[2,4,32,2,4,256]{5,4,3,2,1,0:T(4,128)(2,1)S(1)} copy(bf16[2,4,32,2,4,256]{5,2,3,0,1,4:T(8,128)(2,1)S(1)} %bitcast.26) | data formatting | bytes 2097152 | tf_op jit(solution)/shard_map/transpose | solution.py:255
  78.3 1.2 %reshape.136 = bf16[2,128,2,1024]{3,2,1,0:T(2,128)(2,1)} reshape(bf16[2,4,32,2,4,256]{5,4,3,2,1,0:T(4,128)(2,1)S(1)} %copy.13) | data formatting | bytes 2097152 | tf_op jit(solution)/shard_map/reshape | solution.py:256
  (3 shorter events, 0.0 us)
Async XLA Ops:
  0.6 16.6 %copy-start = (s32[4,64,2]{1,2,0:T(2,128)S(1)}, s32[4,64,2]{1,2,0:T(2,128)}, u32[]{:S(2)}) copy-start(s32[4,64,2]{1,2,0:T(2,128)} %param.7) | copy-start | bytes 6148
  3.6 7.2 %copy-start.2 = (bf16[1,256,2048]{2,1,0:T(8,128)(2,1)S(1)}, bf16[1,256,2048]{2,1,0:T(8,128)(2,1)}, u32[]{:S(2)}) copy-start(bf16[1,256,2048]{2,1,0:T(8,128)(2,1)} %param.5) | copy-start | bytes 3145732
  3.6 10.0 %copy-start.1 = (bf16[1,256,2048]{2,1,0:T(8,128)(2,1)S(1)}, bf16[1,256,2048]{2,1,0:T(8,128)(2,1)}, u32[]{:S(2)}) copy-start(bf16[1,256,2048]{2,1,0:T(8,128)(2,1)} %param.4) | copy-start | bytes 3145732
  3.6 24.9 %all-to-all-start = ((bf16[16,2,2,32,256]{4,3,2,1,0:T(8,128)(2,1)}), bf16[16,2,2,32,256]{4,3,2,1,0:T(8,128)(2,1)S(1)}, u32[]{:S(2)}, u32[]{:S(2)}) async-start(bf16[16,2,2,32,256]{4,3,2,1,0:T(8,128)(2,1)} %bitcast.25), calls=%async_computation | async-start | bytes 2097152 | tf_op jit(solution)/shard_map/all_to_all | solution.py:167
  11.5 21.1 %collective-permute-start.4 = (bf16[64,2048]{1,0:T(8,128)(2,1)}, bf16[64,2048]{1,0:T(8,128)(2,1)S(1)}, u32[]{:S(2)}, u32[]{:S(2)}) collective-permute-start(bf16[64,2048]{1,0:T(8,128)(2,1)} %slice.13), channel_id=1, source_target_pairs={{4,0},{8,4},{12,8},{16,12},{20,16},{24,20},{28,24},{32,28},{36,32}... | collective-permute-start | bytes 786440 | tf_op jit(solution)/shard_map/ppermute | solution.py:171
  14.3 19.0 %collective-permute-start.3 = (bf16[64,2048]{1,0:T(8,128)(2,1)}, bf16[64,2048]{1,0:T(8,128)(2,1)}, u32[]{:S(2)}, u32[]{:S(2)}) collective-permute-start(bf16[64,2048]{1,0:T(8,128)(2,1)} %slice.12), channel_id=1, source_target_pairs={{4,0},{8,4},{12,8},{16,12},{20,16},{24,20},{28,24},{32,28},{36,32}... | collective-permute-start | bytes 786440 | tf_op jit(solution)/shard_map/ppermute | solution.py:171
  29.2 10.4 %collective-permute-start.5 = (bf16[4,2,32,256]{3,2,1,0:T(8,128)(2,1)S(1)}, bf16[4,2,32,256]{3,2,1,0:T(8,128)(2,1)S(1)}, u32[]{:S(2)}, u32[]{:S(2)}) collective-permute-start(bf16[4,2,32,256]{3,2,1,0:T(8,128)(2,1)S(1)} %get-tuple-element.32), channel_id=1, source_target_pairs={{0,64},{64,128},{128,192},{192,0},{1,65},{65,129},{129,193},{193,1... | collective-permute-start | bytes 393224 | tf_op jit(solution)/shard_map/ppermute | solution.py:156
  29.8 9.7 %collective-permute-start.6 = (bf16[4,2,32,256]{3,2,1,0:T(8,128)(2,1)S(1)}, bf16[4,2,32,256]{3,2,1,0:T(8,128)(2,1)S(1)}, u32[]{:S(2)}, u32[]{:S(2)}) collective-permute-start(bf16[4,2,32,256]{3,2,1,0:T(8,128)(2,1)S(1)} %get-tuple-element.33), channel_id=1, source_target_pairs={{0,128},{64,192},{128,0},{192,64},{1,129},{65,193},{129,1},{193,65... | collective-permute-start | bytes 393224 | tf_op jit(solution)/shard_map/ppermute | solution.py:156
  30.9 9.6 %collective-permute-start.7 = (bf16[4,2,32,256]{3,2,1,0:T(8,128)(2,1)S(1)}, bf16[4,2,32,256]{3,2,1,0:T(8,128)(2,1)S(1)}, u32[]{:S(2)}, u32[]{:S(2)}) collective-permute-start(bf16[4,2,32,256]{3,2,1,0:T(8,128)(2,1)S(1)} %get-tuple-element.34), channel_id=1, source_target_pairs={{0,192},{64,0},{128,64},{192,128},{1,193},{65,1},{129,65},{193,129... | collective-permute-start | bytes 393224 | tf_op jit(solution)/shard_map/ppermute | solution.py:156
  32.6 13.4 %collective-permute-start = (bf16[4,2,32,256]{3,2,1,0:T(8,128)(2,1)S(1)}, bf16[4,2,32,256]{3,2,1,0:T(8,128)(2,1)S(1)}, u32[]{:S(2)}, u32[]{:S(2)}) collective-permute-start(bf16[4,2,32,256]{3,2,1,0:T(8,128)(2,1)S(1)} %get-tuple-element.27), channel_id=1, source_target_pairs={{0,64},{64,128},{128,192},{192,0},{1,65},{65,129},{129,193},{193,1... | collective-permute-start | bytes 393224 | tf_op jit(solution)/shard_map/ppermute | solution.py:156
  33.3 12.8 %collective-permute-start.1 = (bf16[4,2,32,256]{3,2,1,0:T(8,128)(2,1)S(1)}, bf16[4,2,32,256]{3,2,1,0:T(8,128)(2,1)S(1)}, u32[]{:S(2)}, u32[]{:S(2)}) collective-permute-start(bf16[4,2,32,256]{3,2,1,0:T(8,128)(2,1)S(1)} %get-tuple-element.28), channel_id=1, source_target_pairs={{0,128},{64,192},{128,0},{192,64},{1,129},{65,193},{129,1},{193,65... | collective-permute-start | bytes 393224 | tf_op jit(solution)/shard_map/ppermute | solution.py:156
  39.5 6.6 %collective-permute-start.2 = (bf16[4,2,32,256]{3,2,1,0:T(8,128)(2,1)S(1)}, bf16[4,2,32,256]{3,2,1,0:T(8,128)(2,1)S(1)}, u32[]{:S(2)}, u32[]{:S(2)}) collective-permute-start(bf16[4,2,32,256]{3,2,1,0:T(8,128)(2,1)S(1)} %get-tuple-element.29), channel_id=1, source_target_pairs={{0,192},{64,0},{128,64},{192,128},{1,193},{65,1},{129,65},{193,129... | collective-permute-start | bytes 393224 | tf_op jit(solution)/shard_map/ppermute | solution.py:156
  42.8 10.3 %collective-permute-start.12 = (bf16[4,2,32,256]{3,2,1,0:T(8,128)(2,1)S(1)}, bf16[4,2,32,256]{3,2,1,0:T(8,128)(2,1)S(1)}, u32[]{:S(2)}, u32[]{:S(2)}) collective-permute-start(bf16[4,2,32,256]{3,2,1,0:T(8,128)(2,1)S(1)} %get-tuple-element.41), channel_id=1, source_target_pairs={{0,192},{64,0},{128,64},{192,128},{1,193},{65,1},{129,65},{193,129... | collective-permute-start | bytes 393224 | tf_op jit(solution)/shard_map/ppermute | solution.py:156
  45.2 7.9 %collective-permute-start.13 = (bf16[4,2,32,256]{3,2,1,0:T(8,128)(2,1)S(1)}, bf16[4,2,32,256]{3,2,1,0:T(8,128)(2,1)S(1)}, u32[]{:S(2)}, u32[]{:S(2)}) collective-permute-start(bf16[4,2,32,256]{3,2,1,0:T(8,128)(2,1)S(1)} %get-tuple-element.42), channel_id=1, source_target_pairs={{0,128},{64,192},{128,0},{192,64},{1,129},{65,193},{129,1},{193,65... | collective-permute-start | bytes 393224 | tf_op jit(solution)/shard_map/ppermute | solution.py:156
  46.1 8.6 %collective-permute-start.14 = (bf16[4,2,32,256]{3,2,1,0:T(8,128)(2,1)S(1)}, bf16[4,2,32,256]{3,2,1,0:T(8,128)(2,1)S(1)}, u32[]{:S(2)}, u32[]{:S(2)}) collective-permute-start(bf16[4,2,32,256]{3,2,1,0:T(8,128)(2,1)S(1)} %get-tuple-element.43), channel_id=1, source_target_pairs={{0,64},{64,128},{128,192},{192,0},{1,65},{65,129},{129,193},{193,1... | collective-permute-start | bytes 393224 | tf_op jit(solution)/shard_map/ppermute | solution.py:156
  48.2 7.9 %collective-permute-start.11 = (bf16[4,2,32,256]{3,2,1,0:T(8,128)(2,1)S(1)}, bf16[4,2,32,256]{3,2,1,0:T(8,128)(2,1)S(1)}, u32[]{:S(2)}, u32[]{:S(2)}) collective-permute-start(bf16[4,2,32,256]{3,2,1,0:T(8,128)(2,1)S(1)} %get-tuple-element.39), channel_id=1, source_target_pairs={{0,192},{64,0},{128,64},{192,128},{1,193},{65,1},{129,65},{193,129... | collective-permute-start | bytes 393224 | tf_op jit(solution)/shard_map/ppermute | solution.py:156
  51.6 6.5 %collective-permute-start.9 = (bf16[4,2,32,256]{3,2,1,0:T(8,128)(2,1)S(1)}, bf16[4,2,32,256]{3,2,1,0:T(8,128)(2,1)S(1)}, u32[]{:S(2)}, u32[]{:S(2)}) collective-permute-start(bf16[4,2,32,256]{3,2,1,0:T(8,128)(2,1)S(1)} %get-tuple-element.36), channel_id=1, source_target_pairs={{0,128},{64,192},{128,0},{192,64},{1,129},{65,193},{129,1},{193,65... | collective-permute-start | bytes 393224 | tf_op jit(solution)/shard_map/ppermute | solution.py:156
  53.1 6.4 %collective-permute-start.10 = (bf16[4,2,32,256]{3,2,1,0:T(8,128)(2,1)S(1)}, bf16[4,2,32,256]{3,2,1,0:T(8,128)(2,1)S(1)}, u32[]{:S(2)}, u32[]{:S(2)}) collective-permute-start(bf16[4,2,32,256]{3,2,1,0:T(8,128)(2,1)S(1)} %get-tuple-element.37), channel_id=1, source_target_pairs={{0,64},{64,128},{128,192},{192,0},{1,65},{65,129},{129,193},{193,1... | collective-permute-start | bytes 393224 | tf_op jit(solution)/shard_map/ppermute | solution.py:156
  60.8 16.7 %all-to-all-start.1 = ((bf16[16,2,2,32,256]{4,3,2,1,0:T(8,128)(2,1)}), bf16[16,2,2,32,256]{4,3,2,1,0:T(8,128)(2,1)S(1)}, u32[]{:S(2)}, u32[]{:S(2)}) async-start(bf16[16,2,2,32,256]{4,3,2,1,0:T(8,128)(2,1)} %collect.5), calls=%async_computation.1 | async-start | bytes 2097152 | tf_op jit(solution)/shard_map/all_to_all | solution.py:253
  64.6 7.7 %collective-permute-start.8 = (bf16[64,2048]{1,0:T(8,128)(2,1)S(1)}, bf16[64,2048]{1,0:T(8,128)(2,1)S(1)}, u32[]{:S(2)}, u32[]{:S(2)}) collective-permute-start(bf16[64,2048]{1,0:T(8,128)(2,1)S(1)} %slice.14), channel_id=1, source_target_pairs={{0,4},{4,8},{8,12},{12,16},{16,20},{20,24},{24,28},{28,32},{32,36}... | collective-permute-start | bytes 786440 | tf_op jit(solution)/shard_map/ppermute | solution.py:226
